TPU v7x, 256 devices: a whole 4x4x8 slice. The times are simulated.
256 devices in a mesh: section: 4 (over x_hi, core), seq: 64 (over y, x_lo, z).
Axes of the slice: x: 4 (x_hi: 2, x_lo: 2; x = x_hi * 2 + x_lo), y: 4, z: 8, core: 2. Of those that a mesh axis runs over, the one named last changes fastest.
Arguments:
- layer_input: bfloat16 [4, 4096, 4, 1536], P('section', 'seq'), may hold values from -300 to 300
- norm_gain: float32 [4, 1536], P('section'), may hold values from 0.1 to 1.9
- queries: bfloat16 [4, 4096, 4, 1024], P('section', 'seq'), may hold values from -6 to 6
- key_states: bfloat16 [4, 4096, 4, 1024], P('section', 'seq'), may hold values from -6 to 6
- value_states: bfloat16 [4, 4096, 4, 1024], P('section', 'seq'), may hold values from -6 to 6
- out_grad: bfloat16 [4, 4096, 4, 1536], P('section', 'seq'), may hold values from -6 to 6
- out_weight: bfloat16 [4, 1024, 1536], P('section', 'seq'), may hold values from -0.1875 to 0.1875
- qkv_weight: bfloat16 [4, 1536, 3072], P('section', 'seq'), may hold values from -0.15625 to 0.15625
- lengths: int32 [4, 4], P('section'), may hold values from 2048 to 4096
Outputs:
- passed_grad: bfloat16 [4, 4096, 4, 1536], P('section', 'seq')
All inputs are finite; a program needn't handle non-finite values.
Results may differ from a plain program's by a relative error of at most 0.0034.
Values may be sent and summed in bfloat16 or wider, within the bound.
No kernel may reach another device: no remote copies, remote signals or barrier semaphores. Data moves between devices by JAX's collectives and lax.ppermute only.
A program may use at most 128 MiB of HBM per device.

v0:
```python
import jax
import jax.numpy as jnp
from jax import lax
from jax.sharding import PartitionSpec as P

HEADS = 16
HS = 64


EPSILON = 1e-05
MASKED = -1e30
ROW_DOT = (((1,), (1,)), ((), ()))
COL_DOT = (((0,), (0,)), ((), ()))


def shifted(shard, axis, by):
    count = lax.axis_size(axis)
    return lax.ppermute(shard, axis, [(i, (i + by) % count) for i in range(count)])


def item_backward(query_rows, key_rows, value_rows, grad_rows, key_valid):
    length = query_rows.shape[0]
    block = min(512, length)
    scale = HS ** (-0.5)
    offsets = jnp.arange(0, length, block)
    zeros = jnp.zeros((length, query_rows.shape[1]), jnp.float32)

    def step(carry, offset):
        key_total, value_total = carry
        query_block = lax.dynamic_slice_in_dim(query_rows, offset, block, 0)
        grad_block = lax.dynamic_slice_in_dim(grad_rows, offset, block, 0)
        scores = (
            lax.dot_general(query_block, key_rows, ROW_DOT, preferred_element_type=jnp.float32)
            * scale
        )
        scores = jnp.where(key_valid[None, :], scores, MASKED)
        largest = jnp.max(scores, axis=1, keepdims=True)
        weights = jnp.exp(scores - largest)
        probs = weights / jnp.sum(weights, axis=1, keepdims=True)
        probs_low = probs.astype(jnp.bfloat16)
        grad_probs = lax.dot_general(
            grad_block, value_rows, ROW_DOT, preferred_element_type=jnp.float32
        )
        centre = jnp.sum(probs * grad_probs, axis=1, keepdims=True)
        grad_scores = (probs * (grad_probs - centre) * scale).astype(jnp.bfloat16)
        query_grad = jnp.dot(grad_scores, key_rows, preferred_element_type=jnp.float32)
        key_total = key_total + lax.dot_general(
            grad_scores, query_block, COL_DOT, preferred_element_type=jnp.float32
        )
        value_total = value_total + lax.dot_general(
            probs_low, grad_block, COL_DOT, preferred_element_type=jnp.float32
        )
        return ((key_total, value_total), query_grad.astype(jnp.bfloat16))

    (key_total, value_total), query_parts = lax.scan(step, (zeros, zeros), offsets)
    query_grad = query_parts.reshape(length, query_rows.shape[1])
    return (query_grad, key_total.astype(jnp.bfloat16), value_total.astype(jnp.bfloat16))


def split_items(columns):
    length = columns.shape[0]
    count = columns.shape[1] // HS
    return columns.reshape(length, count, HS).transpose(1, 0, 2)


def join_items(items):
    count = items.shape[0]
    length = items.shape[1]
    return items.transpose(1, 0, 2).reshape(length, count * HS)


def project_grad(flat_grad, out_rows):
    return lax.dot_general(
        flat_grad,
        lax.all_gather(out_rows, "seq", axis=0, tiled=True),
        ROW_DOT,
        preferred_element_type=jnp.float32,
    ).astype(jnp.bfloat16)


def on_device(
    layer_input,
    norm_gain,
    queries,
    key_states,
    value_states,
    out_grad,
    out_weight,
    qkv_weight,
    lengths,
):
    frames = queries.shape[1]
    records = queries.shape[2]
    features = queries.shape[3]
    model_width = out_grad.shape[3]
    flat_grad = out_grad[0].reshape(frames * records, model_width)
    frame_queries = queries[0].reshape(frames, records * features)
    frame_keys = key_states[0].reshape(frames, records * features)
    frame_values = value_states[0].reshape(frames, records * features)
    attn_grad = project_grad(flat_grad, out_weight[0])
    head_queries, head_keys, head_values, head_grads = (
        lax.all_to_all(frame_queries, "seq", split_axis=1, concat_axis=0, tiled=True),
        lax.all_to_all(frame_keys, "seq", split_axis=1, concat_axis=0, tiled=True),
        lax.all_to_all(frame_values, "seq", split_axis=1, concat_axis=0, tiled=True),
        lax.all_to_all(
            attn_grad.reshape(frames, records * features),
            "seq",
            split_axis=1,
            concat_axis=0,
            tiled=True,
        ),
    )
    items_here = head_queries.shape[1] // HS
    length = head_queries.shape[0]
    item_ids = lax.axis_index("seq") * items_here + jnp.arange(items_here, dtype=jnp.int32)
    record_ids = item_ids // HEADS
    record_pick = jnp.arange(records, dtype=jnp.int32)[None, :] == record_ids[:, None]
    item_lengths = jnp.sum(jnp.where(record_pick, lengths[0][None, :], 0), axis=1)
    key_valid = jnp.arange(length, dtype=jnp.int32)[None, :] < item_lengths[:, None]
    query_grad, key_gradient, value_grad = lax.map(
        lambda group: item_backward(*group),
        (
            split_items(head_queries),
            split_items(head_keys),
            split_items(head_values),
            split_items(head_grads),
            key_valid,
        ),
    )
    query_back, key_backward, value_back = (
        lax.all_to_all(join_items(query_grad), "seq", split_axis=0, concat_axis=1, tiled=True),
        lax.all_to_all(join_items(key_gradient), "seq", split_axis=0, concat_axis=1, tiled=True),
        lax.all_to_all(join_items(value_grad), "seq", split_axis=0, concat_axis=1, tiled=True),
    )
    joined = jnp.concatenate(
        [
            query_back.reshape(frames * records, features),
            key_backward.reshape(frames * records, features),
            value_back.reshape(frames * records, features),
        ],
        axis=1,
    )
    norm_grad = lax.dot_general(
        joined,
        lax.all_gather(qkv_weight[0], "seq", axis=0, tiled=True),
        ROW_DOT,
        preferred_element_type=jnp.float32,
    )
    inputs = layer_input[0].reshape(frames * records, model_width).astype(jnp.float32)
    row_average = jnp.mean(inputs, axis=1, keepdims=True)
    centered_input = inputs - row_average
    var = jnp.mean(centered_input * centered_input, axis=1, keepdims=True)
    inverse_deviation = 1.0 / jnp.sqrt(var + EPSILON)
    normalized_input = centered_input * inverse_deviation
    scaled_rows = norm_grad * norm_gain[0][None, :]
    residual_branch = inverse_deviation * (
        scaled_rows
        - jnp.mean(scaled_rows, axis=1, keepdims=True)
        - normalized_input * jnp.mean(scaled_rows * normalized_input, axis=1, keepdims=True)
    )
    input_grad = (flat_grad.astype(jnp.float32) + residual_branch).astype(jnp.bfloat16)
    input_grad = input_grad.reshape(1, frames, records, model_width)
    return shifted(input_grad, "section", -1)


def solution(mesh):
    in_specs = (
        P("section", "seq", None, None),
        P("section", None),
        P("section", "seq", None, None),
        P("section", "seq", None, None),
        P("section", "seq", None, None),
        P("section", "seq", None, None),
        P("section", "seq", None),
        P("section", "seq", None),
        P("section", None),
    )
    out_specs = P("section", "seq", None, None)
    return jax.shard_map(
        on_device, mesh=mesh, in_specs=in_specs, out_specs=out_specs, check_vma=False
    )
```

profile of v0, /device:TPU:1, one launch (start us, length us, event | category | flops | bytes accessed | tf_op | source)
XLA Modules:
  0.0 689.1 jit_solution(5161656915856913208)
XLA Ops:
  11.3 13.6 %all-to-all-start = ((bf16[64,2,2048]{2,1,0:T(2,128)(2,1)}), bf16[64,2,2048]{2,1,0:T(2,128)(2,1)S(1)}, u32[]{:S(2)}, u32[]{:S(2)}) async-start(bf16[64,2,2048]{2,1,0:T(2,128)(2,1)} %reshape.136), calls=%async_computation | async-start | bytes 1048576 | tf_op jit(solution)/shard_map/all_to_all | solution.py:102
  27.8 15.0 %all-to-all-done = bf16[64,2,2048]{2,1,0:T(2,128)(2,1)S(1)} async-done(((bf16[64,2,2048]{2,1,0:T(2,128)(2,1)}), bf16[64,2,2048]{2,1,0:T(2,128)(2,1)S(1)}, u32[]{:S(2)}, u32[]{:S(2)}) %all-to-all-start) | async-done | bytes 524320 | tf_op jit(solution)/shard_map/all_to_all | solution.py:102
  42.8 6.8 all-to-all-start.1
  53.8 12.4 %all-to-all-done.1 = bf16[64,2,2048]{2,1,0:T(2,128)(2,1)S(1)} async-done(((bf16[64,2,2048]{2,1,0:T(2,128)(2,1)}), bf16[64,2,2048]{2,1,0:T(2,128)(2,1)S(1)}, u32[]{:S(2)}, u32[]{:S(2)}) %all-to-all-start.1) | async-done | bytes 524320 | tf_op jit(solution)/shard_map/all_to_all | solution.py:103
  66.2 8.1 %all-to-all-start.3 = ((bf16[64,2,2048]{2,1,0:T(2,128)(2,1)}), bf16[64,2,2048]{2,1,0:T(2,128)(2,1)}, u32[]{:S(2)}, u32[]{:S(2)}) async-start(bf16[64,2,2048]{2,1,0:T(2,128)(2,1)} %reshape.142), calls=%async_computation.3 | async-start | bytes 1048576 | tf_op jit(solution)/shard_map/all_to_all | solution.py:104
  75.9 200.7 %all-gather.5.cloned.1.call-done = bf16[1,1024,1536]{2,1,0:T(8,128)(2,1)} async-done(((bf16[1,16,1536]{2,1,0:T(8,128)(2,1)}), bf16[1,1024,1536]{2,1,0:T(8,128)(2,1)}) %all-gather.5.cloned.1.call-update) | async-done | bytes 3145744 | tf_op jit(solution)/shard_map/all_gather | solution.py:75
  284.3 6.9 %all-to-all-start.2 = ((bf16[64,2,2048]{2,1,0:T(2,128)(2,1)}), bf16[64,2,2048]{2,1,0:T(2,128)(2,1)}, u32[]{:S(2)}, u32[]{:S(2)}) async-start(bf16[64,2,2048]{2,1,0:T(2,128)(2,1)} %reshape.140), calls=%async_computation.2 | async-start | bytes 1048576 | tf_op jit(solution)/shard_map/all_to_all | solution.py:105
  298.7 6.2 all-to-all-done.2
  307.9 221.4 %while.26 = (s32[]{:T(128)}, f32[4096,64]{0,1:T(8,128)S(1)}, f32[4096,64]{0,1:T(8,128)}, bf16[8,512,64]{1,2,0:T(8,128)(2,1)}, s32[8]{0:T(128)S(1)}, /*index=5*/b...) while((s32[]{:T(128)}, f32[4096,64]{0,1:T(8,128)S(1)}, ...), condition=%wide.region_7.8_spmd.clone, body=%wide.region_3.7_spmd.clone.sunk | while | flops 1397787136 | bytes 147438384 | solution.py:55
  318.1 6.7 convolution_add_fusion.5
  345.4 7.0 %convolution_add_fusion.5 = f32[4096,64]{0,1:T(8,128)} fusion(f32[4096,64]{0,1:T(8,128)} %get-tuple-element.238, pred[]{:T(512)S(6)} %compare.5, bf16[4096,64]{1,0:T(8,128)(2,1)} %get-tuple-element.256, s32[]{:T(128)S(6)} %select_n.51, f32[512,4096]{1,0:T(8,128)} %copy-done, f32[512]{0:T(512)S(1)} %fusion.63, f32[512]{0:T(512)S(1)} %get-tuple-element.220, ...), kind=kOutput, calls=%fused_computation.8.clone.1 | convolution fusion | flops 279445504 | bytes 10625029 | tf_op jit(solution)/shard_map/while/body/eval_jaxpr/while/body/eval_jaxpr/dot_general | solution.py:50
  373.0 7.0 %convolution_add_fusion.5 = f32[4096,64]{0,1:T(8,128)} fusion(f32[4096,64]{0,1:T(8,128)} %get-tuple-element.238, pred[]{:T(512)S(6)} %compare.5, bf16[4096,64]{1,0:T(8,128)(2,1)} %get-tuple-element.256, s32[]{:T(128)S(6)} %select_n.51, f32[512,4096]{1,0:T(8,128)} %copy-done, f32[512]{0:T(512)S(1)} %fusion.63, f32[512]{0:T(512)S(1)} %get-tuple-element.220, ...), kind=kOutput, calls=%fused_computation.8.clone.1 | convolution fusion | flops 279445504 | bytes 10625029 | tf_op jit(solution)/shard_map/while/body/eval_jaxpr/while/body/eval_jaxpr/dot_general | solution.py:50
  400.7 7.0 %convolution_add_fusion.5 = f32[4096,64]{0,1:T(8,128)} fusion(f32[4096,64]{0,1:T(8,128)} %get-tuple-element.238, pred[]{:T(512)S(6)} %compare.5, bf16[4096,64]{1,0:T(8,128)(2,1)} %get-tuple-element.256, s32[]{:T(128)S(6)} %select_n.51, f32[512,4096]{1,0:T(8,128)} %copy-done, f32[512]{0:T(512)S(1)} %fusion.63, f32[512]{0:T(512)S(1)} %get-tuple-element.220, ...), kind=kOutput, calls=%fused_computation.8.clone.1 | convolution fusion | flops 279445504 | bytes 10625029 | tf_op jit(solution)/shard_map/while/body/eval_jaxpr/while/body/eval_jaxpr/dot_general | solution.py:50
  428.4 7.0 %convolution_add_fusion.5 = f32[4096,64]{0,1:T(8,128)} fusion(f32[4096,64]{0,1:T(8,128)} %get-tuple-element.238, pred[]{:T(512)S(6)} %compare.5, bf16[4096,64]{1,0:T(8,128)(2,1)} %get-tuple-element.256, s32[]{:T(128)S(6)} %select_n.51, f32[512,4096]{1,0:T(8,128)} %copy-done, f32[512]{0:T(512)S(1)} %fusion.63, f32[512]{0:T(512)S(1)} %get-tuple-element.220, ...), kind=kOutput, calls=%fused_computation.8.clone.1 | convolution fusion | flops 279445504 | bytes 10625029 | tf_op jit(solution)/shard_map/while/body/eval_jaxpr/while/body/eval_jaxpr/dot_general | solution.py:50
  456.0 7.0 %convolution_add_fusion.5 = f32[4096,64]{0,1:T(8,128)} fusion(f32[4096,64]{0,1:T(8,128)} %get-tuple-element.238, pred[]{:T(512)S(6)} %compare.5, bf16[4096,64]{1,0:T(8,128)(2,1)} %get-tuple-element.256, s32[]{:T(128)S(6)} %select_n.51, f32[512,4096]{1,0:T(8,128)} %copy-done, f32[512]{0:T(512)S(1)} %fusion.63, f32[512]{0:T(512)S(1)} %get-tuple-element.220, ...), kind=kOutput, calls=%fused_computation.8.clone.1 | convolution fusion | flops 279445504 | bytes 10625029 | tf_op jit(solution)/shard_map/while/body/eval_jaxpr/while/body/eval_jaxpr/dot_general | solution.py:50
  483.7 7.0 %convolution_add_fusion.5 = f32[4096,64]{0,1:T(8,128)} fusion(f32[4096,64]{0,1:T(8,128)} %get-tuple-element.238, pred[]{:T(512)S(6)} %compare.5, bf16[4096,64]{1,0:T(8,128)(2,1)} %get-tuple-element.256, s32[]{:T(128)S(6)} %select_n.51, f32[512,4096]{1,0:T(8,128)} %copy-done, f32[512]{0:T(512)S(1)} %fusion.63, f32[512]{0:T(512)S(1)} %get-tuple-element.220, ...), kind=kOutput, calls=%fused_computation.8.clone.1 | convolution fusion | flops 279445504 | bytes 10625029 | tf_op jit(solution)/shard_map/while/body/eval_jaxpr/while/body/eval_jaxpr/dot_general | solution.py:50
  511.3 7.0 %convolution_add_fusion.5 = f32[4096,64]{0,1:T(8,128)} fusion(f32[4096,64]{0,1:T(8,128)} %get-tuple-element.238, pred[]{:T(512)S(6)} %compare.5, bf16[4096,64]{1,0:T(8,128)(2,1)} %get-tuple-element.256, s32[]{:T(128)S(6)} %select_n.51, f32[512,4096]{1,0:T(8,128)} %copy-done, f32[512]{0:T(512)S(1)} %fusion.63, f32[512]{0:T(512)S(1)} %get-tuple-element.220, ...), kind=kOutput, calls=%fused_computation.8.clone.1 | convolution fusion | flops 279445504 | bytes 10625029 | tf_op jit(solution)/shard_map/while/body/eval_jaxpr/while/body/eval_jaxpr/dot_general | solution.py:50
  540.5 13.5 %all-to-all-done.4 = bf16[64,2,2048]{2,1,0:T(2,128)(2,1)S(1)} async-done(((bf16[64,2,2048]{2,1,0:T(2,128)(2,1)}), bf16[64,2,2048]{2,1,0:T(2,128)(2,1)S(1)}, u32[]{:S(2)}, u32[]{:S(2)}) %all-to-all-start.4) | async-done | bytes 524320 | tf_op jit(solution)/shard_map/all_to_all | solution.py:131
  564.8 9.1 %all-to-all-done.5 = bf16[64,2,2048]{2,1,0:T(2,128)(2,1)} async-done(((bf16[64,2,2048]{2,1,0:T(2,128)(2,1)}), bf16[64,2,2048]{2,1,0:T(2,128)(2,1)}, u32[]{:S(2)}, u32[]{:S(2)}) %all-to-all-start.5) | async-done | bytes 524320 | tf_op jit(solution)/shard_map/all_to_all | solution.py:132
  573.9 6.5 all-to-all-start.6
  603.2 22.1 %all-gather.7.cloned.1.call-done = bf16[1,1536,3072]{2,1,0:T(8,128)(2,1)} async-done(((bf16[1,24,3072]{2,1,0:T(8,128)(2,1)}), bf16[1,1536,3072]{2,1,0:T(8,128)(2,1)}) %all-gather.7.cloned.1.call-update) | async-done | bytes 9437200 | tf_op jit(solution)/shard_map/all_gather | solution.py:145
  625.3 6.9 %fusion.36 = (f32[256]{0:T(256)S(1)}, f32[256]{0:T(256)S(1)}, f32[256,1536]{1,0:T(8,128)S(1)}) fusion(f32[256]{0:T(256)S(1)} %sqrt.6, f32[256,1536]{1,0:T(8,128)S(1)} %reshape.132, f32[256]{0:T(256)S(1)} %div.40, f32[1536]{0:T(1024)S(1)} %reduce.3, bf16[1,1536,3072]{2,1,0:T(8,128)(2,1)} %all-gather.7.cloned.1.call-done, ...), kind=kOutput, calls=%fused_computation.49 | convolution fusion | flops 2422996480 | bytes 14166016 | tf_op jit(solution)/shard_map/dot_general | solution.py:143
  633.1 36.5 %collective-permute-start = (bf16[1,64,4,1536]{3,2,1,0:T(4,128)(2,1)S(1)}, bf16[1,64,4,1536]{3,2,1,0:T(4,128)(2,1)S(1)}, u32[]{:S(2)}, u32[]{:S(2)}) collective-permute-start(bf16[1,64,4,1536]{3,2,1,0:T(4,128)(2,1)S(1)} %reshape.131), channel_id=1, source_target_pairs={{0,192},{64,0},{128,64},{192,128},{1,193},{65,1},{129,65},{193,129... | collective-permute-start | bytes 2359304 | tf_op jit(solution)/shard_map/ppermute | solution.py:18
  669.6 11.6 %collective-permute-done = bf16[1,64,4,1536]{3,2,1,0:T(4,128)(2,1)S(1)} collective-permute-done((bf16[1,64,4,1536]{3,2,1,0:T(4,128)(2,1)S(1)}, bf16[1,64,4,1536]{3,2,1,0:T(4,128)(2,1)S(1)}, u32[]{:S(2)}, u32[]{:S(2)}) %collective-permute-start) | collective-permute-done | bytes 786464 | tf_op jit(solution)/shard_map/ppermute | solution.py:18
  (191 shorter events, 228.8 us)
Async XLA Ops:
  6.5 18.4 %copy-start.8 = (bf16[1,64,4,1024]{3,2,1,0:T(4,128)(2,1)S(1)}, bf16[1,64,4,1024]{3,2,1,0:T(4,128)(2,1)}, u32[]{:S(2)}) copy-start(bf16[1,64,4,1024]{3,2,1,0:T(4,128)(2,1)} %param.14) | copy-start | bytes 1572868
  6.5 270.1 %all-gather.5.cloned.1.call-start = ((), (), s32[]{:S(2)}) async-start(), calls=%async_computation.7 | async-start | bytes 3194880 | tf_op jit(solution)/shard_map/all_gather | solution.py:75
  11.3 31.5 %all-to-all-start = ((bf16[64,2,2048]{2,1,0:T(2,128)(2,1)}), bf16[64,2,2048]{2,1,0:T(2,128)(2,1)S(1)}, u32[]{:S(2)}, u32[]{:S(2)}) async-start(bf16[64,2,2048]{2,1,0:T(2,128)(2,1)} %reshape.136), calls=%async_computation | async-start | bytes 1048576 | tf_op jit(solution)/shard_map/all_to_all | solution.py:102
  42.8 23.4 %all-to-all-start.1 = ((bf16[64,2,2048]{2,1,0:T(2,128)(2,1)}), bf16[64,2,2048]{2,1,0:T(2,128)(2,1)S(1)}, u32[]{:S(2)}, u32[]{:S(2)}) async-start(bf16[64,2,2048]{2,1,0:T(2,128)(2,1)} %reshape.138), calls=%async_computation.1 | async-start | bytes 1048576 | tf_op jit(solution)/shard_map/all_to_all | solution.py:103
  66.2 215.9 %copy-start.5 = (bf16[64,2,2048]{2,1,0:T(2,128)(2,1)}, bf16[64,2,2048]{2,1,0:T(2,128)(2,1)S(1)}, u32[]{:S(2)}) copy-start(bf16[64,2,2048]{2,1,0:T(2,128)(2,1)S(1)} %all-to-all-done.1) | copy-start | bytes 1572868
  66.2 218.1 %all-to-all-start.3 = ((bf16[64,2,2048]{2,1,0:T(2,128)(2,1)}), bf16[64,2,2048]{2,1,0:T(2,128)(2,1)}, u32[]{:S(2)}, u32[]{:S(2)}) async-start(bf16[64,2,2048]{2,1,0:T(2,128)(2,1)} %reshape.142), calls=%async_computation.3 | async-start | bytes 1048576 | tf_op jit(solution)/shard_map/all_to_all | solution.py:104
  75.9 204.4 %copy-start.3 = (bf16[256,1536]{1,0:T(8,128)(2,1)}, bf16[256,1536]{1,0:T(8,128)(2,1)S(1)}, u32[]{:S(2)}) copy-start(bf16[256,1536]{1,0:T(8,128)(2,1)S(1)} %reshape_squeeze.2) | copy-start | bytes 2359300
  280.3 11.8 %copy-start.10 = (s32[1,4]{1,0:T(1,128)S(1)}, s32[1,4]{1,0:T(1,128)}, u32[]{:S(2)}) copy-start(s32[1,4]{1,0:T(1,128)} %param.19) | copy-start | bytes 52
  284.3 20.6 %all-to-all-start.2 = ((bf16[64,2,2048]{2,1,0:T(2,128)(2,1)}), bf16[64,2,2048]{2,1,0:T(2,128)(2,1)}, u32[]{:S(2)}, u32[]{:S(2)}) async-start(bf16[64,2,2048]{2,1,0:T(2,128)(2,1)} %reshape.140), calls=%async_computation.2 | async-start | bytes 1048576 | tf_op jit(solution)/shard_map/all_to_all | solution.py:105
  291.2 334.1 %all-gather.7.cloned.1.call-start = ((), (), s32[]{:S(2)}) async-start(), calls=%async_computation.8 | async-start | bytes 9584640 | tf_op jit(solution)/shard_map/all_gather | solution.py:145
  373.0 7.1 %copy-start.1 = (f32[512,4096]{1,0:T(8,128)S(1)}, f32[512,4096]{1,0:T(8,128)}, u32[]{:S(2)}) copy-start(f32[512,4096]{1,0:T(8,128)} %copy-done) | copy-start | bytes 25165828 | tf_op jit(solution)/shard_map/while/body/eval_jaxpr/while
  373.0 7.0 %copy-start.7 = (bf16[4096,64]{1,0:T(8,128)(2,1)S(1)}, bf16[4096,64]{1,0:T(8,128)(2,1)}, u32[]{:S(2)}) copy-start(bf16[4096,64]{1,0:T(8,128)(2,1)} %get-tuple-element.257) | copy-start | bytes 1572868 | tf_op jit(solution)/shard_map/while/body/eval_jaxpr/while
  400.7 7.1 %copy-start.1 = (f32[512,4096]{1,0:T(8,128)S(1)}, f32[512,4096]{1,0:T(8,128)}, u32[]{:S(2)}) copy-start(f32[512,4096]{1,0:T(8,128)} %copy-done) | copy-start | bytes 25165828 | tf_op jit(solution)/shard_map/while/body/eval_jaxpr/while
  400.7 7.0 %copy-start.7 = (bf16[4096,64]{1,0:T(8,128)(2,1)S(1)}, bf16[4096,64]{1,0:T(8,128)(2,1)}, u32[]{:S(2)}) copy-start(bf16[4096,64]{1,0:T(8,128)(2,1)} %get-tuple-element.257) | copy-start | bytes 1572868 | tf_op jit(solution)/shard_map/while/body/eval_jaxpr/while
  456.0 7.1 %copy-start.1 = (f32[512,4096]{1,0:T(8,128)S(1)}, f32[512,4096]{1,0:T(8,128)}, u32[]{:S(2)}) copy-start(f32[512,4096]{1,0:T(8,128)} %copy-done) | copy-start | bytes 25165828 | tf_op jit(solution)/shard_map/while/body/eval_jaxpr/while
  456.0 7.0 %copy-start.7 = (bf16[4096,64]{1,0:T(8,128)(2,1)S(1)}, bf16[4096,64]{1,0:T(8,128)(2,1)}, u32[]{:S(2)}) copy-start(bf16[4096,64]{1,0:T(8,128)(2,1)} %get-tuple-element.257) | copy-start | bytes 1572868 | tf_op jit(solution)/shard_map/while/body/eval_jaxpr/while
  483.7 7.0 %copy-start.1 = (f32[512,4096]{1,0:T(8,128)S(1)}, f32[512,4096]{1,0:T(8,128)}, u32[]{:S(2)}) copy-start(f32[512,4096]{1,0:T(8,128)} %copy-done) | copy-start | bytes 25165828 | tf_op jit(solution)/shard_map/while/body/eval_jaxpr/while
  531.9 27.6 %copy-start.2 = (bf16[1,64,4,1536]{3,2,1,0:T(4,128)(2,1)S(1)}, bf16[1,64,4,1536]{3,2,1,0:T(4,128)(2,1)}, u32[]{:S(2)}) copy-start(bf16[1,64,4,1536]{3,2,1,0:T(4,128)(2,1)} %param.11) | copy-start | bytes 2359300
  533.5 20.5 %all-to-all-start.4 = ((bf16[64,2,2048]{2,1,0:T(2,128)(2,1)}), bf16[64,2,2048]{2,1,0:T(2,128)(2,1)S(1)}, u32[]{:S(2)}, u32[]{:S(2)}) async-start(bf16[64,2,2048]{2,1,0:T(2,128)(2,1)} %reshape.148), calls=%async_computation.4 | async-start | bytes 1048576 | tf_op jit(solution)/shard_map/all_to_all | solution.py:131
  554.0 19.9 %all-to-all-start.5 = ((bf16[64,2,2048]{2,1,0:T(2,128)(2,1)}), bf16[64,2,2048]{2,1,0:T(2,128)(2,1)}, u32[]{:S(2)}, u32[]{:S(2)}) async-start(bf16[64,2,2048]{2,1,0:T(2,128)(2,1)} %reshape.146), calls=%async_computation.5 | async-start | bytes 1048576 | tf_op jit(solution)/shard_map/all_to_all | solution.py:132
  559.6 22.0 %copy-start.9 = (f32[1,1536]{1,0:T(1,128)S(1)}, f32[1,1536]{1,0:T(1,128)}, u32[]{:S(2)}) copy-start(f32[1,1536]{1,0:T(1,128)} %param.12) | copy-start | bytes 18436
  573.9 24.8 %all-to-all-start.6 = ((bf16[64,2,2048]{2,1,0:T(2,128)(2,1)}), bf16[64,2,2048]{2,1,0:T(2,128)(2,1)S(1)}, u32[]{:S(2)}, u32[]{:S(2)}) async-start(bf16[64,2,2048]{2,1,0:T(2,128)(2,1)} %reshape.144), calls=%async_computation.6 | async-start | bytes 1048576 | tf_op jit(solution)/shard_map/all_to_all | solution.py:133
  603.2 29.1 %copy-start.4 = (bf16[256,1536]{1,0:T(8,128)(2,1)S(1)}, bf16[256,1536]{1,0:T(8,128)(2,1)}, u32[]{:S(2)}) copy-start(bf16[256,1536]{1,0:T(8,128)(2,1)} %copy-done.3) | copy-start | bytes 2359300
  633.1 48.1 %collective-permute-start = (bf16[1,64,4,1536]{3,2,1,0:T(4,128)(2,1)S(1)}, bf16[1,64,4,1536]{3,2,1,0:T(4,128)(2,1)S(1)}, u32[]{:S(2)}, u32[]{:S(2)}) collective-permute-start(bf16[1,64,4,1536]{3,2,1,0:T(4,128)(2,1)S(1)} %reshape.131), channel_id=1, source_target_pairs={{0,192},{64,0},{128,64},{192,128},{1,193},{65,1},{129,65},{193,129... | collective-permute-start | bytes 2359304 | tf_op jit(solution)/shard_map/ppermute | solution.py:18
  (18 other events, 94.7 us)
Sparse Core Ops, SparseCore 0:
  9.1 267.4 all-gather.4
  293.9 331.4 all-gather.6
where the time goes:
time: 698 us; the launch traced here: 689 us
  waiting for transfers between devices  295 us (42%)
  matrix products  134 us (19%)
  starting transfers between devices  88.9 us (13%)
  local copies, waits for them, and re-layouts  85.7 us (12%)
  other arithmetic  57.5 us (8%)
  loops' own time  14.4 us (2%)
  between operations  14.1 us (2%)
    all_gather x1, waiting for transfers between devices, project_grad(): lax.all_gather(out_rows, 'seq', axis=0, tiled=True)  201 us
    dot_general x8, matrix products, step(): lax.dot_general(probs_low, grad_block, COL_DOT, preferred_element_type=jn...  55.8 us
    ppermute x1, starting transfers between devices, shifted(): lax.ppermute(shard, axis, [(i, (i + by) % count) for i in range(count)])  36.5 us
    dot_general x8, matrix products, step(): lax.dot_general(grad_block, value_rows, ROW_DOT, preferred_element_type=j...  31.8 us
    convert_element_type x8, other arithmetic, step(): grad_scores = (probs * (grad_probs - centre) * scale).astype(jnp.bfloat16)  31.5 us
    while x48, local copies, waits for them, and re-layouts  26.4 us
    unnamed x31, local copies, waits for them, and re-layouts  26 us
    all_gather x1, waiting for transfers between devices, on_device(): lax.all_gather(qkv_weight[0], 'seq', axis=0, tiled=True)  22.1 us
  transfers between devices with their start and end apart: 10, of which 9 were waited for; matrix products, arithmetic and copies ran while one was open for 34% of the time, Pallas kernels for 0%

commit v1 on v0

v1 whole, which is shorter than its diff:
```python
import functools

import jax
import jax.numpy as jnp
from jax import lax
from jax.experimental import pallas as pl
from jax.experimental.pallas import tpu as pltpu
from jax.sharding import PartitionSpec as P

HEADS = 16
HS = 64
EPSILON = 1e-05
MASKED = -1e30
SCALE = HS**-0.5
ROW_DOT = (((1,), (1,)), ((), ()))
PLAIN_DOT = (((1,), (0,)), ((), ()))
MIB = 1024 * 1024
QB = 256
KB = 256
Y, X, Z = 4, 2, 8
BF16 = jnp.bfloat16
F32 = jnp.float32
WHOLE = pl.BlockSpec(memory_space=pltpu.VMEM)


def cost(flops, moved, exps=0):
    return pl.CostEstimate(flops=flops, bytes_accessed=moved, transcendentals=exps)


def halves(even, odd):
    first = jnp.concatenate([even[:, :HS], odd[:, :HS]], axis=1)
    second = jnp.concatenate([even[:, HS:], odd[:, HS:]], axis=1)
    return first, second


def seq_pairs(dy, dx, dz):
    pairs = []
    for y in range(Y):
        for x in range(X):
            for z in range(Z):
                to = ((y + dy) % Y) * X * Z + ((x + dx) % X) * Z + (z + dz) % Z
                pairs.append((y * X * Z + x * Z + z, to))
    return pairs


def pack_kernel(q_ref, k_ref, v_ref, out_ref):
    half = q_ref.shape[0] // 2
    for n, ref in enumerate((q_ref, k_ref, v_ref)):
        for pair in range(ref.shape[1] // 128):
            tile = ref[:, pair * 128 : (pair + 1) * 128]
            first, second = halves(tile[:half], tile[half:])
            out_ref[2 * pair, n * half : (n + 1) * half, :] = first
            out_ref[2 * pair + 1, n * half : (n + 1) * half, :] = second


def pack_items(q, k, v):
    frames, lanes = q.shape
    out = jax.ShapeDtypeStruct((lanes // HS, 3 * frames // 2, 128), BF16)
    return pl.pallas_call(
        pack_kernel,
        out_shape=out,
        in_specs=[WHOLE] * 3,
        out_specs=WHOLE,
        compiler_params=pltpu.CompilerParams(vmem_limit_bytes=16 * MIB),
        cost_estimate=cost(0, 3 * MIB),
    )(q, k, v)


def place_kernel(owner_ref, *refs):
    out_ref = refs[-1]
    for n, ref in enumerate(refs[:-1]):
        out_ref[owner_ref[n]] = ref[...]


def place(owners, pieces):
    out = jax.ShapeDtypeStruct((len(pieces),) + pieces[0].shape, BF16)
    size = 2 * len(pieces) * pieces[0].size
    return pl.pallas_call(
        place_kernel,
        out_shape=out,
        in_specs=[pl.BlockSpec(memory_space=pltpu.SMEM)] + [WHOLE] * len(pieces),
        out_specs=WHOLE,
        compiler_params=pltpu.CompilerParams(vmem_limit_bytes=2 * size + 4 * MIB),
        cost_estimate=cost(0, 2 * size),
    )(owners, *pieces)


def project_kernel(owner_ref, grad_ref, *refs):
    out_ref = refs[-1]
    records = grad_ref.shape[0] // 64
    grads = grad_ref[...]
    for n, ref in enumerate(refs[:-1]):
        owner = owner_ref[n]
        tile = lax.dot_general(grads, ref[...], ROW_DOT, preferred_element_type=F32).astype(BF16)
        for r in range(records):
            first, second = halves(tile[r * 64 : r * 64 + 32], tile[r * 64 + 32 : r * 64 + 64])
            out_ref[r * HEADS + 2 * owner] = first
            out_ref[r * HEADS + 2 * owner + 1] = second


def project(owners, grads, pieces):
    rows, width = grads.shape
    items = (rows // 64) * HEADS
    return pl.pallas_call(
        project_kernel,
        out_shape=jax.ShapeDtypeStruct((items, 32, 128), BF16),
        in_specs=[pl.BlockSpec(memory_space=pltpu.SMEM)] + [WHOLE] * (1 + len(pieces)),
        out_specs=WHOLE,
        compiler_params=pltpu.CompilerParams(vmem_limit_bytes=20 * MIB),
        cost_estimate=cost(2 * rows * width * 1024, 2 * (rows * width + 1024 * width + rows * 1024)),
    )(owners, grads, *pieces)


def fold(values, op):
    return op(values.reshape(values.shape[0] // 8, 8, values.shape[1]), axis=0)


def weights_kernel(length_ref, r_ref, w_ref, l_ref, qt_ref, kt_ref, kz_ref, s_ref):
    step = pl.program_id(0)
    sources = r_ref.shape[0]
    rows = sources * 32
    length = 2 * rows

    @pl.when(step == 0)
    def _():
        valid = length_ref[0]
        packed_q = r_ref[:, 0:32, :].reshape(rows, 128)
        packed_k = r_ref[:, 32:64, :].reshape(rows, 128)
        q_turned = packed_q.T
        k_turned = packed_k.T
        for half in range(2):
            qt_ref[0:HS, half * rows : (half + 1) * rows] = q_turned[half * HS : (half + 1) * HS, :]
            kt_ref[:, half * rows : (half + 1) * rows] = k_turned[half * HS : (half + 1) * HS, :]
        row_id = lax.broadcasted_iota(jnp.int32, (HS, length), 0)
        qt_ref[HS:128, :] = jnp.where(row_id == 0, 1.0, 0.0).astype(BF16)
        spot = lax.broadcasted_iota(jnp.int32, (rows, HS), 0)
        lane = lax.broadcasted_iota(jnp.int32, (rows, HS), 1)
        for half in range(2):
            frame = (spot // 32) * 64 + half * 32 + spot % 32
            bias = jnp.where((lane == 0) & (frame >= valid), MASKED, 0.0).astype(BF16)
            keys = packed_k[:, half * HS : (half + 1) * HS] * SCALE
            kz_ref[half * rows : (half + 1) * rows, :] = jnp.concatenate([keys.astype(BF16), bias], axis=1)

    queries = qt_ref[:, pl.ds(pl.multiple_of(step * QB, QB), QB)]

    def first(j, top):
        at = pl.ds(pl.multiple_of(j * KB, KB), KB)
        s = lax.dot_general(kz_ref[at, :], queries, PLAIN_DOT, preferred_element_type=F32)
        s_ref[at, :] = s
        return jnp.maximum(top, fold(s, jnp.max))

    top = lax.fori_loop(0, length // KB, first, jnp.full((8, QB), -jnp.inf, F32), unroll=2)
    top = jnp.max(top, axis=0, keepdims=True)

    def second(j, total):
        at = pl.ds(pl.multiple_of(j * KB, KB), KB)
        w = jnp.exp(s_ref[at, :] - top)
        w_ref[0, at, :] = w.astype(BF16)
        return total + fold(w, jnp.sum)

    total = lax.fori_loop(0, length // KB, second, jnp.zeros((8, QB), F32), unroll=2)
    l_ref[...] = jnp.sum(total, axis=0, keepdims=True)


def softmax_weights(valid, received):
    length = received.shape[0] * 64
    blocks = length // QB
    fixed = lambda shape: pl.BlockSpec(shape, lambda i: (0,) * len(shape))
    return pl.pallas_call(
        weights_kernel,
        grid=(blocks,),
        out_shape=[
            jax.ShapeDtypeStruct((blocks, length, QB), BF16),
            jax.ShapeDtypeStruct((1, length), F32),
            jax.ShapeDtypeStruct((128, length), BF16),
            jax.ShapeDtypeStruct((HS, length), BF16),
        ],
        in_specs=[pl.BlockSpec(memory_space=pltpu.SMEM), WHOLE],
        out_specs=[
            pl.BlockSpec((1, length, QB), lambda i: (i, 0, 0)),
            pl.BlockSpec((1, QB), lambda i: (0, i)),
            fixed((128, length)),
            fixed((HS, length)),
        ],
        scratch_shapes=[pltpu.VMEM((length, 128), BF16), pltpu.VMEM((length, QB), F32)],
        compiler_params=pltpu.CompilerParams(vmem_limit_bytes=40 * MIB),
        cost_estimate=cost(8 * length * length * HS, 2 * length * length, length * length),
    )(valid, received)


def grads_kernel(w_ref, l_ref, qt_ref, kt_ref, r_ref, g_ref, dq_ref, dkv_ref, gt_ref, dp_ref, acc_ref, dqt_ref):
    step = pl.program_id(0)
    sources = r_ref.shape[0]
    rows = sources * 32
    length = 2 * rows
    per = KB // 32

    @pl.when(step == 0)
    def _():
        turned = g_ref[...].reshape(rows, 128).T
        for half in range(2):
            gt_ref[:, half * rows : (half + 1) * rows] = turned[half * HS : (half + 1) * HS, :]
        acc_ref[...] = jnp.zeros_like(acc_ref)

    here = pl.ds(pl.multiple_of(step * QB, QB), QB)
    grads = gt_ref[:, here]
    none = jnp.zeros((HS, QB), BF16)
    inverse = 1.0 / l_ref[:, here]

    def first(half, side, j, centre):
        at = pl.ds(pl.multiple_of(half * rows + j * KB, KB), KB)
        values = r_ref[pl.ds(j * per, per), 64:96, :].reshape(KB, 128)
        dp = lax.dot_general(values, side, PLAIN_DOT, preferred_element_type=F32)
        dp_ref[at, :] = dp
        return centre + fold(w_ref[0, at, :].astype(F32) * dp, jnp.sum)

    centre = jnp.zeros((8, QB), F32)
    for half in range(2):
        side = jnp.concatenate([grads, none] if half == 0 else [none, grads], axis=0)
        centre = lax.fori_loop(0, rows // KB, functools.partial(first, half, side), centre, unroll=2)
    centre = jnp.sum(centre, axis=0, keepdims=True) * inverse

    scaled_q = (qt_ref[0:HS, here].astype(F32) * (inverse * SCALE)).astype(BF16)
    scaled_g = (grads.astype(F32) * inverse).astype(BF16)
    side_t = jnp.concatenate([scaled_q, none], axis=0)
    side_w = jnp.concatenate([none, scaled_g], axis=0)

    def second(j, dqt):
        at = pl.ds(pl.multiple_of(j * KB, KB), KB)
        w = w_ref[0, at, :]
        t = (w.astype(F32) * (dp_ref[at, :] - centre)).astype(BF16)
        acc_ref[at, :] += lax.dot_general(
            t, side_t, ROW_DOT, preferred_element_type=F32
        ) + lax.dot_general(w, side_w, ROW_DOT, preferred_element_type=F32)
        return dqt + lax.dot_general(kt_ref[:, at], t, PLAIN_DOT, preferred_element_type=F32)

    dqt = lax.fori_loop(0, length // KB, second, jnp.zeros((HS, QB), F32), unroll=2)
    dqt = dqt * (inverse * SCALE)
    steps = rows // QB

    @pl.when(step < steps)
    def _():
        dqt_ref[0:HS, pl.ds(pl.multiple_of(step * QB, QB), QB)] = dqt

    @pl.when(step >= steps)
    def _():
        dqt_ref[HS:128, pl.ds(pl.multiple_of((step - steps) * QB, QB), QB)] = dqt

    @pl.when(step == 2 * steps - 1)
    def _():
        dq_ref[...] = dqt_ref[...].T.astype(BF16).reshape(sources, 32, 128)
        for half in range(2):
            part = acc_ref[half * rows : (half + 1) * rows, :].astype(BF16)
            dkv_ref[:, half * 32 : (half + 1) * 32, :] = part.reshape(sources, 32, 128)


def attention_grads(weights, sums, queries_t, keys_t, received, received_grads):
    blocks, length, _ = weights.shape
    sources = received.shape[0]
    return pl.pallas_call(
        grads_kernel,
        grid=(blocks,),
        out_shape=[
            jax.ShapeDtypeStruct((sources, 32, 128), BF16),
            jax.ShapeDtypeStruct((sources, 64, 128), BF16),
        ],
        in_specs=[pl.BlockSpec((1, length, QB), lambda i: (i, 0, 0))] + [WHOLE] * 5,
        out_specs=[WHOLE, WHOLE],
        scratch_shapes=[
            pltpu.VMEM((HS, length), BF16),
            pltpu.VMEM((length, QB), F32),
            pltpu.VMEM((length, 128), F32),
            pltpu.VMEM((128, length // 2), F32),
        ],
        compiler_params=pltpu.CompilerParams(vmem_limit_bytes=40 * MIB),
        cost_estimate=cost(32 * length * length * HS, 2 * length * length),
    )(weights, sums, queries_t, keys_t, received, received_grads)


def finish_kernel(dq_ref, dkv_ref, w_ref, x_ref, g_ref, gain_ref, out_ref, j_ref, n_ref):
    records = x_ref.shape[0]
    frames = x_ref.shape[1]
    width = x_ref.shape[2]
    features = HEADS * HS
    for r in range(records):
        for pair in range(HEADS // 2):
            item = r * HEADS + 2 * pair
            at = slice(pair * 128, (pair + 1) * 128)
            first, second = halves(dq_ref[item], dq_ref[item + 1])
            j_ref[r * frames : r * frames + 32, at] = first
            j_ref[r * frames + 32 : (r + 1) * frames, at] = second
            keys, values = halves(dkv_ref[item], dkv_ref[item + 1])
            span = slice(r * frames, (r + 1) * frames)
            j_ref[span, features + pair * 128 : features + (pair + 1) * 128] = keys
            j_ref[span, 2 * features + pair * 128 : 2 * features + (pair + 1) * 128] = values
    step = 256
    for n in range(width // step):
        n_ref[:, n * step : (n + 1) * step] = lax.dot_general(
            j_ref[...], w_ref[n * step : (n + 1) * step, :], ROW_DOT, preferred_element_type=F32
        )
    for r in range(records):
        x = x_ref[r].astype(F32)
        centred = x - jnp.mean(x, axis=1, keepdims=True)
        var = jnp.mean(centred * centred, axis=1, keepdims=True)
        deviation = lax.rsqrt(var + EPSILON)
        normal = centred * deviation
        scaled = n_ref[r * frames : (r + 1) * frames, :] * gain_ref[...]
        residual = deviation * (
            scaled
            - jnp.mean(scaled, axis=1, keepdims=True)
            - normal * jnp.mean(scaled * normal, axis=1, keepdims=True)
        )
        out_ref[r] = (g_ref[r].astype(F32) + residual).astype(BF16)


def finish(dq, dkv, weight, inputs, grads, gain):
    records, frames, width = inputs.shape
    return pl.pallas_call(
        finish_kernel,
        out_shape=jax.ShapeDtypeStruct(inputs.shape, BF16),
        in_specs=[WHOLE] * 6,
        out_specs=WHOLE,
        scratch_shapes=[
            pltpu.VMEM((records * frames, 3 * HEADS * HS), BF16),
            pltpu.VMEM((records * frames, width), F32),
        ],
        compiler_params=pltpu.CompilerParams(vmem_limit_bytes=40 * MIB),
        cost_estimate=cost(2 * records * frames * width * 3072, 2 * 3072 * width),
    )(dq, dkv, weight, inputs, grads, gain)


def exchange(items):
    return lax.all_to_all(items, "seq", split_axis=0, concat_axis=0, tiled=True)


def gathered_pieces(rows, seq):
    z = lax.rem(seq, Z)
    others = [lax.ppermute(rows, "seq", seq_pairs(0, 0, k)) for k in range(1, Z)]
    owners = jnp.stack([lax.rem(z - k + Z, Z) for k in range(Z)])
    group = place(owners, [rows] + others).reshape(Z * rows.shape[0], rows.shape[1])
    pieces = [group]
    steps = [(0, 0)]
    for dy, dx in ((0, 1), (1, 0), (3, 0), (1, 1), (3, 1), (2, 0), (2, 1)):
        pieces.append(lax.ppermute(group, "seq", seq_pairs(dy, dx, 0)))
        steps.append((dy, dx))
    y = seq // (X * Z)
    x = lax.rem(seq // Z, X)
    places = jnp.stack([lax.rem(y - dy + Y, Y) * X + lax.rem(x - dx + X, X) for dy, dx in steps])
    return places, pieces


def on_device(
    layer_input,
    norm_gain,
    queries,
    key_states,
    value_states,
    out_grad,
    out_weight,
    qkv_weight,
    lengths,
):
    frames, records, features = queries.shape[1:]
    width = out_grad.shape[3]
    seq = lax.axis_index("seq").astype(jnp.int32)
    flat = lambda array: array[0].reshape(frames, records * features)
    packed = pack_items(flat(queries), flat(key_states), flat(value_states))
    received = exchange(packed)
    grads = out_grad[0].transpose(1, 0, 2)
    inputs = layer_input[0].transpose(1, 0, 2)
    pairs, out_pieces = gathered_pieces(out_weight[0], seq)
    attn_grad = project(pairs, grads.reshape(records * frames, width), out_pieces)
    received_grads = exchange(attn_grad)
    record = seq // HEADS
    valid = jnp.sum(jnp.where(jnp.arange(records) == record, lengths[0], 0)).reshape(1)
    weights, sums, queries_t, keys_t = softmax_weights(valid, received)
    dq, dkv = attention_grads(weights, sums, queries_t, keys_t, received, received_grads)
    dq = exchange(dq)
    dkv = exchange(dkv)
    places, qkv_pieces = gathered_pieces(qkv_weight[0], seq)
    weight = place(places, qkv_pieces).reshape(width, 3 * features)
    result = finish(dq, dkv, weight, inputs, grads, norm_gain)
    count = lax.axis_size("section")
    moved = lax.ppermute(result, "section", [(i, (i - 1) % count) for i in range(count)])
    return moved.transpose(1, 0, 2)[None]


def solution(mesh):
    rows = P("section", "seq", None, None)
    in_specs = (
        rows,
        P("section", None),
        rows,
        rows,
        rows,
        rows,
        P("section", "seq", None),
        P("section", "seq", None),
        P("section", None),
    )
    return jax.shard_map(on_device, mesh=mesh, in_specs=in_specs, out_specs=rows, check_vma=False)
```

time: 698 us -> 433 us (0.62); the launches traced: 689 us -> 432 us
  matrix products: 134 us -> 0 us
  Pallas kernels: 0 us -> 128 us
  waiting for transfers between devices: 295 us -> 178 us
  local copies, waits for them, and re-layouts: 85.7 us -> 19.2 us
  other arithmetic: 57.5 us -> 0.66 us
  starting transfers between devices: 88.9 us -> 106 us
  loops' own time: 14.4 us -> 0 us
  between operations: 14.1 us -> 0.17 us
    all_gather x2 -> x0, waiting for transfers between devices: 223 us -> none  [the longest x1 201 us: project_grad(): lax.all_gather(out_rows, 'seq', axis=0, tiled=True)]
    ppermute x1 -> x29, waiting for transfers between devices: 11.6 us -> 178 us  [the longest x14 112 us: gathered_pieces(): pieces.append(lax.ppermute(group, 'seq', seq_pairs(dy, dx, 0)))]
    dot_general x42 -> x0, matrix products: 134 us -> none  [the longest x8 55.8 us: step(): lax.dot_general(probs_low, grad_block, COL_DOT, preferred_element_type=jn...]
    pallas_call x0 -> x8, Pallas kernels: none -> 128 us  [the longest x1 71.5 us: attention_grads(): pl.pallas_call(grads_kernel, grid=(blocks,), out_shape=[jax.ShapeDtypeStr...]
    all_to_all x7 -> x4, waiting for transfers between devices: 59.2 us -> 0.01 us  [exchange(): return lax.all_to_all(items, 'seq', split_axis=0, concat_axis=0, tiled=True)]
    convert_element_type x11 -> x0, other arithmetic: 34.2 us -> none  [the longest x8 31.5 us: step(): grad_scores = (probs * (grad_probs - centre) * scale).astype(jnp.bfloat16)]
    ppermute x1 -> x29, starting transfers between devices: 36.5 us -> 67 us  [the longest x14 29.2 us: gathered_pieces(): lax.ppermute(rows, 'seq', seq_pairs(0, 0, k))]
    while x49 -> x0, local copies, waits for them, and re-layouts: 27.8 us -> none
  transfers between devices with their start and end apart: 10 -> 33, of which waited for: 9 -> 22; matrix products, arithmetic and copies ran while one was open for 34% -> 1% of each run, Pallas kernels for 0% -> 12%
where the time goes in v1:
time: 433 us; the launch traced here: 432 us
  waiting for transfers between devices  178 us (41%)
  Pallas kernels  128 us (30%)
  starting transfers between devices  106 us (24%)
  local copies, waits for them, and re-layouts  19.2 us (4%)
    ppermute x14, waiting for transfers between devices, gathered_pieces(): pieces.append(lax.ppermute(group, 'seq', seq_pairs(dy, dx, 0)))  112 us
    pallas_call x1, Pallas kernels, attention_grads(): pl.pallas_call(grads_kernel, grid=(blocks,), out_shape=[jax.ShapeDtypeStr...  71.5 us
    ppermute x14, waiting for transfers between devices, gathered_pieces(): lax.ppermute(rows, 'seq', seq_pairs(0, 0, k))  54.2 us
    pallas_call x1, Pallas kernels, softmax_weights(): pl.pallas_call(weights_kernel, grid=(blocks,), out_shape=[jax.ShapeDtypeS...  43.9 us
    all_to_all x4, starting transfers between devices, exchange(): return lax.all_to_all(items, 'seq', split_axis=0, concat_axis=0, tiled=True)  39 us
    ppermute x14, starting transfers between devices, gathered_pieces(): lax.ppermute(rows, 'seq', seq_pairs(0, 0, k))  29.2 us
    ppermute x14, starting transfers between devices, gathered_pieces(): pieces.append(lax.ppermute(group, 'seq', seq_pairs(dy, dx, 0)))  26 us
    unnamed x29, local copies, waits for them, and re-layouts  17.6 us
  transfers between devices with their start and end apart: 33, of which 22 were waited for; matrix products, arithmetic and copies ran while one was open for 1% of the time, Pallas kernels for 12%

profile of v1, /device:TPU:1, one launch (start us, length us, event | category | flops | bytes accessed | tf_op | source)
XLA Modules:
  0.0 432.4 jit_solution(10940904541716585905)
XLA Ops:
  3.3 13.7 %all-to-all-start = ((bf16[64,96,128]{2,1,0:T(8,128)(2,1)}), bf16[64,96,128]{2,1,0:T(8,128)(2,1)S(1)}, u32[]{:S(2)}, u32[]{:S(2)}) async-start(bf16[64,96,128]{2,1,0:T(8,128)(2,1)} %shard_map.91), calls=%async_computation | async-start | bytes 3145728 | tf_op jit(solution)/shard_map/all_to_all | solution.py:333
  27.1 25.7 %collective-permute-done.refs_1_ = bf16[16,1536]{1,0:T(8,128)(2,1)S(1)} collective-permute-done((bf16[16,1536]{1,0:T(8,128)(2,1)S(1)}, bf16[16,1536]{1,0:T(8,128)(2,1)S(1)}, u32[]{:S(2)}, u32[]{:S(2)}) %collective-permute-start) | collective-permute-done | bytes 49184 | tf_op jit(solution)/shard_map/ppermute | solution.py:338
  58.5 3.9 collective-permute-done.3.refs_4_
  76.1 5.4 %collective-permute-done.10.refs_4_ = bf16[128,1536]{1,0:T(8,128)(2,1)} collective-permute-done((bf16[128,1536]{1,0:T(8,128)(2,1)S(1)}, bf16[128,1536]{1,0:T(8,128)(2,1)}, u32[]{:S(2)}, u32[]{:S(2)}) %collective-permute-start.10) | collective-permute-done | bytes 393248 | tf_op jit(solution)/shard_map/ppermute | solution.py:344
  81.4 7.0 %collective-permute-done.11.refs_5_ = bf16[128,1536]{1,0:T(8,128)(2,1)} collective-permute-done((bf16[128,1536]{1,0:T(8,128)(2,1)S(1)}, bf16[128,1536]{1,0:T(8,128)(2,1)}, u32[]{:S(2)}, u32[]{:S(2)}) %collective-permute-start.11) | collective-permute-done | bytes 393248 | tf_op jit(solution)/shard_map/ppermute | solution.py:344
  91.9 6.8 %collective-permute-done.13.refs_7_ = bf16[128,1536]{1,0:T(8,128)(2,1)} collective-permute-done((bf16[128,1536]{1,0:T(8,128)(2,1)S(1)}, bf16[128,1536]{1,0:T(8,128)(2,1)}, u32[]{:S(2)}, u32[]{:S(2)}) %collective-permute-start.13) | collective-permute-done | bytes 393248 | tf_op jit(solution)/shard_map/ppermute | solution.py:344
  98.7 4.1 shard_map.94
  102.9 6.5 %all-to-all-start.1 = ((bf16[64,32,128]{2,1,0:T(8,128)(2,1)}), bf16[64,32,128]{2,1,0:T(8,128)(2,1)S(1)}, u32[]{:S(2)}, u32[]{:S(2)}) async-start(bf16[64,32,128]{2,1,0:T(8,128)(2,1)} %shard_map.94), calls=%async_computation.1 | async-start | bytes 1048576 | tf_op jit(solution)/shard_map/all_to_all | solution.py:333
  110.1 43.9 %shard_map.92 = (bf16[16,4096,256]{2,1,0:T(8,128)(2,1)}, f32[1,4096]{1,0:T(1,128)S(1)}, bf16[128,4096]{1,0:T(8,128)(2,1)S(1)}, bf16[64,4096]{1,0:T(8,128)(2,1)S(1)}) custom-call(s32[1]{0:T(128)} %bitcast.1.length_ref, bf16[64,96,128]{2,1,0:T(8,128)(2,1)S(1)} %all-to-all-done.r_ref), custom_call_target="tpu_custom_call" | custom-call | flops 8589934592 | bytes 33554432 | tf_op jit(solution)/shard_map/pallas_call | solution.py:169
  156.2 71.5 %shard_map.95 = (bf16[64,32,128]{2,1,0:T(8,128)(2,1)}, bf16[64,64,128]{2,1,0:T(8,128)(2,1)S(1)}) custom-call(bf16[16,4096,256]{2,1,0:T(8,128)(2,1)} %get-tuple-element.11.w_ref, f32[1,4096]{1,0:T(1,128)S(1)} %get-tuple-element.12.l_ref, bf16[128,4096]{1,0:T(8,128)(2,1)S(1)} %copy-done.8, bf16[64,4096]{1,0:T(8,128)(2,1)S(1)} %get-tuple-element.14.kt_ref, ...), custom_call_target="tpu_custom_call" | custom-call | flops 34359738368 | bytes 33554432 | tf_op jit(solution)/shard_map/pallas_call | solution.py:260
  228.7 10.7 %all-to-all-start.2 = ((bf16[64,32,128]{2,1,0:T(8,128)(2,1)}), bf16[64,32,128]{2,1,0:T(8,128)(2,1)S(1)}, u32[]{:S(2)}, u32[]{:S(2)}) async-start(bf16[64,32,128]{2,1,0:T(8,128)(2,1)} %get-tuple-element.15), calls=%async_computation.2 | async-start | bytes 1048576 | tf_op jit(solution)/shard_map/all_to_all | solution.py:333
  255.7 7.6 %collective-permute-done.16.refs_3_ = bf16[24,3072]{1,0:T(8,128)(2,1)S(1)} collective-permute-done((bf16[24,3072]{1,0:T(8,128)(2,1)}, bf16[24,3072]{1,0:T(8,128)(2,1)S(1)}, u32[]{:S(2)}, u32[]{:S(2)}) %collective-permute-start.16) | collective-permute-done | bytes 147488 | tf_op jit(solution)/shard_map/ppermute | solution.py:338
  263.4 5.8 %collective-permute-done.17.refs_4_ = bf16[24,3072]{1,0:T(8,128)(2,1)S(1)} collective-permute-done((bf16[24,3072]{1,0:T(8,128)(2,1)}, bf16[24,3072]{1,0:T(8,128)(2,1)S(1)}, u32[]{:S(2)}, u32[]{:S(2)}) %collective-permute-start.17) | collective-permute-done | bytes 147488 | tf_op jit(solution)/shard_map/ppermute | solution.py:338
  269.2 4.9 %collective-permute-done.19.refs_6_ = bf16[24,3072]{1,0:T(8,128)(2,1)S(1)} collective-permute-done((bf16[24,3072]{1,0:T(8,128)(2,1)}, bf16[24,3072]{1,0:T(8,128)(2,1)S(1)}, u32[]{:S(2)}, u32[]{:S(2)}) %collective-permute-start.19) | collective-permute-done | bytes 147488 | tf_op jit(solution)/shard_map/ppermute | solution.py:338
  281.5 8.1 %all-to-all-start.3 = ((bf16[64,64,128]{2,1,0:T(8,128)(2,1)}), bf16[64,64,128]{2,1,0:T(8,128)(2,1)S(1)}, u32[]{:S(2)}, u32[]{:S(2)}) async-start(bf16[64,64,128]{2,1,0:T(8,128)(2,1)} %copy-done.3), calls=%async_computation.3 | async-start | bytes 2097152 | tf_op jit(solution)/shard_map/all_to_all | solution.py:333
  295.7 14.0 %collective-permute-done.21.refs_1_ = bf16[192,3072]{1,0:T(8,128)(2,1)} collective-permute-done((bf16[192,3072]{1,0:T(8,128)(2,1)S(1)}, bf16[192,3072]{1,0:T(8,128)(2,1)}, u32[]{:S(2)}, u32[]{:S(2)}) %collective-permute-start.21) | collective-permute-done | bytes 1179680 | tf_op jit(solution)/shard_map/ppermute | solution.py:344
  317.8 9.1 %collective-permute-done.23.refs_3_ = bf16[192,3072]{1,0:T(8,128)(2,1)S(1)} collective-permute-done((bf16[192,3072]{1,0:T(8,128)(2,1)S(1)}, bf16[192,3072]{1,0:T(8,128)(2,1)S(1)}, u32[]{:S(2)}, u32[]{:S(2)}) %collective-permute-start.23) | collective-permute-done | bytes 1179680 | tf_op jit(solution)/shard_map/ppermute | solution.py:344
  326.9 14.5 %collective-permute-done.24.refs_4_ = bf16[192,3072]{1,0:T(8,128)(2,1)S(1)} collective-permute-done((bf16[192,3072]{1,0:T(8,128)(2,1)S(1)}, bf16[192,3072]{1,0:T(8,128)(2,1)S(1)}, u32[]{:S(2)}, u32[]{:S(2)}) %collective-permute-start.24) | collective-permute-done | bytes 1179680 | tf_op jit(solution)/shard_map/ppermute | solution.py:344
  341.4 23.9 %collective-permute-done.25.refs_5_ = bf16[192,3072]{1,0:T(8,128)(2,1)S(1)} collective-permute-done((bf16[192,3072]{1,0:T(8,128)(2,1)S(1)}, bf16[192,3072]{1,0:T(8,128)(2,1)S(1)}, u32[]{:S(2)}, u32[]{:S(2)}) %collective-permute-start.25) | collective-permute-done | bytes 1179680 | tf_op jit(solution)/shard_map/ppermute | solution.py:344
  367.6 25.3 %collective-permute-done.27.refs_7_ = bf16[192,3072]{1,0:T(8,128)(2,1)S(1)} collective-permute-done((bf16[192,3072]{1,0:T(8,128)(2,1)S(1)}, bf16[192,3072]{1,0:T(8,128)(2,1)S(1)}, u32[]{:S(2)}, u32[]{:S(2)}) %collective-permute-start.27) | collective-permute-done | bytes 1179680 | tf_op jit(solution)/shard_map/ppermute | solution.py:344
  395.2 3.6 copy-done
  398.8 3.7 copy-done.1
  407.0 11.9 %collective-permute-start.28 = (bf16[4,64,1536]{2,1,0:T(8,128)(2,1)S(1)}, bf16[4,64,1536]{2,1,0:T(8,128)(2,1)S(1)}, u32[]{:S(2)}, u32[]{:S(2)}) collective-permute-start(bf16[4,64,1536]{2,1,0:T(8,128)(2,1)S(1)} %shard_map.98), channel_id=1, source_target_pairs={{0,192},{64,0},{128,64},{192,128},{1,193},{65,1},{129,65},{193,129... | collective-permute-start | bytes 2359304 | tf_op jit(solution)/shard_map/ppermute | solution.py:384
  418.9 12.0 %collective-permute-done.28 = bf16[4,64,1536]{2,1,0:T(8,128)(2,1)S(1)} collective-permute-done((bf16[4,64,1536]{2,1,0:T(8,128)(2,1)S(1)}, bf16[4,64,1536]{2,1,0:T(8,128)(2,1)S(1)}, u32[]{:S(2)}, u32[]{:S(2)}) %collective-permute-start.28) | collective-permute-done | bytes 786464 | tf_op jit(solution)/shard_map/ppermute | solution.py:384
  (83 shorter events, 88.5 us)
Async XLA Ops:
  3.3 99.5 %all-to-all-start = ((bf16[64,96,128]{2,1,0:T(8,128)(2,1)}), bf16[64,96,128]{2,1,0:T(8,128)(2,1)S(1)}, u32[]{:S(2)}, u32[]{:S(2)}) async-start(bf16[64,96,128]{2,1,0:T(8,128)(2,1)} %shard_map.91), calls=%async_computation | async-start | bytes 3145728 | tf_op jit(solution)/shard_map/all_to_all | solution.py:333
  17.0 35.7 %collective-permute-start = (bf16[16,1536]{1,0:T(8,128)(2,1)S(1)}, bf16[16,1536]{1,0:T(8,128)(2,1)S(1)}, u32[]{:S(2)}, u32[]{:S(2)}) collective-permute-start(bf16[16,1536]{1,0:T(8,128)(2,1)S(1)} %bitcast.79), channel_id=1, source_target_pairs={{0,1},{1,2},{2,3},{3,4},{4,5},{5,6},{6,7},{7,0},{8,9},{9,10},{10,1... | collective-permute-start | bytes 147464 | tf_op jit(solution)/shard_map/ppermute | solution.py:338
  18.1 37.7 %collective-permute-start.1 = (bf16[16,1536]{1,0:T(8,128)(2,1)S(1)}, bf16[16,1536]{1,0:T(8,128)(2,1)S(1)}, u32[]{:S(2)}, u32[]{:S(2)}) collective-permute-start(bf16[16,1536]{1,0:T(8,128)(2,1)S(1)} %bitcast.80), channel_id=1, source_target_pairs={{0,2},{1,3},{2,4},{3,5},{4,6},{5,7},{6,0},{7,1},{8,10},{9,11},{10,... | collective-permute-start | bytes 147464 | tf_op jit(solution)/shard_map/ppermute | solution.py:338
  20.2 38.3 %collective-permute-start.2 = (bf16[16,1536]{1,0:T(8,128)(2,1)S(1)}, bf16[16,1536]{1,0:T(8,128)(2,1)S(1)}, u32[]{:S(2)}, u32[]{:S(2)}) collective-permute-start(bf16[16,1536]{1,0:T(8,128)(2,1)S(1)} %bitcast.81), channel_id=1, source_target_pairs={{0,3},{1,4},{2,5},{3,6},{4,7},{5,0},{6,1},{7,2},{8,11},{9,12},{10,... | collective-permute-start | bytes 147464 | tf_op jit(solution)/shard_map/ppermute | solution.py:338
  22.6 39.8 %collective-permute-start.3 = (bf16[16,1536]{1,0:T(8,128)(2,1)S(1)}, bf16[16,1536]{1,0:T(8,128)(2,1)S(1)}, u32[]{:S(2)}, u32[]{:S(2)}) collective-permute-start(bf16[16,1536]{1,0:T(8,128)(2,1)S(1)} %bitcast.82), channel_id=1, source_target_pairs={{0,4},{1,5},{2,6},{3,7},{4,0},{5,1},{6,2},{7,3},{8,12},{9,13},{10,... | collective-permute-start | bytes 147464 | tf_op jit(solution)/shard_map/ppermute | solution.py:338
  24.7 37.7 %collective-permute-start.4 = (bf16[16,1536]{1,0:T(8,128)(2,1)S(1)}, bf16[16,1536]{1,0:T(8,128)(2,1)S(1)}, u32[]{:S(2)}, u32[]{:S(2)}) collective-permute-start(bf16[16,1536]{1,0:T(8,128)(2,1)S(1)} %bitcast.83), channel_id=1, source_target_pairs={{0,5},{1,6},{2,7},{3,0},{4,1},{5,2},{6,3},{7,4},{8,13},{9,14},{10,... | collective-permute-start | bytes 147464 | tf_op jit(solution)/shard_map/ppermute | solution.py:338
  67.0 21.5 %collective-permute-start.11 = (bf16[128,1536]{1,0:T(8,128)(2,1)S(1)}, bf16[128,1536]{1,0:T(8,128)(2,1)}, u32[]{:S(2)}, u32[]{:S(2)}) collective-permute-start(bf16[128,1536]{1,0:T(8,128)(2,1)S(1)} %bitcast.67), channel_id=1, source_target_pairs={{0,56},{1,57},{2,58},{3,59},{4,60},{5,61},{6,62},{7,63},{8,48},{9,... | collective-permute-start | bytes 1179656 | tf_op jit(solution)/shard_map/ppermute | solution.py:344
  70.8 21.1 %collective-permute-start.12 = (bf16[128,1536]{1,0:T(8,128)(2,1)S(1)}, bf16[128,1536]{1,0:T(8,128)(2,1)}, u32[]{:S(2)}, u32[]{:S(2)}) collective-permute-start(bf16[128,1536]{1,0:T(8,128)(2,1)S(1)} %bitcast.68), channel_id=1, source_target_pairs={{0,32},{1,33},{2,34},{3,35},{4,36},{5,37},{6,38},{7,39},{8,40},{9,... | collective-permute-start | bytes 1179656 | tf_op jit(solution)/shard_map/ppermute | solution.py:344
  73.4 25.3 %collective-permute-start.13 = (bf16[128,1536]{1,0:T(8,128)(2,1)S(1)}, bf16[128,1536]{1,0:T(8,128)(2,1)}, u32[]{:S(2)}, u32[]{:S(2)}) collective-permute-start(bf16[128,1536]{1,0:T(8,128)(2,1)S(1)} %bitcast.69), channel_id=1, source_target_pairs={{0,40},{1,41},{2,42},{3,43},{4,44},{5,45},{6,46},{7,47},{8,32},{9,... | collective-permute-start | bytes 1179656 | tf_op jit(solution)/shard_map/ppermute | solution.py:344
  102.9 52.1 %all-to-all-start.1 = ((bf16[64,32,128]{2,1,0:T(8,128)(2,1)}), bf16[64,32,128]{2,1,0:T(8,128)(2,1)S(1)}, u32[]{:S(2)}, u32[]{:S(2)}) async-start(bf16[64,32,128]{2,1,0:T(8,128)(2,1)} %shard_map.94), calls=%async_computation.1 | async-start | bytes 1048576 | tf_op jit(solution)/shard_map/all_to_all | solution.py:333
  228.7 52.8 %all-to-all-start.2 = ((bf16[64,32,128]{2,1,0:T(8,128)(2,1)}), bf16[64,32,128]{2,1,0:T(8,128)(2,1)S(1)}, u32[]{:S(2)}, u32[]{:S(2)}) async-start(bf16[64,32,128]{2,1,0:T(8,128)(2,1)} %get-tuple-element.15), calls=%async_computation.2 | async-start | bytes 1048576 | tf_op jit(solution)/shard_map/all_to_all | solution.py:333
  245.0 24.2 %collective-permute-start.17 = (bf16[24,3072]{1,0:T(8,128)(2,1)}, bf16[24,3072]{1,0:T(8,128)(2,1)S(1)}, u32[]{:S(2)}, u32[]{:S(2)}) collective-permute-start(bf16[24,3072]{1,0:T(8,128)(2,1)} %bitcast.74), channel_id=1, source_target_pairs={{0,4},{1,5},{2,6},{3,7},{4,0},{5,1},{6,2},{7,3},{8,12},{9,13},{10,... | collective-permute-start | bytes 442376 | tf_op jit(solution)/shard_map/ppermute | solution.py:338
  247.1 22.1 %collective-permute-start.18 = (bf16[24,3072]{1,0:T(8,128)(2,1)}, bf16[24,3072]{1,0:T(8,128)(2,1)S(1)}, u32[]{:S(2)}, u32[]{:S(2)}) collective-permute-start(bf16[24,3072]{1,0:T(8,128)(2,1)} %bitcast.75), channel_id=1, source_target_pairs={{0,5},{1,6},{2,7},{3,0},{4,1},{5,2},{6,3},{7,4},{8,13},{9,14},{10,... | collective-permute-start | bytes 442376 | tf_op jit(solution)/shard_map/ppermute | solution.py:338
  249.5 24.6 %collective-permute-start.19 = (bf16[24,3072]{1,0:T(8,128)(2,1)}, bf16[24,3072]{1,0:T(8,128)(2,1)S(1)}, u32[]{:S(2)}, u32[]{:S(2)}) collective-permute-start(bf16[24,3072]{1,0:T(8,128)(2,1)} %bitcast.76), channel_id=1, source_target_pairs={{0,6},{1,7},{2,0},{3,1},{4,2},{5,3},{6,4},{7,5},{8,14},{9,15},{10,... | collective-permute-start | bytes 442376 | tf_op jit(solution)/shard_map/ppermute | solution.py:338
  253.4 24.1 %collective-permute-start.20 = (bf16[24,3072]{1,0:T(8,128)(2,1)}, bf16[24,3072]{1,0:T(8,128)(2,1)S(1)}, u32[]{:S(2)}, u32[]{:S(2)}) collective-permute-start(bf16[24,3072]{1,0:T(8,128)(2,1)} %bitcast.77), channel_id=1, source_target_pairs={{0,7},{1,0},{2,1},{3,2},{4,3},{5,4},{6,5},{7,6},{8,15},{9,8},{10,9... | collective-permute-start | bytes 442376 | tf_op jit(solution)/shard_map/ppermute | solution.py:338
  279.0 30.6 %collective-permute-start.21 = (bf16[192,3072]{1,0:T(8,128)(2,1)S(1)}, bf16[192,3072]{1,0:T(8,128)(2,1)}, u32[]{:S(2)}, u32[]{:S(2)}) collective-permute-start(bf16[192,3072]{1,0:T(8,128)(2,1)S(1)} %bitcast.51), channel_id=1, source_target_pairs={{0,8},{1,9},{2,10},{3,11},{4,12},{5,13},{6,14},{7,15},{8,0},{9,1},... | collective-permute-start | bytes 3538952 | tf_op jit(solution)/shard_map/ppermute | solution.py:344
  280.3 32.0 %collective-permute-start.22 = (bf16[192,3072]{1,0:T(8,128)(2,1)S(1)}, bf16[192,3072]{1,0:T(8,128)(2,1)}, u32[]{:S(2)}, u32[]{:S(2)}) collective-permute-start(bf16[192,3072]{1,0:T(8,128)(2,1)S(1)} %bitcast.52), channel_id=1, source_target_pairs={{0,16},{1,17},{2,18},{3,19},{4,20},{5,21},{6,22},{7,23},{8,24},{9,... | collective-permute-start | bytes 3538952 | tf_op jit(solution)/shard_map/ppermute | solution.py:344
  281.5 117.3 %all-to-all-start.3 = ((bf16[64,64,128]{2,1,0:T(8,128)(2,1)}), bf16[64,64,128]{2,1,0:T(8,128)(2,1)S(1)}, u32[]{:S(2)}, u32[]{:S(2)}) async-start(bf16[64,64,128]{2,1,0:T(8,128)(2,1)} %copy-done.3), calls=%async_computation.3 | async-start | bytes 2097152 | tf_op jit(solution)/shard_map/all_to_all | solution.py:333
  289.6 37.3 %collective-permute-start.23 = (bf16[192,3072]{1,0:T(8,128)(2,1)S(1)}, bf16[192,3072]{1,0:T(8,128)(2,1)S(1)}, u32[]{:S(2)}, u32[]{:S(2)}) collective-permute-start(bf16[192,3072]{1,0:T(8,128)(2,1)S(1)} %bitcast.53), channel_id=1, source_target_pairs={{0,48},{1,49},{2,50},{3,51},{4,52},{5,53},{6,54},{7,55},{8,56},{9,... | collective-permute-start | bytes 3538952 | tf_op jit(solution)/shard_map/ppermute | solution.py:344
  292.1 49.3 %collective-permute-start.24 = (bf16[192,3072]{1,0:T(8,128)(2,1)S(1)}, bf16[192,3072]{1,0:T(8,128)(2,1)S(1)}, u32[]{:S(2)}, u32[]{:S(2)}) collective-permute-start(bf16[192,3072]{1,0:T(8,128)(2,1)S(1)} %bitcast.54), channel_id=1, source_target_pairs={{0,24},{1,25},{2,26},{3,27},{4,28},{5,29},{6,30},{7,31},{8,16},{9,... | collective-permute-start | bytes 3538952 | tf_op jit(solution)/shard_map/ppermute | solution.py:344
  292.1 73.2 %collective-permute-start.25 = (bf16[192,3072]{1,0:T(8,128)(2,1)S(1)}, bf16[192,3072]{1,0:T(8,128)(2,1)S(1)}, u32[]{:S(2)}, u32[]{:S(2)}) collective-permute-start(bf16[192,3072]{1,0:T(8,128)(2,1)S(1)} %bitcast.55), channel_id=1, source_target_pairs={{0,56},{1,57},{2,58},{3,59},{4,60},{5,61},{6,62},{7,63},{8,48},{9,... | collective-permute-start | bytes 3538952 | tf_op jit(solution)/shard_map/ppermute | solution.py:344
  309.7 58.0 %collective-permute-start.26 = (bf16[192,3072]{1,0:T(8,128)(2,1)S(1)}, bf16[192,3072]{1,0:T(8,128)(2,1)S(1)}, u32[]{:S(2)}, u32[]{:S(2)}) collective-permute-start(bf16[192,3072]{1,0:T(8,128)(2,1)S(1)} %bitcast.56), channel_id=1, source_target_pairs={{0,32},{1,33},{2,34},{3,35},{4,36},{5,37},{6,38},{7,39},{8,40},{9,... | collective-permute-start | bytes 3538952 | tf_op jit(solution)/shard_map/ppermute | solution.py:344
  312.3 80.6 %collective-permute-start.27 = (bf16[192,3072]{1,0:T(8,128)(2,1)S(1)}, bf16[192,3072]{1,0:T(8,128)(2,1)S(1)}, u32[]{:S(2)}, u32[]{:S(2)}) collective-permute-start(bf16[192,3072]{1,0:T(8,128)(2,1)S(1)} %bitcast.57), channel_id=1, source_target_pairs={{0,40},{1,41},{2,42},{3,43},{4,44},{5,45},{6,46},{7,47},{8,32},{9,... | collective-permute-start | bytes 3538952 | tf_op jit(solution)/shard_map/ppermute | solution.py:344
  407.0 23.9 %collective-permute-start.28 = (bf16[4,64,1536]{2,1,0:T(8,128)(2,1)S(1)}, bf16[4,64,1536]{2,1,0:T(8,128)(2,1)S(1)}, u32[]{:S(2)}, u32[]{:S(2)}) collective-permute-start(bf16[4,64,1536]{2,1,0:T(8,128)(2,1)S(1)} %shard_map.98), channel_id=1, source_target_pairs={{0,192},{64,0},{128,64},{192,128},{1,193},{65,1},{129,65},{193,129... | collective-permute-start | bytes 2359304 | tf_op jit(solution)/shard_map/ppermute | solution.py:384
  (21 other events, 222.7 us)

commit v2 on v1

v2 whole, which is shorter than its diff:
```python
import functools

import jax
import jax.numpy as jnp
from jax import lax
from jax.experimental import pallas as pl
from jax.experimental.pallas import tpu as pltpu
from jax.sharding import PartitionSpec as P

HEADS = 16
HS = 64
EPSILON = 1e-05
MASKED = -1e30
SCALE = HS**-0.5
ROW_DOT = (((1,), (1,)), ((), ()))
PLAIN_DOT = (((1,), (0,)), ((), ()))
MIB = 1024 * 1024
QB = 256
KB = 256
UNROLL1 = True
UNROLL2 = True
Y, X, Z = 4, 2, 8
BF16 = jnp.bfloat16
F32 = jnp.float32
WHOLE = pl.BlockSpec(memory_space=pltpu.VMEM)


def cost(flops, moved, exps=0):
    return pl.CostEstimate(flops=flops, bytes_accessed=moved, transcendentals=exps)


def halves(even, odd):
    first = jnp.concatenate([even[:, :HS], odd[:, :HS]], axis=1)
    second = jnp.concatenate([even[:, HS:], odd[:, HS:]], axis=1)
    return first, second


def seq_pairs(dy, dx, dz):
    pairs = []
    for y in range(Y):
        for x in range(X):
            for z in range(Z):
                to = ((y + dy) % Y) * X * Z + ((x + dx) % X) * Z + (z + dz) % Z
                pairs.append((y * X * Z + x * Z + z, to))
    return pairs


def pack_kernel(q_ref, k_ref, v_ref, out_ref):
    half = q_ref.shape[0] // 2
    for n, ref in enumerate((q_ref, k_ref, v_ref)):
        for pair in range(ref.shape[1] // 128):
            tile = ref[:, pair * 128 : (pair + 1) * 128]
            first, second = halves(tile[:half], tile[half:])
            out_ref[2 * pair, n * half : (n + 1) * half, :] = first
            out_ref[2 * pair + 1, n * half : (n + 1) * half, :] = second


def pack_items(q, k, v):
    frames, lanes = q.shape
    out = jax.ShapeDtypeStruct((lanes // HS, 3 * frames // 2, 128), BF16)
    return pl.pallas_call(
        pack_kernel,
        out_shape=out,
        in_specs=[WHOLE] * 3,
        out_specs=WHOLE,
        compiler_params=pltpu.CompilerParams(vmem_limit_bytes=16 * MIB),
        cost_estimate=cost(0, 3 * MIB),
    )(q, k, v)


def place_kernel(owner_ref, *refs):
    out_ref = refs[-1]
    for n, ref in enumerate(refs[:-1]):
        out_ref[owner_ref[n]] = ref[...]


def place(owners, pieces):
    out = jax.ShapeDtypeStruct((len(pieces),) + pieces[0].shape, BF16)
    size = 2 * len(pieces) * pieces[0].size
    return pl.pallas_call(
        place_kernel,
        out_shape=out,
        in_specs=[pl.BlockSpec(memory_space=pltpu.SMEM)] + [WHOLE] * len(pieces),
        out_specs=WHOLE,
        compiler_params=pltpu.CompilerParams(vmem_limit_bytes=2 * size + 4 * MIB),
        cost_estimate=cost(0, 2 * size),
    )(owners, *pieces)


def project_kernel(owner_ref, grad_ref, *refs):
    out_ref = refs[-1]
    records = grad_ref.shape[0] // 64
    grads = grad_ref[...]
    for n, ref in enumerate(refs[:-1]):
        owner = owner_ref[n]
        tile = lax.dot_general(grads, ref[...], ROW_DOT, preferred_element_type=F32).astype(BF16)
        for r in range(records):
            first, second = halves(tile[r * 64 : r * 64 + 32], tile[r * 64 + 32 : r * 64 + 64])
            out_ref[r * HEADS + 2 * owner] = first
            out_ref[r * HEADS + 2 * owner + 1] = second


def project(owners, grads, pieces):
    rows, width = grads.shape
    items = (rows // 64) * HEADS
    return pl.pallas_call(
        project_kernel,
        out_shape=jax.ShapeDtypeStruct((items, 32, 128), BF16),
        in_specs=[pl.BlockSpec(memory_space=pltpu.SMEM)] + [WHOLE] * (1 + len(pieces)),
        out_specs=WHOLE,
        compiler_params=pltpu.CompilerParams(vmem_limit_bytes=20 * MIB),
        cost_estimate=cost(2 * rows * width * 1024, 2 * (rows * width + 1024 * width + rows * 1024)),
    )(owners, grads, *pieces)


def fold(values, op):
    return op(values.reshape(values.shape[0] // 8, 8, values.shape[1]), axis=0)


def prepare_kernel(length_ref, r_ref, kz_ref, qt_ref, kt_ref):
    sources = r_ref.shape[0]
    rows = sources * 32
    length = 2 * rows
    valid = length_ref[0]
    packed_q = r_ref[:, 0:32, :].reshape(rows, 128)
    packed_k = r_ref[:, 32:64, :].reshape(rows, 128)
    q_turned = packed_q.T
    k_turned = packed_k.T
    for half in range(2):
        qt_ref[0:HS, half * rows : (half + 1) * rows] = q_turned[half * HS : (half + 1) * HS, :]
        kt_ref[:, half * rows : (half + 1) * rows] = k_turned[half * HS : (half + 1) * HS, :]
    row_id = lax.broadcasted_iota(jnp.int32, (HS, length), 0)
    qt_ref[HS:128, :] = jnp.where(row_id == 0, 1.0, 0.0).astype(BF16)
    spot = lax.broadcasted_iota(jnp.int32, (rows, HS), 0)
    lane = lax.broadcasted_iota(jnp.int32, (rows, HS), 1)
    for half in range(2):
        frame = (spot // 32) * 64 + half * 32 + spot % 32
        bias = jnp.where((lane == 0) & (frame >= valid), MASKED, 0.0).astype(BF16)
        keys = packed_k[:, half * HS : (half + 1) * HS] * SCALE
        kz_ref[half * rows : (half + 1) * rows, :] = jnp.concatenate([keys.astype(BF16), bias], axis=1)


def prepare(valid, received):
    length = received.shape[0] * 64
    return pl.pallas_call(
        prepare_kernel,
        out_shape=[
            jax.ShapeDtypeStruct((length, 128), BF16),
            jax.ShapeDtypeStruct((128, length), BF16),
            jax.ShapeDtypeStruct((HS, length), BF16),
        ],
        in_specs=[pl.BlockSpec(memory_space=pltpu.SMEM), WHOLE],
        out_specs=[WHOLE] * 3,
        compiler_params=pltpu.CompilerParams(vmem_limit_bytes=16 * MIB),
        cost_estimate=cost(0, 4 * MIB),
    )(valid, received)


def weights_kernel(kz_ref, qt_ref, w_ref, l_ref, s_ref):
    length = kz_ref.shape[0]
    queries = qt_ref[...]

    def first(j, top):
        at = pl.ds(pl.multiple_of(j * KB, KB), KB)
        s = lax.dot_general(kz_ref[at, :], queries, PLAIN_DOT, preferred_element_type=F32)
        s_ref[at, :] = s
        return jnp.maximum(top, fold(s, jnp.max))

    top = lax.fori_loop(0, length // KB, first, jnp.full((8, QB), -jnp.inf, F32), unroll=UNROLL1)
    top = jnp.max(top, axis=0, keepdims=True)

    def second(j, total):
        at = pl.ds(pl.multiple_of(j * KB, KB), KB)
        w = jnp.exp(s_ref[at, :] - top)
        w_ref[0, at, :] = w
        return total + fold(w, jnp.sum)

    total = lax.fori_loop(0, length // KB, second, jnp.zeros((8, QB), F32), unroll=UNROLL1)
    l_ref[...] = jnp.sum(total, axis=0, keepdims=True)


def softmax_weights(part, keys, queries_t):
    length = keys.shape[0]
    blocks = length // QB // 2
    return pl.pallas_call(
        weights_kernel,
        grid=(blocks,),
        out_shape=[
            jax.ShapeDtypeStruct((blocks, length, QB), F32),
            jax.ShapeDtypeStruct((1, length // 2), F32),
        ],
        in_specs=[WHOLE, pl.BlockSpec((128, QB), lambda i: (0, part * blocks + i))],
        out_specs=[
            pl.BlockSpec((1, length, QB), lambda i: (i, 0, 0)),
            pl.BlockSpec((1, QB), lambda i: (0, i)),
        ],
        scratch_shapes=[pltpu.VMEM((length, QB), F32)],
        compiler_params=pltpu.CompilerParams(vmem_limit_bytes=24 * MIB),
        cost_estimate=cost(4 * length * length * HS, 2 * length * length, length * length // 2),
    )(keys, queries_t)


def grads_kernel(part, w_ref, l_ref, qt_ref, kt_ref, r_ref, g_ref, *refs):
    if part == 0:
        dq_ref, acc_ref, gt_ref, dp_ref = refs
    else:
        begun_dq_ref, begun_ref, out_ref, gt_ref, dp_ref, acc_ref, dq_ref = refs
    step = pl.program_id(0)
    sources = r_ref.shape[0]
    rows = sources * 32
    length = 2 * rows
    per = KB // 32

    @pl.when(step == 0)
    def _():
        gt_ref[...] = g_ref[...].reshape(rows, 128).T[part * HS : (part + 1) * HS, :]
        acc_ref[...] = jnp.zeros_like(acc_ref) if part == 0 else begun_ref[...]

    here = pl.ds(pl.multiple_of(step * QB, QB), QB)
    grads = gt_ref[:, here]
    none = jnp.zeros((HS, QB), BF16)
    inverse = 1.0 / l_ref[...]

    def first(half, side, j, centre):
        at = pl.ds(pl.multiple_of(half * rows + j * KB, KB), KB)
        values = r_ref[pl.ds(j * per, per), 64:96, :].reshape(KB, 128)
        dp = lax.dot_general(values, side, PLAIN_DOT, preferred_element_type=F32)
        dp_ref[at, :] = dp
        return centre + fold(w_ref[0, at, :] * inverse * dp, jnp.sum)

    centre = jnp.zeros((8, QB), F32)
    for half in range(2):
        side = jnp.concatenate([grads, none] if half == 0 else [none, grads], axis=0)
        centre = lax.fori_loop(0, rows // KB, functools.partial(first, half, side), centre, unroll=UNROLL2)
    centre = jnp.sum(centre, axis=0, keepdims=True)

    scaled_q = (qt_ref[0:HS, :] * SCALE).astype(BF16)
    side_t = jnp.concatenate([scaled_q, none], axis=0)
    side_w = jnp.concatenate([none, grads], axis=0)

    def second(j, dqt):
        at = pl.ds(pl.multiple_of(j * KB, KB), KB)
        p = w_ref[0, at, :] * inverse
        t = (p * (dp_ref[at, :] - centre)).astype(BF16)
        acc_ref[at, :] += lax.dot_general(
            t, side_t, ROW_DOT, preferred_element_type=F32
        ) + lax.dot_general(p.astype(BF16), side_w, ROW_DOT, preferred_element_type=F32)
        return dqt + lax.dot_general(kt_ref[:, at], t, PLAIN_DOT, preferred_element_type=F32)

    dqt = lax.fori_loop(0, length // KB, second, jnp.zeros((HS, QB), F32), unroll=UNROLL2)
    dq_ref[:, here] = dqt * SCALE

    if part == 1:

        @pl.when(step == pl.num_programs(0) - 1)
        def _():
            both = jnp.concatenate([begun_dq_ref[...], dq_ref[...]], axis=0)
            out_ref[:, 0:32, :] = both.T.astype(BF16).reshape(sources, 32, 128)
            for half in range(2):
                lanes = acc_ref[half * rows : (half + 1) * rows, :].astype(BF16)
                at = slice(32 + half * 32, 64 + half * 32)
                out_ref[:, at, :] = lanes.reshape(sources, 32, 128)


def attention_grads(part, weights, sums, queries_t, keys_t, received, received_grads, begun=()):
    blocks, length, _ = weights.shape
    sources = received.shape[0]
    dq = jax.ShapeDtypeStruct((HS, length // 2), F32)
    acc = jax.ShapeDtypeStruct((length, 128), F32)
    scratch = [pltpu.VMEM((HS, length // 2), BF16), pltpu.VMEM((length, QB), F32)]
    if part == 0:
        out_shape = [dq, acc]
        out_specs = [WHOLE, WHOLE]
    else:
        out_shape = jax.ShapeDtypeStruct((sources, 96, 128), BF16)
        out_specs = WHOLE
        scratch += [pltpu.VMEM((length, 128), F32), pltpu.VMEM((HS, length // 2), F32)]
    return pl.pallas_call(
        functools.partial(grads_kernel, part),
        grid=(blocks,),
        out_shape=out_shape,
        in_specs=[
            pl.BlockSpec((1, length, QB), lambda i: (i, 0, 0)),
            pl.BlockSpec((1, QB), lambda i: (0, i)),
            pl.BlockSpec((128, QB), lambda i: (0, part * blocks + i)),
        ]
        + [WHOLE] * (3 + len(begun)),
        out_specs=out_specs,
        scratch_shapes=scratch,
        compiler_params=pltpu.CompilerParams(vmem_limit_bytes=40 * MIB),
        cost_estimate=cost(16 * length * length * HS, 2 * length * length),
    )(weights, sums, queries_t, keys_t, received, received_grads, *begun)


def finish_kernel(back_ref, w_ref, x_ref, g_ref, gain_ref, out_ref, j_ref, n_ref):
    records = x_ref.shape[0]
    frames = x_ref.shape[1]
    width = x_ref.shape[2]
    features = HEADS * HS
    for r in range(records):
        for pair in range(HEADS // 2):
            item = r * HEADS + 2 * pair
            at = slice(pair * 128, (pair + 1) * 128)
            first, second = halves(back_ref[item, 0:32], back_ref[item + 1, 0:32])
            j_ref[r * frames : r * frames + 32, at] = first
            j_ref[r * frames + 32 : (r + 1) * frames, at] = second
            keys, values = halves(back_ref[item, 32:96], back_ref[item + 1, 32:96])
            span = slice(r * frames, (r + 1) * frames)
            j_ref[span, features + pair * 128 : features + (pair + 1) * 128] = keys
            j_ref[span, 2 * features + pair * 128 : 2 * features + (pair + 1) * 128] = values
    step = 256
    for n in range(width // step):
        n_ref[:, n * step : (n + 1) * step] = lax.dot_general(
            j_ref[...], w_ref[n * step : (n + 1) * step, :], ROW_DOT, preferred_element_type=F32
        )
    for r in range(records):
        x = x_ref[r].astype(F32)
        centred = x - jnp.mean(x, axis=1, keepdims=True)
        var = jnp.mean(centred * centred, axis=1, keepdims=True)
        deviation = lax.rsqrt(var + EPSILON)
        normal = centred * deviation
        scaled = n_ref[r * frames : (r + 1) * frames, :] * gain_ref[...]
        residual = deviation * (
            scaled
            - jnp.mean(scaled, axis=1, keepdims=True)
            - normal * jnp.mean(scaled * normal, axis=1, keepdims=True)
        )
        out_ref[r] = (g_ref[r].astype(F32) + residual).astype(BF16)


def finish(back, weight, inputs, grads, gain):
    records, frames, width = inputs.shape
    return pl.pallas_call(
        finish_kernel,
        out_shape=jax.ShapeDtypeStruct(inputs.shape, BF16),
        in_specs=[WHOLE] * 5,
        out_specs=WHOLE,
        scratch_shapes=[
            pltpu.VMEM((records * frames, 3 * HEADS * HS), BF16),
            pltpu.VMEM((records * frames, width), F32),
        ],
        compiler_params=pltpu.CompilerParams(vmem_limit_bytes=40 * MIB),
        cost_estimate=cost(2 * records * frames * width * 3072, 2 * 3072 * width),
    )(back, weight, inputs, grads, gain)


def exchange(items, groups=None):
    return lax.all_to_all(items, "seq", split_axis=0, concat_axis=0, tiled=True, axis_index_groups=groups)


def after(value, *others):
    return lax.optimization_barrier((value,) + others)[0]


def across(rows, dy, dx):
    return lax.ppermute(rows, "seq", seq_pairs(dy, dx, 0))


NEAR = ((0, 1), (1, 0), (3, 0))
DIAGONAL = ((1, 1), (3, 1))
FAR = ((2, 0), (2, 1))
STEPS = ((0, 0),) + NEAR + DIAGONAL + FAR


def on_device(
    layer_input,
    norm_gain,
    queries,
    key_states,
    value_states,
    out_grad,
    out_weight,
    qkv_weight,
    lengths,
):
    frames, records, features = queries.shape[1:]
    width = out_grad.shape[3]
    seq = lax.axis_index("seq").astype(jnp.int32)
    y, x, z = seq // (X * Z), lax.rem(seq // Z, X), lax.rem(seq, Z)
    along_z = jnp.stack([lax.rem(z - k + Z, Z) for k in range(Z)])
    places = jnp.stack([lax.rem(y - dy + Y, Y) * X + lax.rem(x - dx + X, X) for dy, dx in STEPS])
    z_groups = [[g * Z + k for k in range(Z)] for g in range(X * Y)]

    flat = lambda array: array[0].reshape(frames, records * features)
    packed = pack_items(flat(queries), flat(key_states), flat(value_states))
    out_rows = [out_weight[0]] + [
        lax.ppermute(out_weight[0], "seq", seq_pairs(0, 0, k)) for k in range(1, Z)
    ]
    out_group = place(along_z, out_rows).reshape(-1, width)
    received = exchange(after(packed, out_group))
    grads = out_grad[0].transpose(1, 0, 2)
    inputs = layer_input[0].transpose(1, 0, 2)
    out_pieces = [out_group] + [across(out_group, *step) for step in STEPS[1:]]
    attn_grad = project(places, grads.reshape(records * frames, width), out_pieces)
    received_grads = exchange(after(attn_grad, received))

    record = seq // HEADS
    valid = jnp.sum(jnp.where(jnp.arange(records) == record, lengths[0], 0)).reshape(1)
    keys, queries_t, keys_t = prepare(valid, received)
    weights_0, sums_0 = softmax_weights(0, keys, queries_t)
    copies = jnp.broadcast_to(qkv_weight, (Z,) + qkv_weight.shape[1:])
    group = exchange(after(copies, received_grads, sums_0), z_groups).reshape(-1, qkv_weight.shape[2])
    weights_1, sums_1 = softmax_weights(1, after(keys, received_grads, sums_0), queries_t)
    rest = (queries_t, keys_t, received, received_grads)
    begun = attention_grads(0, weights_0, after(sums_0, group, sums_1), *rest)
    near = [across(group, *step) for step in NEAR]
    gradients = attention_grads(1, weights_1, after(sums_1, *near), *rest, begun)
    diagonal = [across(after(group, *near), *step) for step in DIAGONAL]
    back = exchange(after(gradients, *diagonal))
    far = [across(after(group, *diagonal), *step) for step in FAR]
    weight = place(places, [group] + near + diagonal + far).reshape(width, 3 * features)
    result = finish(back, weight, inputs, grads, norm_gain)
    count = lax.axis_size("section")
    moved = lax.ppermute(result, "section", [(i, (i - 1) % count) for i in range(count)])
    return moved.transpose(1, 0, 2)[None]


def solution(mesh):
    rows = P("section", "seq", None, None)
    in_specs = (
        rows,
        P("section", None),
        rows,
        rows,
        rows,
        rows,
        P("section", "seq", None),
        P("section", "seq", None),
        P("section", None),
    )
    return jax.shard_map(on_device, mesh=mesh, in_specs=in_specs, out_specs=rows, check_vma=False)
```

time: 433 us -> 349 us (0.81)
  waiting for transfers between devices: 178 us -> 138 us
  Pallas kernels: 128 us -> 89 us
  starting transfers between devices: 106 us -> 83.7 us
  local copies, waits for them, and re-layouts: 19.2 us -> 36.2 us
    ppermute x28 -> x21, waiting for transfers between devices: 166 us -> 113 us  [the longest x14 111 us: across(): return lax.ppermute(rows, 'seq', seq_pairs(dy, dx, 0))]
    pallas_call x1 -> x3, Pallas kernels: 71.5 us -> 49.1 us  [the longest x2 47.4 us: attention_grads(): pl.pallas_call(functools.partial(grads_kernel, part), grid=(blocks,), out...]
    pallas_call x1 -> x2, Pallas kernels: 43.9 us -> 28.9 us  [softmax_weights(): pl.pallas_call(weights_kernel, grid=(blocks,), out_shape=[jax.ShapeDtypeS...]
    unnamed x29 -> x71, local copies, waits for them, and re-layouts: 17.6 us -> 32.3 us
    all_to_all x4, waiting for transfers between devices: 0.01 us -> 12.8 us  [exchange(): lax.all_to_all(items, 'seq', split_axis=0, concat_axis=0, tiled=True, axi...]
    all_to_all x4, starting transfers between devices: 39 us -> 26.7 us  [exchange(): lax.all_to_all(items, 'seq', split_axis=0, concat_axis=0, tiled=True, axi...]
    ppermute x1, starting transfers between devices: 11.9 us -> 3.5 us  [on_device(): lax.ppermute(result, 'section', [(i, (i - 1) % count) for i in range(coun...]
    ppermute x28 -> x21, starting transfers between devices: 55.2 us -> 53.4 us  [the longest x14 36.2 us: across(): return lax.ppermute(rows, 'seq', seq_pairs(dy, dx, 0))]
  transfers between devices with their start and end apart: 33 -> 26, of which waited for: 22 -> 10; matrix products, arithmetic and copies ran while one was open for 1% -> 2% of each run, Pallas kernels for 12% -> 24%
where the time goes in v2:
time: 349 us; the launch traced here: 348 us
  waiting for transfers between devices  138 us (40%)
  Pallas kernels  89 us (26%)
  starting transfers between devices  83.7 us (24%)
  local copies, waits for them, and re-layouts  36.2 us (10%)
    ppermute x14, waiting for transfers between devices, across(): return lax.ppermute(rows, 'seq', seq_pairs(dy, dx, 0))  111 us
    pallas_call x2, Pallas kernels, attention_grads(): pl.pallas_call(functools.partial(grads_kernel, part), grid=(blocks,), out...  47.4 us
    ppermute x14, starting transfers between devices, across(): return lax.ppermute(rows, 'seq', seq_pairs(dy, dx, 0))  36.2 us
    unnamed x71, local copies, waits for them, and re-layouts  32.3 us
    pallas_call x2, Pallas kernels, softmax_weights(): pl.pallas_call(weights_kernel, grid=(blocks,), out_shape=[jax.ShapeDtypeS...  28.9 us
    all_to_all x4, starting transfers between devices, exchange(): lax.all_to_all(items, 'seq', split_axis=0, concat_axis=0, tiled=True, axi...  26.7 us
    ppermute x7, starting transfers between devices, on_device(): lax.ppermute(out_weight[0], 'seq', seq_pairs(0, 0, k))  17.3 us
    all_to_all x4, waiting for transfers between devices, exchange(): lax.all_to_all(items, 'seq', split_axis=0, concat_axis=0, tiled=True, axi...  12.8 us
  transfers between devices with their start and end apart: 26, of which 10 were waited for; matrix products, arithmetic and copies ran while one was open for 2% of the time, Pallas kernels for 24%

profile of v2, /device:TPU:1, one launch (start us, length us, event | category | flops | bytes accessed | tf_op | source)
XLA Modules:
  0.0 347.5 jit_solution(1281752076210101151)
XLA Ops:
  5.5 3.8 %collective-permute-start.2 = (bf16[16,1536]{1,0:T(8,128)(2,1)}, bf16[16,1536]{1,0:T(8,128)(2,1)S(1)}, u32[]{:S(2)}, u32[]{:S(2)}) collective-permute-start(bf16[16,1536]{1,0:T(8,128)(2,1)} %bitcast.73), channel_id=1, source_target_pairs={{0,3},{1,4},{2,5},{3,6},{4,7},{5,0},{6,1},{7,2},{8,11},{9,12},{10,... | collective-permute-start | bytes 147464 | tf_op jit(solution)/shard_map/ppermute | solution.py:387
  9.7 4.5 %collective-permute-start.4 = (bf16[16,1536]{1,0:T(8,128)(2,1)}, bf16[16,1536]{1,0:T(8,128)(2,1)S(1)}, u32[]{:S(2)}, u32[]{:S(2)}) collective-permute-start(bf16[16,1536]{1,0:T(8,128)(2,1)} %bitcast.75), channel_id=1, source_target_pairs={{0,5},{1,6},{2,7},{3,0},{4,1},{5,2},{6,3},{7,4},{8,13},{9,14},{10,... | collective-permute-start | bytes 147464 | tf_op jit(solution)/shard_map/ppermute | solution.py:387
  23.2 8.0 %all-to-all-start = ((bf16[64,96,128]{2,1,0:T(8,128)(2,1)}), bf16[64,96,128]{2,1,0:T(8,128)(2,1)S(1)}, u32[]{:S(2)}, u32[]{:S(2)}) async-start(bf16[64,96,128]{2,1,0:T(8,128)(2,1)} %shard_map.91), calls=%async_computation | async-start | bytes 3145728 | tf_op jit(solution)/shard_map/all_to_all | solution.py:348
  35.0 3.6 %collective-permute-start.11 = (bf16[128,1536]{1,0:T(8,128)(2,1)S(1)}, bf16[128,1536]{1,0:T(8,128)(2,1)}, u32[]{:S(2)}, u32[]{:S(2)}) collective-permute-start(bf16[128,1536]{1,0:T(8,128)(2,1)S(1)} %bitcast.67), channel_id=1, source_target_pairs={{0,56},{1,57},{2,58},{3,59},{4,60},{5,61},{6,62},{7,63},{8,48},{9,... | collective-permute-start | bytes 1179656 | tf_op jit(solution)/shard_map/ppermute | solution.py:356
  38.6 8.8 %collective-permute-done.7.refs_1_ = bf16[128,1536]{1,0:T(8,128)(2,1)S(1)} collective-permute-done((bf16[128,1536]{1,0:T(8,128)(2,1)S(1)}, bf16[128,1536]{1,0:T(8,128)(2,1)S(1)}, u32[]{:S(2)}, u32[]{:S(2)}) %collective-permute-start.7) | collective-permute-done | bytes 393248 | tf_op jit(solution)/shard_map/ppermute | solution.py:356
  50.2 14.8 %collective-permute-start.13 = (bf16[128,1536]{1,0:T(8,128)(2,1)S(1)}, bf16[128,1536]{1,0:T(8,128)(2,1)}, u32[]{:S(2)}, u32[]{:S(2)}) collective-permute-start(bf16[128,1536]{1,0:T(8,128)(2,1)S(1)} %bitcast.69), channel_id=1, source_target_pairs={{0,40},{1,41},{2,42},{3,43},{4,44},{5,45},{6,46},{7,47},{8,32},{9,... | collective-permute-start | bytes 1179656 | tf_op jit(solution)/shard_map/ppermute | solution.py:356
  66.4 9.0 %collective-permute-done.11.refs_5_ = bf16[128,1536]{1,0:T(8,128)(2,1)} collective-permute-done((bf16[128,1536]{1,0:T(8,128)(2,1)S(1)}, bf16[128,1536]{1,0:T(8,128)(2,1)}, u32[]{:S(2)}, u32[]{:S(2)}) %collective-permute-start.11) | collective-permute-done | bytes 393248 | tf_op jit(solution)/shard_map/ppermute | solution.py:356
  76.9 8.9 %collective-permute-done.13.refs_7_ = bf16[128,1536]{1,0:T(8,128)(2,1)} collective-permute-done((bf16[128,1536]{1,0:T(8,128)(2,1)S(1)}, bf16[128,1536]{1,0:T(8,128)(2,1)}, u32[]{:S(2)}, u32[]{:S(2)}) %collective-permute-start.13) | collective-permute-done | bytes 393248 | tf_op jit(solution)/shard_map/ppermute | solution.py:356
  85.8 4.2 %shard_map.94 = bf16[64,32,128]{2,1,0:T(8,128)(2,1)} custom-call(s32[8]{0:T(128)S(1)} %stack.71.owner_ref, bf16[256,1536]{1,0:T(8,128)(2,1)S(1)} %bitcast.49, bf16[128,1536]{1,0:T(8,128)(2,1)S(1)} %bitcast.70, bf16[128,1536]{1,0:T(8,128)(2,1)S(1)} %collective-permute-done.7.refs_1_, bf16[128,1536]{1,0:T(8,128)(2,1)S(1)} %collective-permute-done.8.refs_2_, ...), custom_call_target="tpu_custom_call" | custom-call | flops 805306368 | bytes 4456448 | tf_op jit(solution)/shard_map/pallas_call | solution.py:106
  90.0 7.7 %all-to-all-start.1 = ((bf16[64,32,128]{2,1,0:T(8,128)(2,1)}), bf16[64,32,128]{2,1,0:T(8,128)(2,1)S(1)}, u32[]{:S(2)}, u32[]{:S(2)}) async-start(bf16[64,32,128]{2,1,0:T(8,128)(2,1)} %shard_map.94), calls=%async_computation.1 | async-start | bytes 1048576 | tf_op jit(solution)/shard_map/all_to_all | solution.py:348
  100.0 14.4 %shard_map.95 = (f32[8,4096,256]{2,1,0:T(8,128)}, f32[1,2048]{1,0:T(1,128)S(1)}) custom-call(bf16[4096,128]{1,0:T(8,128)(2,1)S(1)} %get-tuple-element.28.kz_ref, bf16[128,4096]{1,0:T(8,128)(2,1)S(1)} %get-tuple-element.26.qt_ref), custom_call_target="tpu_custom_call" | custom-call | flops 4294967296 | bytes 33554432 | tf_op jit(solution)/shard_map/pallas_call | solution.py:185
  118.7 6.2 %all-to-all-start.2 = ((bf16[8,24,3072]{2,1,0:T(8,128)(2,1)}), bf16[8,24,3072]{2,1,0:T(8,128)(2,1)S(1)}, u32[]{:S(2)}, u32[]{:S(2)}) async-start(bf16[8,24,3072]{2,1,0:T(8,128)(2,1)} %broadcast_in_dim.16), calls=%async_computation.2 | async-start | bytes 2359296 | tf_op jit(solution)/shard_map/all_to_all | solution.py:348
  127.3 14.5 %shard_map.96 = (f32[8,4096,256]{2,1,0:T(8,128)}, f32[1,2048]{1,0:T(1,128)S(1)}) custom-call(bf16[4096,128]{1,0:T(8,128)(2,1)S(1)} %copy-done.24, bf16[128,4096]{1,0:T(8,128)(2,1)S(1)} %copy-done.20), custom_call_target="tpu_custom_call" | custom-call | flops 4294967296 | bytes 33554432 | tf_op jit(solution)/shard_map/pallas_call | solution.py:185
  141.9 12.8 %all-to-all-done.2 = bf16[8,24,3072]{2,1,0:T(8,128)(2,1)S(1)} async-done(((bf16[8,24,3072]{2,1,0:T(8,128)(2,1)}), bf16[8,24,3072]{2,1,0:T(8,128)(2,1)S(1)}, u32[]{:S(2)}, u32[]{:S(2)}) %all-to-all-start.2) | async-done | bytes 1179680 | tf_op jit(solution)/shard_map/all_to_all | solution.py:348
  162.5 23.6 %shard_map.97 = (f32[64,2048]{1,0:T(8,128)S(1)}, f32[4096,128]{1,0:T(8,128)S(1)}) custom-call(f32[8,4096,256]{2,1,0:T(8,128)} %get-tuple-element.34.w_ref, f32[1,2048]{1,0:T(1,128)S(1)} %copy-done.29, bf16[128,4096]{1,0:T(8,128)(2,1)S(1)} %copy-done.21, bf16[64,4096]{1,0:T(8,128)(2,1)S(1)} %copy-done.26, bf16[64,96,128]{2,1,0:T(8,128)(2,1)S(1)} %all-to-all-done.r_ref, ...), custom_call_target="tpu_custom_call" | custom-call | flops 17179869184 | bytes 33554432 | tf_op jit(solution)/shard_map/pallas_call | solution.py:278
  188.3 3.6 %collective-permute-start.18 = (bf16[192,3072]{1,0:T(8,128)(2,1)S(1)}, bf16[192,3072]{1,0:T(8,128)(2,1)S(1)}, u32[]{:S(2)}, u32[]{:S(2)}) collective-permute-start(bf16[192,3072]{1,0:T(8,128)(2,1)S(1)} %bitcast.55), channel_id=1, source_target_pairs={{0,56},{1,57},{2,58},{3,59},{4,60},{5,61},{6,62},{7,63},{8,48},{9,... | collective-permute-start | bytes 3538952 | tf_op jit(solution)/shard_map/ppermute | solution.py:356
  191.9 23.8 %shard_map.98 = bf16[64,96,128]{2,1,0:T(8,128)(2,1)S(1)} custom-call(f32[8,4096,256]{2,1,0:T(8,128)} %get-tuple-element.29.w_ref, f32[1,2048]{1,0:T(1,128)S(1)} %get-tuple-element.32.l_ref, bf16[128,4096]{1,0:T(8,128)(2,1)S(1)} %copy-done.22, bf16[64,4096]{1,0:T(8,128)(2,1)S(1)} %copy-done.27, bf16[64,96,128]{2,1,0:T(8,128)(2,1)S(1)} %all-to-all-done.r_ref, ...), custom_call_target="tpu_custom_call" | custom-call | flops 17179869184 | bytes 33554432 | tf_op jit(solution)/shard_map/pallas_call | solution.py:278
  217.9 20.3 %collective-permute-done.18.refs_5_ = bf16[192,3072]{1,0:T(8,128)(2,1)S(1)} collective-permute-done((bf16[192,3072]{1,0:T(8,128)(2,1)S(1)}, bf16[192,3072]{1,0:T(8,128)(2,1)S(1)}, u32[]{:S(2)}, u32[]{:S(2)}) %collective-permute-start.18) | collective-permute-done | bytes 1179680 | tf_op jit(solution)/shard_map/ppermute | solution.py:356
  239.2 4.8 %all-to-all-start.3 = ((bf16[64,96,128]{2,1,0:T(8,128)(2,1)}), bf16[64,96,128]{2,1,0:T(8,128)(2,1)S(1)}, u32[]{:S(2)}, u32[]{:S(2)}) async-start(bf16[64,96,128]{2,1,0:T(8,128)(2,1)} %copy-done.3), calls=%async_computation.3 | async-start | bytes 3145728 | tf_op jit(solution)/shard_map/all_to_all | solution.py:348
  250.0 62.4 %collective-permute-done.19.refs_6_ = bf16[192,3072]{1,0:T(8,128)(2,1)S(1)} collective-permute-done((bf16[192,3072]{1,0:T(8,128)(2,1)S(1)}, bf16[192,3072]{1,0:T(8,128)(2,1)S(1)}, u32[]{:S(2)}, u32[]{:S(2)}) %collective-permute-start.19) | collective-permute-done | bytes 1179680 | tf_op jit(solution)/shard_map/ppermute | solution.py:356
  318.7 3.7 %copy-done = bf16[8,192,3072]{2,1,0:T(8,128)(2,1)} copy-done((bf16[8,192,3072]{2,1,0:T(8,128)(2,1)}, bf16[8,192,3072]{2,1,0:T(8,128)(2,1)S(1)}, u32[]{:S(2)}) %copy-start) | copy-done | bytes 9437208
  322.3 3.7 %copy-done.1 = bf16[8,192,3072]{2,1,0:T(8,128)(2,1)S(1)} copy-done((bf16[8,192,3072]{2,1,0:T(8,128)(2,1)S(1)}, bf16[8,192,3072]{2,1,0:T(8,128)(2,1)}, u32[]{:S(2)}) %copy-start.1) | copy-done | bytes 9437208
  330.5 3.5 %collective-permute-start.21 = (bf16[4,64,1536]{2,1,0:T(8,128)(2,1)S(1)}, bf16[4,64,1536]{2,1,0:T(8,128)(2,1)S(1)}, u32[]{:S(2)}, u32[]{:S(2)}) collective-permute-start(bf16[4,64,1536]{2,1,0:T(8,128)(2,1)S(1)} %shard_map.100), channel_id=1, source_target_pairs={{0,192},{64,0},{128,64},{192,128},{1,193},{65,1},{129,65},{193,129... | collective-permute-start | bytes 2359304 | tf_op jit(solution)/shard_map/ppermute | solution.py:414
  334.0 12.0 %collective-permute-done.21 = bf16[4,64,1536]{2,1,0:T(8,128)(2,1)S(1)} collective-permute-done((bf16[4,64,1536]{2,1,0:T(8,128)(2,1)S(1)}, bf16[4,64,1536]{2,1,0:T(8,128)(2,1)S(1)}, u32[]{:S(2)}, u32[]{:S(2)}) %collective-permute-start.21) | collective-permute-done | bytes 786464 | tf_op jit(solution)/shard_map/ppermute | solution.py:414
  (114 shorter events, 64.7 us)
Async XLA Ops:
  0.0 14.1 %collective-permute-start = (bf16[16,1536]{1,0:T(8,128)(2,1)}, bf16[16,1536]{1,0:T(8,128)(2,1)S(1)}, u32[]{:S(2)}, u32[]{:S(2)}) collective-permute-start(bf16[16,1536]{1,0:T(8,128)(2,1)} %bitcast.71), channel_id=1, source_target_pairs={{0,1},{1,2},{2,3},{3,4},{4,5},{5,6},{6,7},{7,0},{8,9},{9,10},{10,1... | collective-permute-start | bytes 147464 | tf_op jit(solution)/shard_map/ppermute | solution.py:387
  2.5 14.1 %collective-permute-start.1 = (bf16[16,1536]{1,0:T(8,128)(2,1)}, bf16[16,1536]{1,0:T(8,128)(2,1)S(1)}, u32[]{:S(2)}, u32[]{:S(2)}) collective-permute-start(bf16[16,1536]{1,0:T(8,128)(2,1)} %bitcast.72), channel_id=1, source_target_pairs={{0,2},{1,3},{2,4},{3,5},{4,6},{5,7},{6,0},{7,1},{8,10},{9,11},{10,... | collective-permute-start | bytes 147464 | tf_op jit(solution)/shard_map/ppermute | solution.py:387
  5.5 15.2 %collective-permute-start.2 = (bf16[16,1536]{1,0:T(8,128)(2,1)}, bf16[16,1536]{1,0:T(8,128)(2,1)S(1)}, u32[]{:S(2)}, u32[]{:S(2)}) collective-permute-start(bf16[16,1536]{1,0:T(8,128)(2,1)} %bitcast.73), channel_id=1, source_target_pairs={{0,3},{1,4},{2,5},{3,6},{4,7},{5,0},{6,1},{7,2},{8,11},{9,12},{10,... | collective-permute-start | bytes 147464 | tf_op jit(solution)/shard_map/ppermute | solution.py:387
  9.2 11.5 %collective-permute-start.3 = (bf16[16,1536]{1,0:T(8,128)(2,1)}, bf16[16,1536]{1,0:T(8,128)(2,1)S(1)}, u32[]{:S(2)}, u32[]{:S(2)}) collective-permute-start(bf16[16,1536]{1,0:T(8,128)(2,1)} %bitcast.74), channel_id=1, source_target_pairs={{0,4},{1,5},{2,6},{3,7},{4,0},{5,1},{6,2},{7,3},{8,12},{9,13},{10,... | collective-permute-start | bytes 147464 | tf_op jit(solution)/shard_map/ppermute | solution.py:387
  9.7 11.0 %collective-permute-start.4 = (bf16[16,1536]{1,0:T(8,128)(2,1)}, bf16[16,1536]{1,0:T(8,128)(2,1)S(1)}, u32[]{:S(2)}, u32[]{:S(2)}) collective-permute-start(bf16[16,1536]{1,0:T(8,128)(2,1)} %bitcast.75), channel_id=1, source_target_pairs={{0,5},{1,6},{2,7},{3,0},{4,1},{5,2},{6,3},{7,4},{8,13},{9,14},{10,... | collective-permute-start | bytes 147464 | tf_op jit(solution)/shard_map/ppermute | solution.py:387
  23.2 66.8 %all-to-all-start = ((bf16[64,96,128]{2,1,0:T(8,128)(2,1)}), bf16[64,96,128]{2,1,0:T(8,128)(2,1)S(1)}, u32[]{:S(2)}, u32[]{:S(2)}) async-start(bf16[64,96,128]{2,1,0:T(8,128)(2,1)} %shard_map.91), calls=%async_computation | async-start | bytes 3145728 | tf_op jit(solution)/shard_map/all_to_all | solution.py:348
  31.2 16.1 %collective-permute-start.7 = (bf16[128,1536]{1,0:T(8,128)(2,1)S(1)}, bf16[128,1536]{1,0:T(8,128)(2,1)S(1)}, u32[]{:S(2)}, u32[]{:S(2)}) collective-permute-start(bf16[128,1536]{1,0:T(8,128)(2,1)S(1)} %bitcast.63), channel_id=1, source_target_pairs={{0,8},{1,9},{2,10},{3,11},{4,12},{5,13},{6,14},{7,15},{8,0},{9,1},... | collective-permute-start | bytes 1179656 | tf_op jit(solution)/shard_map/ppermute | solution.py:356
  32.3 17.9 %collective-permute-start.8 = (bf16[128,1536]{1,0:T(8,128)(2,1)S(1)}, bf16[128,1536]{1,0:T(8,128)(2,1)S(1)}, u32[]{:S(2)}, u32[]{:S(2)}) collective-permute-start(bf16[128,1536]{1,0:T(8,128)(2,1)S(1)} %bitcast.64), channel_id=1, source_target_pairs={{0,16},{1,17},{2,18},{3,19},{4,20},{5,21},{6,22},{7,23},{8,24},{9,... | collective-permute-start | bytes 1179656 | tf_op jit(solution)/shard_map/ppermute | solution.py:356
  33.5 32.8 %collective-permute-start.9 = (bf16[128,1536]{1,0:T(8,128)(2,1)S(1)}, bf16[128,1536]{1,0:T(8,128)(2,1)}, u32[]{:S(2)}, u32[]{:S(2)}) collective-permute-start(bf16[128,1536]{1,0:T(8,128)(2,1)S(1)} %bitcast.65), channel_id=1, source_target_pairs={{0,48},{1,49},{2,50},{3,51},{4,52},{5,53},{6,54},{7,55},{8,56},{9,... | collective-permute-start | bytes 1179656 | tf_op jit(solution)/shard_map/ppermute | solution.py:356
  35.0 31.3 %collective-permute-start.10 = (bf16[128,1536]{1,0:T(8,128)(2,1)S(1)}, bf16[128,1536]{1,0:T(8,128)(2,1)}, u32[]{:S(2)}, u32[]{:S(2)}) collective-permute-start(bf16[128,1536]{1,0:T(8,128)(2,1)S(1)} %bitcast.66), channel_id=1, source_target_pairs={{0,24},{1,25},{2,26},{3,27},{4,28},{5,29},{6,30},{7,31},{8,16},{9,... | collective-permute-start | bytes 1179656 | tf_op jit(solution)/shard_map/ppermute | solution.py:356
  35.0 40.4 %collective-permute-start.11 = (bf16[128,1536]{1,0:T(8,128)(2,1)S(1)}, bf16[128,1536]{1,0:T(8,128)(2,1)}, u32[]{:S(2)}, u32[]{:S(2)}) collective-permute-start(bf16[128,1536]{1,0:T(8,128)(2,1)S(1)} %bitcast.67), channel_id=1, source_target_pairs={{0,56},{1,57},{2,58},{3,59},{4,60},{5,61},{6,62},{7,63},{8,48},{9,... | collective-permute-start | bytes 1179656 | tf_op jit(solution)/shard_map/ppermute | solution.py:356
  47.4 29.5 %collective-permute-start.12 = (bf16[128,1536]{1,0:T(8,128)(2,1)S(1)}, bf16[128,1536]{1,0:T(8,128)(2,1)}, u32[]{:S(2)}, u32[]{:S(2)}) collective-permute-start(bf16[128,1536]{1,0:T(8,128)(2,1)S(1)} %bitcast.68), channel_id=1, source_target_pairs={{0,32},{1,33},{2,34},{3,35},{4,36},{5,37},{6,38},{7,39},{8,40},{9,... | collective-permute-start | bytes 1179656 | tf_op jit(solution)/shard_map/ppermute | solution.py:356
  50.2 35.6 %collective-permute-start.13 = (bf16[128,1536]{1,0:T(8,128)(2,1)S(1)}, bf16[128,1536]{1,0:T(8,128)(2,1)}, u32[]{:S(2)}, u32[]{:S(2)}) collective-permute-start(bf16[128,1536]{1,0:T(8,128)(2,1)S(1)} %bitcast.69), channel_id=1, source_target_pairs={{0,40},{1,41},{2,42},{3,43},{4,44},{5,45},{6,46},{7,47},{8,32},{9,... | collective-permute-start | bytes 1179656 | tf_op jit(solution)/shard_map/ppermute | solution.py:356
  90.0 26.5 %all-to-all-start.1 = ((bf16[64,32,128]{2,1,0:T(8,128)(2,1)}), bf16[64,32,128]{2,1,0:T(8,128)(2,1)S(1)}, u32[]{:S(2)}, u32[]{:S(2)}) async-start(bf16[64,32,128]{2,1,0:T(8,128)(2,1)} %shard_map.94), calls=%async_computation.1 | async-start | bytes 1048576 | tf_op jit(solution)/shard_map/all_to_all | solution.py:348
  118.7 36.0 %all-to-all-start.2 = ((bf16[8,24,3072]{2,1,0:T(8,128)(2,1)}), bf16[8,24,3072]{2,1,0:T(8,128)(2,1)S(1)}, u32[]{:S(2)}, u32[]{:S(2)}) async-start(bf16[8,24,3072]{2,1,0:T(8,128)(2,1)} %broadcast_in_dim.16), calls=%async_computation.2 | async-start | bytes 2359296 | tf_op jit(solution)/shard_map/all_to_all | solution.py:348
  154.7 31.5 %collective-permute-start.14 = (bf16[192,3072]{1,0:T(8,128)(2,1)S(1)}, bf16[192,3072]{1,0:T(8,128)(2,1)S(1)}, u32[]{:S(2)}, u32[]{:S(2)}) collective-permute-start(bf16[192,3072]{1,0:T(8,128)(2,1)S(1)} %bitcast.51), channel_id=1, source_target_pairs={{0,8},{1,9},{2,10},{3,11},{4,12},{5,13},{6,14},{7,15},{8,0},{9,1},... | collective-permute-start | bytes 3538952 | tf_op jit(solution)/shard_map/ppermute | solution.py:356
  155.8 31.4 %collective-permute-start.15 = (bf16[192,3072]{1,0:T(8,128)(2,1)S(1)}, bf16[192,3072]{1,0:T(8,128)(2,1)S(1)}, u32[]{:S(2)}, u32[]{:S(2)}) collective-permute-start(bf16[192,3072]{1,0:T(8,128)(2,1)S(1)} %bitcast.52), channel_id=1, source_target_pairs={{0,16},{1,17},{2,18},{3,19},{4,20},{5,21},{6,22},{7,23},{8,24},{9,... | collective-permute-start | bytes 3538952 | tf_op jit(solution)/shard_map/ppermute | solution.py:356
  157.1 31.2 %collective-permute-start.16 = (bf16[192,3072]{1,0:T(8,128)(2,1)S(1)}, bf16[192,3072]{1,0:T(8,128)(2,1)S(1)}, u32[]{:S(2)}, u32[]{:S(2)}) collective-permute-start(bf16[192,3072]{1,0:T(8,128)(2,1)S(1)} %bitcast.53), channel_id=1, source_target_pairs={{0,48},{1,49},{2,50},{3,51},{4,52},{5,53},{6,54},{7,55},{8,56},{9,... | collective-permute-start | bytes 3538952 | tf_op jit(solution)/shard_map/ppermute | solution.py:356
  188.3 28.6 %collective-permute-start.17 = (bf16[192,3072]{1,0:T(8,128)(2,1)S(1)}, bf16[192,3072]{1,0:T(8,128)(2,1)S(1)}, u32[]{:S(2)}, u32[]{:S(2)}) collective-permute-start(bf16[192,3072]{1,0:T(8,128)(2,1)S(1)} %bitcast.54), channel_id=1, source_target_pairs={{0,24},{1,25},{2,26},{3,27},{4,28},{5,29},{6,30},{7,31},{8,16},{9,... | collective-permute-start | bytes 3538952 | tf_op jit(solution)/shard_map/ppermute | solution.py:356
  188.3 49.9 %collective-permute-start.18 = (bf16[192,3072]{1,0:T(8,128)(2,1)S(1)}, bf16[192,3072]{1,0:T(8,128)(2,1)S(1)}, u32[]{:S(2)}, u32[]{:S(2)}) collective-permute-start(bf16[192,3072]{1,0:T(8,128)(2,1)S(1)} %bitcast.55), channel_id=1, source_target_pairs={{0,56},{1,57},{2,58},{3,59},{4,60},{5,61},{6,62},{7,63},{8,48},{9,... | collective-permute-start | bytes 3538952 | tf_op jit(solution)/shard_map/ppermute | solution.py:356
  239.2 83.1 %all-to-all-start.3 = ((bf16[64,96,128]{2,1,0:T(8,128)(2,1)}), bf16[64,96,128]{2,1,0:T(8,128)(2,1)S(1)}, u32[]{:S(2)}, u32[]{:S(2)}) async-start(bf16[64,96,128]{2,1,0:T(8,128)(2,1)} %copy-done.3), calls=%async_computation.3 | async-start | bytes 3145728 | tf_op jit(solution)/shard_map/all_to_all | solution.py:348
  244.1 68.3 %collective-permute-start.19 = (bf16[192,3072]{1,0:T(8,128)(2,1)S(1)}, bf16[192,3072]{1,0:T(8,128)(2,1)S(1)}, u32[]{:S(2)}, u32[]{:S(2)}) collective-permute-start(bf16[192,3072]{1,0:T(8,128)(2,1)S(1)} %bitcast.56), channel_id=1, source_target_pairs={{0,32},{1,33},{2,34},{3,35},{4,36},{5,37},{6,38},{7,39},{8,40},{9,... | collective-permute-start | bytes 3538952 | tf_op jit(solution)/shard_map/ppermute | solution.py:356
  246.8 65.6 %collective-permute-start.20 = (bf16[192,3072]{1,0:T(8,128)(2,1)S(1)}, bf16[192,3072]{1,0:T(8,128)(2,1)S(1)}, u32[]{:S(2)}, u32[]{:S(2)}) collective-permute-start(bf16[192,3072]{1,0:T(8,128)(2,1)S(1)} %bitcast.57), channel_id=1, source_target_pairs={{0,40},{1,41},{2,42},{3,43},{4,44},{5,45},{6,46},{7,47},{8,32},{9,... | collective-permute-start | bytes 3538952 | tf_op jit(solution)/shard_map/ppermute | solution.py:356
  330.5 15.5 %collective-permute-start.21 = (bf16[4,64,1536]{2,1,0:T(8,128)(2,1)S(1)}, bf16[4,64,1536]{2,1,0:T(8,128)(2,1)S(1)}, u32[]{:S(2)}, u32[]{:S(2)}) collective-permute-start(bf16[4,64,1536]{2,1,0:T(8,128)(2,1)S(1)} %shard_map.100), channel_id=1, source_target_pairs={{0,192},{64,0},{128,64},{192,128},{1,193},{65,1},{129,65},{193,129... | collective-permute-start | bytes 2359304 | tf_op jit(solution)/shard_map/ppermute | solution.py:414
  (35 other events, 371.4 us)

commit v3 on v2

--- a/solution.py
+++ b/solution.py
@@ -16,6 +16,7 @@
 PLAIN_DOT = (((1,), (0,)), ((), ()))
 MIB = 1024 * 1024
 QB = 256
+UNIT = 96
 KB = 256
 UNROLL1 = True
 UNROLL2 = True
@@ -66,25 +67,6 @@
         compiler_params=pltpu.CompilerParams(vmem_limit_bytes=16 * MIB),
         cost_estimate=cost(0, 3 * MIB),
     )(q, k, v)
-
-
-def place_kernel(owner_ref, *refs):
-    out_ref = refs[-1]
-    for n, ref in enumerate(refs[:-1]):
-        out_ref[owner_ref[n]] = ref[...]
-
-
-def place(owners, pieces):
-    out = jax.ShapeDtypeStruct((len(pieces),) + pieces[0].shape, BF16)
-    size = 2 * len(pieces) * pieces[0].size
-    return pl.pallas_call(
-        place_kernel,
-        out_shape=out,
-        in_specs=[pl.BlockSpec(memory_space=pltpu.SMEM)] + [WHOLE] * len(pieces),
-        out_specs=WHOLE,
-        compiler_params=pltpu.CompilerParams(vmem_limit_bytes=2 * size + 4 * MIB),
-        cost_estimate=cost(0, 2 * size),
-    )(owners, *pieces)
 
 
 def project_kernel(owner_ref, grad_ref, *refs):
@@ -156,7 +138,7 @@
     )(valid, received)
 
 
-def weights_kernel(kz_ref, qt_ref, w_ref, l_ref, s_ref):
+def weights_kernel(gate_ref, kz_ref, qt_ref, w_ref, l_ref, s_ref):
     length = kz_ref.shape[0]
     queries = qt_ref[...]
 
@@ -179,9 +161,10 @@
     l_ref[...] = jnp.sum(total, axis=0, keepdims=True)
 
 
-def softmax_weights(part, keys, queries_t):
+def softmax_weights(part, gate, keys, queries_t):
     length = keys.shape[0]
     blocks = length // QB // 2
+    fixed = lambda shape: pl.BlockSpec(shape, lambda i: (0,) * len(shape))
     return pl.pallas_call(
         weights_kernel,
         grid=(blocks,),
@@ -189,7 +172,11 @@
             jax.ShapeDtypeStruct((blocks, length, QB), F32),
             jax.ShapeDtypeStruct((1, length // 2), F32),
         ],
-        in_specs=[WHOLE, pl.BlockSpec((128, QB), lambda i: (0, part * blocks + i))],
+        in_specs=[
+            pl.BlockSpec(memory_space=pltpu.SMEM),
+            fixed(keys.shape),
+            pl.BlockSpec((128, QB), lambda i: (0, part * blocks + i)),
+        ],
         out_specs=[
             pl.BlockSpec((1, length, QB), lambda i: (i, 0, 0)),
             pl.BlockSpec((1, QB), lambda i: (0, i)),
@@ -197,7 +184,7 @@
         scratch_shapes=[pltpu.VMEM((length, QB), F32)],
         compiler_params=pltpu.CompilerParams(vmem_limit_bytes=24 * MIB),
         cost_estimate=cost(4 * length * length * HS, 2 * length * length, length * length // 2),
-    )(keys, queries_t)
+    )(gate, keys, queries_t)
 
 
 def grads_kernel(part, w_ref, l_ref, qt_ref, kt_ref, r_ref, g_ref, *refs):
@@ -270,11 +257,10 @@
     scratch = [pltpu.VMEM((HS, length // 2), BF16), pltpu.VMEM((length, QB), F32)]
     if part == 0:
         out_shape = [dq, acc]
-        out_specs = [WHOLE, WHOLE]
     else:
         out_shape = jax.ShapeDtypeStruct((sources, 96, 128), BF16)
-        out_specs = WHOLE
         scratch += [pltpu.VMEM((length, 128), F32), pltpu.VMEM((HS, length // 2), F32)]
+    fixed = lambda array: pl.BlockSpec(array.shape, lambda i: (0,) * len(array.shape))
     return pl.pallas_call(
         functools.partial(grads_kernel, part),
         grid=(blocks,),
@@ -284,15 +270,21 @@
             pl.BlockSpec((1, QB), lambda i: (0, i)),
             pl.BlockSpec((128, QB), lambda i: (0, part * blocks + i)),
         ]
-        + [WHOLE] * (3 + len(begun)),
-        out_specs=out_specs,
+        + [fixed(array) for array in (keys_t, received, received_grads, *begun)],
+        out_specs=jax.tree.map(fixed, out_shape),
         scratch_shapes=scratch,
-        compiler_params=pltpu.CompilerParams(vmem_limit_bytes=40 * MIB),
+        compiler_params=pltpu.CompilerParams(vmem_limit_bytes=44 * MIB),
         cost_estimate=cost(16 * length * length * HS, 2 * length * length),
     )(weights, sums, queries_t, keys_t, received, received_grads, *begun)
 
 
-def finish_kernel(back_ref, w_ref, x_ref, g_ref, gain_ref, out_ref, j_ref, n_ref):
+def finish_kernel(start_ref, back_ref, x_ref, g_ref, gain_ref, *refs):
+    pieces, (out_ref, j_ref, n_ref, w_ref, sems) = refs[:-5], refs[-5:]
+    copies = []
+    for n, piece in enumerate(pieces):
+        to = pl.ds(pl.multiple_of(start_ref[n] * UNIT, UNIT), piece.shape[0])
+        copies.append(pltpu.make_async_copy(piece, w_ref.at[to, :], sems.at[n]))
+        copies[-1].start()
     records = x_ref.shape[0]
     frames = x_ref.shape[1]
     width = x_ref.shape[2]
@@ -308,6 +300,8 @@
             span = slice(r * frames, (r + 1) * frames)
             j_ref[span, features + pair * 128 : features + (pair + 1) * 128] = keys
             j_ref[span, 2 * features + pair * 128 : 2 * features + (pair + 1) * 128] = values
+    for copy in copies:
+        copy.wait()
     step = 256
     for n in range(width // step):
         n_ref[:, n * step : (n + 1) * step] = lax.dot_general(
@@ -328,20 +322,24 @@
         out_ref[r] = (g_ref[r].astype(F32) + residual).astype(BF16)
 
 
-def finish(back, weight, inputs, grads, gain):
+def finish(starts, pieces, back, inputs, grads, gain):
     records, frames, width = inputs.shape
+    anywhere = pl.BlockSpec(memory_space=pltpu.HBM)
+    depth = pieces[0].shape[1]
     return pl.pallas_call(
         finish_kernel,
         out_shape=jax.ShapeDtypeStruct(inputs.shape, BF16),
-        in_specs=[WHOLE] * 5,
+        in_specs=[pl.BlockSpec(memory_space=pltpu.SMEM)] + [WHOLE] * 4 + [anywhere] * len(pieces),
         out_specs=WHOLE,
         scratch_shapes=[
-            pltpu.VMEM((records * frames, 3 * HEADS * HS), BF16),
+            pltpu.VMEM((records * frames, depth), BF16),
             pltpu.VMEM((records * frames, width), F32),
+            pltpu.VMEM((width, depth), BF16),
+            pltpu.SemaphoreType.DMA((len(pieces),)),
         ],
-        compiler_params=pltpu.CompilerParams(vmem_limit_bytes=40 * MIB),
-        cost_estimate=cost(2 * records * frames * width * 3072, 2 * 3072 * width),
-    )(back, weight, inputs, grads, gain)
+        compiler_params=pltpu.CompilerParams(vmem_limit_bytes=32 * MIB),
+        cost_estimate=cost(2 * records * frames * width * depth, 2 * depth * width),
+    )(starts, back, inputs, grads, gain, *pieces)
 
 
 def exchange(items, groups=None):
@@ -356,10 +354,16 @@
     return lax.ppermute(rows, "seq", seq_pairs(dy, dx, 0))
 
 
-NEAR = ((0, 1), (1, 0), (3, 0))
-DIAGONAL = ((1, 1), (3, 1))
-FAR = ((2, 0), (2, 1))
-STEPS = ((0, 0),) + NEAR + DIAGONAL + FAR
+STEPS = ((0, 0), (0, 1), (1, 0), (3, 0), (1, 1), (3, 1), (2, 0), (2, 1))
+
+
+def nearby(group):
+    return [across(group, *step) for step in STEPS[1:4]]
+
+
+def further(near):
+    partner, below, _ = near
+    return [across(partner, 1, 0), across(partner, 3, 0), across(below, 1, 0)]
 
 
 def on_device(
@@ -376,40 +380,44 @@
     frames, records, features = queries.shape[1:]
     width = out_grad.shape[3]
     seq = lax.axis_index("seq").astype(jnp.int32)
-    y, x, z = seq // (X * Z), lax.rem(seq // Z, X), lax.rem(seq, Z)
-    along_z = jnp.stack([lax.rem(z - k + Z, Z) for k in range(Z)])
+    y, x = seq // (X * Z), lax.rem(seq // Z, X)
     places = jnp.stack([lax.rem(y - dy + Y, Y) * X + lax.rem(x - dx + X, X) for dy, dx in STEPS])
     z_groups = [[g * Z + k for k in range(Z)] for g in range(X * Y)]
 
+    copies = jnp.broadcast_to(out_weight, (Z,) + out_weight.shape[1:])
+    out_group = exchange(copies, z_groups).reshape(-1, width)
     flat = lambda array: array[0].reshape(frames, records * features)
     packed = pack_items(flat(queries), flat(key_states), flat(value_states))
-    out_rows = [out_weight[0]] + [
-        lax.ppermute(out_weight[0], "seq", seq_pairs(0, 0, k)) for k in range(1, Z)
-    ]
-    out_group = place(along_z, out_rows).reshape(-1, width)
     received = exchange(after(packed, out_group))
     grads = out_grad[0].transpose(1, 0, 2)
     inputs = layer_input[0].transpose(1, 0, 2)
-    out_pieces = [out_group] + [across(out_group, *step) for step in STEPS[1:]]
+    near = nearby(out_group)
+    far = further(near)
+    out_pieces = [out_group] + near + far + [across(far[2], 0, 1)]
     attn_grad = project(places, grads.reshape(records * frames, width), out_pieces)
     received_grads = exchange(after(attn_grad, received))
 
     record = seq // HEADS
     valid = jnp.sum(jnp.where(jnp.arange(records) == record, lengths[0], 0)).reshape(1)
     keys, queries_t, keys_t = prepare(valid, received)
-    weights_0, sums_0 = softmax_weights(0, keys, queries_t)
+    weights_0, sums_0 = softmax_weights(0, valid, keys, queries_t)
     copies = jnp.broadcast_to(qkv_weight, (Z,) + qkv_weight.shape[1:])
-    group = exchange(after(copies, received_grads, sums_0), z_groups).reshape(-1, qkv_weight.shape[2])
-    weights_1, sums_1 = softmax_weights(1, after(keys, received_grads, sums_0), queries_t)
+    qkv_group = exchange(after(copies, received_grads, sums_0), z_groups).reshape(-1, qkv_weight.shape[2])
+    weights_1, sums_1 = softmax_weights(1, after(valid, received_grads, sums_0), keys, queries_t)
     rest = (queries_t, keys_t, received, received_grads)
-    begun = attention_grads(0, weights_0, after(sums_0, group, sums_1), *rest)
-    near = [across(group, *step) for step in NEAR]
-    gradients = attention_grads(1, weights_1, after(sums_1, *near), *rest, begun)
-    diagonal = [across(after(group, *near), *step) for step in DIAGONAL]
-    back = exchange(after(gradients, *diagonal))
-    far = [across(after(group, *diagonal), *step) for step in FAR]
-    weight = place(places, [group] + near + diagonal + far).reshape(width, 3 * features)
-    result = finish(back, weight, inputs, grads, norm_gain)
+    begun = attention_grads(0, weights_0, after(sums_0, qkv_group, sums_1), *rest)
+    near = nearby(qkv_group)
+    sums_1, *near = lax.optimization_barrier((sums_1, *near))
+    gradients = attention_grads(1, weights_1, sums_1, *rest, begun)
+    partner, below, above = near
+    diagonal = [across(partner, 1, 0), across(partner, 3, 0)]
+    gradients, *diagonal = lax.optimization_barrier((gradients, *diagonal))
+    back = exchange(gradients)
+    far = []
+    for down, up in ((below, above), tuple(diagonal)):
+        far += [across(down[:UNIT], 1, 0), across(up[UNIT:], 3, 0)]
+    starts = jnp.concatenate([2 * places[:6], jnp.stack([2 * places[6], 2 * places[6] + 1, 2 * places[7], 2 * places[7] + 1])])
+    result = finish(starts, [qkv_group] + near + diagonal + far, back, inputs, grads, norm_gain)
     count = lax.axis_size("section")
     moved = lax.ppermute(result, "section", [(i, (i - 1) % count) for i in range(count)])
     return moved.transpose(1, 0, 2)[None]

time: 349 us -> 288 us (0.83)
  waiting for transfers between devices: 138 us -> 102 us
  starting transfers between devices: 83.7 us -> 58.4 us
  Pallas kernels: 89 us -> 92.9 us
    ppermute x14 -> x16, waiting for transfers between devices: 111 us -> 65.9 us  [across(): return lax.ppermute(rows, 'seq', seq_pairs(dy, dx, 0))]
    ppermute x7 -> x0, starting transfers between devices: 17.3 us -> none  [on_device(): lax.ppermute(out_weight[0], 'seq', seq_pairs(0, 0, k))]
    ppermute x14 -> x16, starting transfers between devices: 36.2 us -> 20 us  [across(): return lax.ppermute(rows, 'seq', seq_pairs(dy, dx, 0))]
    all_to_all x4 -> x5, waiting for transfers between devices: 12.8 us -> 24.1 us  [exchange(): lax.all_to_all(items, 'seq', split_axis=0, concat_axis=0, tiled=True, axi...]
    unnamed x71 -> x59, local copies, waits for them, and re-layouts: 32.3 us -> 21.7 us
    all_to_all x4 -> x5, starting transfers between devices: 26.7 us -> 36 us  [exchange(): lax.all_to_all(items, 'seq', split_axis=0, concat_axis=0, tiled=True, axi...]
    slice x0 -> x4, local copies, waits for them, and re-layouts: none -> 6.78 us  [on_device(): far += [across(down[:UNIT], 1, 0), across(up[UNIT:], 3, 0)]]
    pallas_call x1, Pallas kernels: 3.37 us -> 7.39 us  [finish(): pl.pallas_call(finish_kernel, out_shape=jax.ShapeDtypeStruct(inputs.shape...]
  transfers between devices with their start and end apart: 26 -> 22, of which waited for: 10 -> 10; matrix products, arithmetic and copies ran while one was open for 2% -> 4% of each run, Pallas kernels for 24% -> 30%
where the time goes in v3:
time: 288 us; the launch traced here: 287 us
  waiting for transfers between devices  102 us (35%)
  Pallas kernels  92.9 us (32%)
  starting transfers between devices  58.4 us (20%)
  local copies, waits for them, and re-layouts  33.1 us (11%)
    ppermute x16, waiting for transfers between devices, across(): return lax.ppermute(rows, 'seq', seq_pairs(dy, dx, 0))  65.9 us
    pallas_call x2, Pallas kernels, attention_grads(): pl.pallas_call(functools.partial(grads_kernel, part), grid=(blocks,), out...  47.8 us
    all_to_all x5, starting transfers between devices, exchange(): lax.all_to_all(items, 'seq', split_axis=0, concat_axis=0, tiled=True, axi...  36 us
    pallas_call x2, Pallas kernels, softmax_weights(): pl.pallas_call(weights_kernel, grid=(blocks,), out_shape=[jax.ShapeDtypeS...  30.3 us
    all_to_all x5, waiting for transfers between devices, exchange(): lax.all_to_all(items, 'seq', split_axis=0, concat_axis=0, tiled=True, axi...  24.1 us
    unnamed x59, local copies, waits for them, and re-layouts  21.7 us
    ppermute x16, starting transfers between devices, across(): return lax.ppermute(rows, 'seq', seq_pairs(dy, dx, 0))  20 us
    ppermute x1, waiting for transfers between devices, on_device(): lax.ppermute(result, 'section', [(i, (i - 1) % count) for i in range(coun...  12 us
  transfers between devices with their start and end apart: 22, of which 10 were waited for; matrix products, arithmetic and copies ran while one was open for 4% of the time, Pallas kernels for 30%

profile of v3, /device:TPU:1, one launch (start us, length us, event | category | flops | bytes accessed | tf_op | source)
XLA Modules:
  0.0 287.3 jit_solution(9016836633838526833)
XLA Ops:
  1.7 9.0 %all-to-all-start = ((bf16[8,16,1536]{2,1,0:T(8,128)(2,1)}), bf16[8,16,1536]{2,1,0:T(8,128)(2,1)S(1)}, u32[]{:S(2)}, u32[]{:S(2)}) async-start(bf16[8,16,1536]{2,1,0:T(8,128)(2,1)} %broadcast_in_dim.23), calls=%async_computation | async-start | bytes 786432 | tf_op jit(solution)/shard_map/all_to_all | solution.py:346
  12.9 12.0 %all-to-all-done = bf16[8,16,1536]{2,1,0:T(8,128)(2,1)S(1)} async-done(((bf16[8,16,1536]{2,1,0:T(8,128)(2,1)}), bf16[8,16,1536]{2,1,0:T(8,128)(2,1)S(1)}, u32[]{:S(2)}, u32[]{:S(2)}) %all-to-all-start) | async-done | bytes 393248 | tf_op jit(solution)/shard_map/all_to_all | solution.py:346
  24.9 6.1 %all-to-all-start.1 = ((bf16[64,96,128]{2,1,0:T(8,128)(2,1)}), bf16[64,96,128]{2,1,0:T(8,128)(2,1)S(1)}, u32[]{:S(2)}, u32[]{:S(2)}) async-start(bf16[64,96,128]{2,1,0:T(8,128)(2,1)} %shard_map.92), calls=%async_computation.1 | async-start | bytes 3145728 | tf_op jit(solution)/shard_map/all_to_all | solution.py:346
  33.4 14.5 %collective-permute-done.1.refs_2_ = bf16[128,1536]{1,0:T(8,128)(2,1)S(1)} collective-permute-done((bf16[128,1536]{1,0:T(8,128)(2,1)S(1)}, bf16[128,1536]{1,0:T(8,128)(2,1)S(1)}, u32[]{:S(2)}, u32[]{:S(2)}) %collective-permute-start.1) | collective-permute-done | bytes 393248 | tf_op jit(solution)/shard_map/ppermute | solution.py:354
  47.9 2.7 collective-permute-start.2
  50.6 2.7 collective-permute-start.4
  53.2 11.7 %collective-permute-done.5.refs_6_ = bf16[128,1536]{1,0:T(8,128)(2,1)} collective-permute-done((bf16[128,1536]{1,0:T(8,128)(2,1)S(1)}, bf16[128,1536]{1,0:T(8,128)(2,1)}, u32[]{:S(2)}, u32[]{:S(2)}) %collective-permute-start.5) | collective-permute-done | bytes 393248 | tf_op jit(solution)/shard_map/ppermute | solution.py:354
  67.7 9.0 %collective-permute-done.3.refs_4_ = bf16[128,1536]{1,0:T(8,128)(2,1)} collective-permute-done((bf16[128,1536]{1,0:T(8,128)(2,1)S(1)}, bf16[128,1536]{1,0:T(8,128)(2,1)}, u32[]{:S(2)}, u32[]{:S(2)}) %collective-permute-start.3) | collective-permute-done | bytes 393248 | tf_op jit(solution)/shard_map/ppermute | solution.py:354
  76.7 4.1 %shard_map.91 = bf16[64,32,128]{2,1,0:T(8,128)(2,1)} custom-call(s32[8]{0:T(128)S(1)} %stack.54.owner_ref, bf16[256,1536]{1,0:T(8,128)(2,1)S(1)} %bitcast.43, bf16[128,1536]{1,0:T(8,128)(2,1)S(1)} %bitcast.56, bf16[128,1536]{1,0:T(8,128)(2,1)S(1)} %collective-permute-done.refs_1_, bf16[128,1536]{1,0:T(8,128)(2,1)S(1)} %collective-permute-done.1.refs_2_, ...), custom_call_target="tpu_custom_call" | custom-call | flops 805306368 | bytes 4456448 | tf_op jit(solution)/shard_map/pallas_call | solution.py:88
  80.9 10.1 %all-to-all-start.2 = ((bf16[64,32,128]{2,1,0:T(8,128)(2,1)}), bf16[64,32,128]{2,1,0:T(8,128)(2,1)S(1)}, u32[]{:S(2)}, u32[]{:S(2)}) async-start(bf16[64,32,128]{2,1,0:T(8,128)(2,1)} %shard_map.91), calls=%async_computation.2 | async-start | bytes 1048576 | tf_op jit(solution)/shard_map/all_to_all | solution.py:346
  94.2 15.2 %shard_map.94 = (f32[8,4096,256]{2,1,0:T(8,128)}, f32[1,2048]{1,0:T(1,128)S(1)}) custom-call(s32[1]{0:T(128)} %bitcast.11.length_ref.gate_ref, bf16[4096,128]{1,0:T(8,128)(2,1)S(1)} %get-tuple-element.28.kz_ref, bf16[128,4096]{1,0:T(8,128)(2,1)S(1)} %get-tuple-element.29.qt_ref), custom_call_target="tpu_custom_call" | custom-call | flops 4294967296 | bytes 33554432 | tf_op jit(solution)/shard_map/pallas_call | solution.py:168
  112.6 6.0 %all-to-all-start.3 = ((bf16[8,24,3072]{2,1,0:T(8,128)(2,1)}), bf16[8,24,3072]{2,1,0:T(8,128)(2,1)S(1)}, u32[]{:S(2)}, u32[]{:S(2)}) async-start(bf16[8,24,3072]{2,1,0:T(8,128)(2,1)} %broadcast_in_dim.25), calls=%async_computation.3 | async-start | bytes 2359296 | tf_op jit(solution)/shard_map/all_to_all | solution.py:346
  121.1 15.0 %shard_map.95 = (f32[8,4096,256]{2,1,0:T(8,128)}, f32[1,2048]{1,0:T(1,128)S(1)}) custom-call(s32[1]{0:T(128)} %bitcast.11.length_ref.gate_ref, bf16[4096,128]{1,0:T(8,128)(2,1)S(1)} %copy-done.18, bf16[128,4096]{1,0:T(8,128)(2,1)S(1)} %copy-done.14), custom_call_target="tpu_custom_call" | custom-call | flops 4294967296 | bytes 33554432 | tf_op jit(solution)/shard_map/pallas_call | solution.py:168
  136.1 12.1 %all-to-all-done.3 = bf16[8,24,3072]{2,1,0:T(8,128)(2,1)S(1)} async-done(((bf16[8,24,3072]{2,1,0:T(8,128)(2,1)}), bf16[8,24,3072]{2,1,0:T(8,128)(2,1)S(1)}, u32[]{:S(2)}, u32[]{:S(2)}) %all-to-all-start.3) | async-done | bytes 1179680 | tf_op jit(solution)/shard_map/all_to_all | solution.py:346
  155.4 23.9 %shard_map.96 = (f32[64,2048]{1,0:T(8,128)S(1)}, f32[4096,128]{1,0:T(8,128)S(1)}) custom-call(f32[8,4096,256]{2,1,0:T(8,128)} %get-tuple-element.37.w_ref, f32[1,2048]{1,0:T(1,128)S(1)} %get-tuple-element.38.l_ref, bf16[128,4096]{1,0:T(8,128)(2,1)S(1)} %copy-done.15, bf16[64,4096]{1,0:T(8,128)(2,1)S(1)} %copy-done.20, ...), custom_call_target="tpu_custom_call" | custom-call | flops 17179869184 | bytes 33554432 | tf_op jit(solution)/shard_map/pallas_call | solution.py:264
  184.1 23.9 %shard_map.97 = bf16[64,96,128]{2,1,0:T(8,128)(2,1)S(1)} custom-call(f32[8,4096,256]{2,1,0:T(8,128)} %get-tuple-element.32.w_ref, f32[1,2048]{1,0:T(1,128)S(1)} %get-tuple-element.35.l_ref, bf16[128,4096]{1,0:T(8,128)(2,1)S(1)} %copy-done.16, bf16[64,4096]{1,0:T(8,128)(2,1)S(1)} %copy-done.21, bf16[64,96,128]{2,1,0:T(8,128)(2,1)S(1)} %all-to-all-done.1.r_ref, ...), custom_call_target="tpu_custom_call" | custom-call | flops 17179869184 | bytes 33554432 | tf_op jit(solution)/shard_map/pallas_call | solution.py:264
  209.2 4.7 %all-to-all-start.4 = ((bf16[64,96,128]{2,1,0:T(8,128)(2,1)}), bf16[64,96,128]{2,1,0:T(8,128)(2,1)S(1)}, u32[]{:S(2)}, u32[]{:S(2)}) async-start(bf16[64,96,128]{2,1,0:T(8,128)(2,1)} %copy-done.6), calls=%async_computation.4 | async-start | bytes 3145728 | tf_op jit(solution)/shard_map/all_to_all | solution.py:346
  223.3 2.7 collective-permute-start.15
  228.3 9.6 %collective-permute-done.12.refs_6_ = bf16[96,3072]{1,0:T(8,128)(2,1)} collective-permute-done((bf16[96,3072]{1,0:T(8,128)(2,1)}, bf16[96,3072]{1,0:T(8,128)(2,1)}, u32[]{:S(2)}, u32[]{:S(2)}) %collective-permute-start.12) | collective-permute-done | bytes 589856 | tf_op jit(solution)/shard_map/ppermute | solution.py:354
  237.9 4.2 %collective-permute-done.13.refs_7_ = bf16[96,3072]{1,0:T(8,128)(2,1)} collective-permute-done((bf16[96,3072]{1,0:T(8,128)(2,1)}, bf16[96,3072]{1,0:T(8,128)(2,1)}, u32[]{:S(2)}, u32[]{:S(2)}) %collective-permute-start.13) | collective-permute-done | bytes 589856 | tf_op jit(solution)/shard_map/ppermute | solution.py:354
  242.1 16.4 %collective-permute-done.14.refs_8_ = bf16[96,3072]{1,0:T(8,128)(2,1)} collective-permute-done((bf16[96,3072]{1,0:T(8,128)(2,1)}, bf16[96,3072]{1,0:T(8,128)(2,1)}, u32[]{:S(2)}, u32[]{:S(2)}) %collective-permute-start.14) | collective-permute-done | bytes 589856 | tf_op jit(solution)/shard_map/ppermute | solution.py:354
  264.0 7.4 %shard_map.98 = bf16[4,64,1536]{2,1,0:T(8,128)(2,1)S(1)} custom-call(s32[10]{0:T(128)S(1)} %concatenate.4.start_ref, bf16[64,96,128]{2,1,0:T(8,128)(2,1)S(1)} %all-to-all-done.4.back_ref, bf16[4,64,1536]{2,1,0:T(8,128)(2,1)S(1)} %bitcast.49, bf16[4,64,1536]{2,1,0:T(8,128)(2,1)S(1)} %bitcast.44, f32[1,1536]{1,0:T(1,128)S(1)} %copy-done.12, ...), custom_call_target="tpu_custom_call" | custom-call | flops 2415919104 | bytes 9437184 | tf_op jit(solution)/shard_map/pallas_call | solution.py:329
  271.4 2.4 collective-permute-start.16
  273.8 12.0 %collective-permute-done.16 = bf16[4,64,1536]{2,1,0:T(8,128)(2,1)S(1)} collective-permute-done((bf16[4,64,1536]{2,1,0:T(8,128)(2,1)S(1)}, bf16[4,64,1536]{2,1,0:T(8,128)(2,1)S(1)}, u32[]{:S(2)}, u32[]{:S(2)}) %collective-permute-start.16) | collective-permute-done | bytes 786464 | tf_op jit(solution)/shard_map/ppermute | solution.py:422
  (99 shorter events, 49.6 us)
Async XLA Ops:
  1.7 23.2 %all-to-all-start = ((bf16[8,16,1536]{2,1,0:T(8,128)(2,1)}), bf16[8,16,1536]{2,1,0:T(8,128)(2,1)S(1)}, u32[]{:S(2)}, u32[]{:S(2)}) async-start(bf16[8,16,1536]{2,1,0:T(8,128)(2,1)} %broadcast_in_dim.23), calls=%async_computation | async-start | bytes 786432 | tf_op jit(solution)/shard_map/all_to_all | solution.py:346
  24.9 56.0 %all-to-all-start.1 = ((bf16[64,96,128]{2,1,0:T(8,128)(2,1)}), bf16[64,96,128]{2,1,0:T(8,128)(2,1)S(1)}, u32[]{:S(2)}, u32[]{:S(2)}) async-start(bf16[64,96,128]{2,1,0:T(8,128)(2,1)} %shard_map.92), calls=%async_computation.1 | async-start | bytes 3145728 | tf_op jit(solution)/shard_map/all_to_all | solution.py:346
  31.0 16.8 %collective-permute-start.1 = (bf16[128,1536]{1,0:T(8,128)(2,1)S(1)}, bf16[128,1536]{1,0:T(8,128)(2,1)S(1)}, u32[]{:S(2)}, u32[]{:S(2)}) collective-permute-start(bf16[128,1536]{1,0:T(8,128)(2,1)S(1)} %bitcast.53), channel_id=1, source_target_pairs={{0,16},{1,17},{2,18},{3,19},{4,20},{5,21},{6,22},{7,23},{8,24},{9,... | collective-permute-start | bytes 1179656 | tf_op jit(solution)/shard_map/ppermute | solution.py:354
  32.1 18.4 %collective-permute-start = (bf16[128,1536]{1,0:T(8,128)(2,1)S(1)}, bf16[128,1536]{1,0:T(8,128)(2,1)S(1)}, u32[]{:S(2)}, u32[]{:S(2)}) collective-permute-start(bf16[128,1536]{1,0:T(8,128)(2,1)S(1)} %bitcast.54), channel_id=1, source_target_pairs={{0,8},{1,9},{2,10},{3,11},{4,12},{5,13},{6,14},{7,15},{8,0},{9,1},... | collective-permute-start | bytes 1179656 | tf_op jit(solution)/shard_map/ppermute | solution.py:354
  47.9 17.0 %collective-permute-start.5 = (bf16[128,1536]{1,0:T(8,128)(2,1)S(1)}, bf16[128,1536]{1,0:T(8,128)(2,1)}, u32[]{:S(2)}, u32[]{:S(2)}) collective-permute-start(bf16[128,1536]{1,0:T(8,128)(2,1)S(1)} %collective-permute-done.1.refs_2_), channel_id=1, source_target_pairs={{0,16},{1,17},{2,18},{3,19},{4,20},{5,21},{6,22},{7,23},{8,24},{9,... | collective-permute-start | bytes 1179656 | tf_op jit(solution)/shard_map/ppermute | solution.py:354
  47.9 19.8 %collective-permute-start.2 = (bf16[128,1536]{1,0:T(8,128)(2,1)S(1)}, bf16[128,1536]{1,0:T(8,128)(2,1)}, u32[]{:S(2)}, u32[]{:S(2)}) collective-permute-start(bf16[128,1536]{1,0:T(8,128)(2,1)S(1)} %bitcast.55), channel_id=1, source_target_pairs={{0,48},{1,49},{2,50},{3,51},{4,52},{5,53},{6,54},{7,55},{8,56},{9,... | collective-permute-start | bytes 1179656 | tf_op jit(solution)/shard_map/ppermute | solution.py:354
  50.6 26.2 %collective-permute-start.3 = (bf16[128,1536]{1,0:T(8,128)(2,1)S(1)}, bf16[128,1536]{1,0:T(8,128)(2,1)}, u32[]{:S(2)}, u32[]{:S(2)}) collective-permute-start(bf16[128,1536]{1,0:T(8,128)(2,1)S(1)} %collective-permute-done.refs_1_), channel_id=1, source_target_pairs={{0,16},{1,17},{2,18},{3,19},{4,20},{5,21},{6,22},{7,23},{8,24},{9,... | collective-permute-start | bytes 1179656 | tf_op jit(solution)/shard_map/ppermute | solution.py:354
  50.6 26.2 %collective-permute-start.4 = (bf16[128,1536]{1,0:T(8,128)(2,1)S(1)}, bf16[128,1536]{1,0:T(8,128)(2,1)}, u32[]{:S(2)}, u32[]{:S(2)}) collective-permute-start(bf16[128,1536]{1,0:T(8,128)(2,1)S(1)} %collective-permute-done.refs_1_), channel_id=1, source_target_pairs={{0,48},{1,49},{2,50},{3,51},{4,52},{5,53},{6,54},{7,55},{8,56},{9,... | collective-permute-start | bytes 1179656 | tf_op jit(solution)/shard_map/ppermute | solution.py:354
  64.9 11.8 %collective-permute-start.6 = (bf16[128,1536]{1,0:T(8,128)(2,1)}, bf16[128,1536]{1,0:T(8,128)(2,1)}, u32[]{:S(2)}, u32[]{:S(2)}) collective-permute-start(bf16[128,1536]{1,0:T(8,128)(2,1)} %collective-permute-done.5.refs_6_), channel_id=1, source_target_pairs={{0,8},{1,9},{2,10},{3,11},{4,12},{5,13},{6,14},{7,15},{8,0},{9,1},... | collective-permute-start | bytes 1179656 | tf_op jit(solution)/shard_map/ppermute | solution.py:354
  80.9 30.5 %all-to-all-start.2 = ((bf16[64,32,128]{2,1,0:T(8,128)(2,1)}), bf16[64,32,128]{2,1,0:T(8,128)(2,1)S(1)}, u32[]{:S(2)}, u32[]{:S(2)}) async-start(bf16[64,32,128]{2,1,0:T(8,128)(2,1)} %shard_map.91), calls=%async_computation.2 | async-start | bytes 1048576 | tf_op jit(solution)/shard_map/all_to_all | solution.py:346
  112.6 35.6 %all-to-all-start.3 = ((bf16[8,24,3072]{2,1,0:T(8,128)(2,1)}), bf16[8,24,3072]{2,1,0:T(8,128)(2,1)S(1)}, u32[]{:S(2)}, u32[]{:S(2)}) async-start(bf16[8,24,3072]{2,1,0:T(8,128)(2,1)} %broadcast_in_dim.25), calls=%async_computation.3 | async-start | bytes 2359296 | tf_op jit(solution)/shard_map/all_to_all | solution.py:346
  148.2 31.1 %collective-permute-start.7 = (bf16[192,3072]{1,0:T(8,128)(2,1)S(1)}, bf16[192,3072]{1,0:T(8,128)(2,1)S(1)}, u32[]{:S(2)}, u32[]{:S(2)}) collective-permute-start(bf16[192,3072]{1,0:T(8,128)(2,1)S(1)} %bitcast.45), channel_id=1, source_target_pairs={{0,8},{1,9},{2,10},{3,11},{4,12},{5,13},{6,14},{7,15},{8,0},{9,1},... | collective-permute-start | bytes 3538952 | tf_op jit(solution)/shard_map/ppermute | solution.py:354
  149.4 29.9 %collective-permute-start.8 = (bf16[192,3072]{1,0:T(8,128)(2,1)S(1)}, bf16[192,3072]{1,0:T(8,128)(2,1)S(1)}, u32[]{:S(2)}, u32[]{:S(2)}) collective-permute-start(bf16[192,3072]{1,0:T(8,128)(2,1)S(1)} %bitcast.46), channel_id=1, source_target_pairs={{0,16},{1,17},{2,18},{3,19},{4,20},{5,21},{6,22},{7,23},{8,24},{9,... | collective-permute-start | bytes 3538952 | tf_op jit(solution)/shard_map/ppermute | solution.py:354
  150.6 28.7 %collective-permute-start.9 = (bf16[192,3072]{1,0:T(8,128)(2,1)S(1)}, bf16[192,3072]{1,0:T(8,128)(2,1)S(1)}, u32[]{:S(2)}, u32[]{:S(2)}) collective-permute-start(bf16[192,3072]{1,0:T(8,128)(2,1)S(1)} %bitcast.47), channel_id=1, source_target_pairs={{0,48},{1,49},{2,50},{3,51},{4,52},{5,53},{6,54},{7,55},{8,56},{9,... | collective-permute-start | bytes 3538952 | tf_op jit(solution)/shard_map/ppermute | solution.py:354
  155.4 28.7 %copy-start.21 = (bf16[64,4096]{1,0:T(8,128)(2,1)S(1)}, bf16[64,4096]{1,0:T(8,128)(2,1)}, u32[]{:S(2)}) copy-start(bf16[64,4096]{1,0:T(8,128)(2,1)} %copy-done.19) | copy-start | bytes 1572868
  180.4 28.8 %collective-permute-start.10 = (bf16[192,3072]{1,0:T(8,128)(2,1)S(1)}, bf16[192,3072]{1,0:T(8,128)(2,1)}, u32[]{:S(2)}, u32[]{:S(2)}) collective-permute-start(bf16[192,3072]{1,0:T(8,128)(2,1)S(1)} %collective-permute-done.7.refs_1_), channel_id=1, source_target_pairs={{0,16},{1,17},{2,18},{3,19},{4,20},{5,21},{6,22},{7,23},{8,24},{9,... | collective-permute-start | bytes 3538952 | tf_op jit(solution)/shard_map/ppermute | solution.py:354
  181.4 27.7 %collective-permute-start.11 = (bf16[192,3072]{1,0:T(8,128)(2,1)S(1)}, bf16[192,3072]{1,0:T(8,128)(2,1)}, u32[]{:S(2)}, u32[]{:S(2)}) collective-permute-start(bf16[192,3072]{1,0:T(8,128)(2,1)S(1)} %collective-permute-done.7.refs_1_), channel_id=1, source_target_pairs={{0,48},{1,49},{2,50},{3,51},{4,52},{5,53},{6,54},{7,55},{8,56},{9,... | collective-permute-start | bytes 3538952 | tf_op jit(solution)/shard_map/ppermute | solution.py:354
  209.2 49.8 %all-to-all-start.4 = ((bf16[64,96,128]{2,1,0:T(8,128)(2,1)}), bf16[64,96,128]{2,1,0:T(8,128)(2,1)S(1)}, u32[]{:S(2)}, u32[]{:S(2)}) async-start(bf16[64,96,128]{2,1,0:T(8,128)(2,1)} %copy-done.6), calls=%async_computation.4 | async-start | bytes 3145728 | tf_op jit(solution)/shard_map/all_to_all | solution.py:346
  215.9 22.0 %collective-permute-start.12 = (bf16[96,3072]{1,0:T(8,128)(2,1)}, bf16[96,3072]{1,0:T(8,128)(2,1)}, u32[]{:S(2)}, u32[]{:S(2)}) collective-permute-start(bf16[96,3072]{1,0:T(8,128)(2,1)} %slice.14), channel_id=1, source_target_pairs={{0,16},{1,17},{2,18},{3,19},{4,20},{5,21},{6,22},{7,23},{8,24},{9,... | collective-permute-start | bytes 1769480 | tf_op jit(solution)/shard_map/ppermute | solution.py:354
  217.8 24.4 %collective-permute-start.13 = (bf16[96,3072]{1,0:T(8,128)(2,1)}, bf16[96,3072]{1,0:T(8,128)(2,1)}, u32[]{:S(2)}, u32[]{:S(2)}) collective-permute-start(bf16[96,3072]{1,0:T(8,128)(2,1)} %slice.15), channel_id=1, source_target_pairs={{0,48},{1,49},{2,50},{3,51},{4,52},{5,53},{6,54},{7,55},{8,56},{9,... | collective-permute-start | bytes 1769480 | tf_op jit(solution)/shard_map/ppermute | solution.py:354
  221.4 37.6 %copy-start.12 = (f32[1,1536]{1,0:T(1,128)S(1)}, f32[1,1536]{1,0:T(1,128)}, u32[]{:S(2)}) copy-start(f32[1,1536]{1,0:T(1,128)} %gain_ref.1) | copy-start | bytes 18436
  221.4 37.1 %collective-permute-start.14 = (bf16[96,3072]{1,0:T(8,128)(2,1)}, bf16[96,3072]{1,0:T(8,128)(2,1)}, u32[]{:S(2)}, u32[]{:S(2)}) collective-permute-start(bf16[96,3072]{1,0:T(8,128)(2,1)} %slice.16), channel_id=1, source_target_pairs={{0,16},{1,17},{2,18},{3,19},{4,20},{5,21},{6,22},{7,23},{8,24},{9,... | collective-permute-start | bytes 1769480 | tf_op jit(solution)/shard_map/ppermute | solution.py:354
  223.3 35.7 %collective-permute-start.15 = (bf16[96,3072]{1,0:T(8,128)(2,1)}, bf16[96,3072]{1,0:T(8,128)(2,1)}, u32[]{:S(2)}, u32[]{:S(2)}) collective-permute-start(bf16[96,3072]{1,0:T(8,128)(2,1)} %slice.17), channel_id=1, source_target_pairs={{0,48},{1,49},{2,50},{3,51},{4,52},{5,53},{6,54},{7,55},{8,56},{9,... | collective-permute-start | bytes 1769480 | tf_op jit(solution)/shard_map/ppermute | solution.py:354
  271.4 14.5 %collective-permute-start.16 = (bf16[4,64,1536]{2,1,0:T(8,128)(2,1)S(1)}, bf16[4,64,1536]{2,1,0:T(8,128)(2,1)S(1)}, u32[]{:S(2)}, u32[]{:S(2)}) collective-permute-start(bf16[4,64,1536]{2,1,0:T(8,128)(2,1)S(1)} %shard_map.98), channel_id=1, source_target_pairs={{0,192},{64,0},{128,64},{192,128},{1,193},{65,1},{129,65},{193,129... | collective-permute-start | bytes 2359304 | tf_op jit(solution)/shard_map/ppermute | solution.py:422
  (25 other events, 143.7 us)

commit v4 on v3

--- a/solution.py
+++ b/solution.py
@@ -16,7 +16,6 @@
 PLAIN_DOT = (((1,), (0,)), ((), ()))
 MIB = 1024 * 1024
 QB = 256
-UNIT = 96
 KB = 256
 UNROLL1 = True
 UNROLL2 = True
@@ -24,10 +23,15 @@
 BF16 = jnp.bfloat16
 F32 = jnp.float32
 WHOLE = pl.BlockSpec(memory_space=pltpu.VMEM)
+ROOM = 60 * MIB
 
 
 def cost(flops, moved, exps=0):
     return pl.CostEstimate(flops=flops, bytes_accessed=moved, transcendentals=exps)
+
+
+def fixed(array):
+    return pl.BlockSpec(array.shape, lambda i: (0,) * len(array.shape))
 
 
 def halves(even, odd):
@@ -124,16 +128,18 @@
 
 def prepare(valid, received):
     length = received.shape[0] * 64
+    out_shape = [
+        jax.ShapeDtypeStruct((length, 128), BF16),
+        jax.ShapeDtypeStruct((128, length), BF16),
+        jax.ShapeDtypeStruct((HS, length), BF16),
+    ]
     return pl.pallas_call(
         prepare_kernel,
-        out_shape=[
-            jax.ShapeDtypeStruct((length, 128), BF16),
-            jax.ShapeDtypeStruct((128, length), BF16),
-            jax.ShapeDtypeStruct((HS, length), BF16),
-        ],
-        in_specs=[pl.BlockSpec(memory_space=pltpu.SMEM), WHOLE],
-        out_specs=[WHOLE] * 3,
-        compiler_params=pltpu.CompilerParams(vmem_limit_bytes=16 * MIB),
+        grid=(1,),
+        out_shape=out_shape,
+        in_specs=[pl.BlockSpec(memory_space=pltpu.SMEM), fixed(received)],
+        out_specs=[fixed(shape) for shape in out_shape],
+        compiler_params=pltpu.CompilerParams(vmem_limit_bytes=ROOM),
         cost_estimate=cost(0, 4 * MIB),
     )(valid, received)
 
@@ -164,7 +170,6 @@
 def softmax_weights(part, gate, keys, queries_t):
     length = keys.shape[0]
     blocks = length // QB // 2
-    fixed = lambda shape: pl.BlockSpec(shape, lambda i: (0,) * len(shape))
     return pl.pallas_call(
         weights_kernel,
         grid=(blocks,),
@@ -174,7 +179,7 @@
         ],
         in_specs=[
             pl.BlockSpec(memory_space=pltpu.SMEM),
-            fixed(keys.shape),
+            fixed(keys),
             pl.BlockSpec((128, QB), lambda i: (0, part * blocks + i)),
         ],
         out_specs=[
@@ -182,7 +187,7 @@
             pl.BlockSpec((1, QB), lambda i: (0, i)),
         ],
         scratch_shapes=[pltpu.VMEM((length, QB), F32)],
-        compiler_params=pltpu.CompilerParams(vmem_limit_bytes=24 * MIB),
+        compiler_params=pltpu.CompilerParams(vmem_limit_bytes=ROOM),
         cost_estimate=cost(4 * length * length * HS, 2 * length * length, length * length // 2),
     )(gate, keys, queries_t)
 
@@ -260,7 +265,6 @@
     else:
         out_shape = jax.ShapeDtypeStruct((sources, 96, 128), BF16)
         scratch += [pltpu.VMEM((length, 128), F32), pltpu.VMEM((HS, length // 2), F32)]
-    fixed = lambda array: pl.BlockSpec(array.shape, lambda i: (0,) * len(array.shape))
     return pl.pallas_call(
         functools.partial(grads_kernel, part),
         grid=(blocks,),
@@ -273,16 +277,17 @@
         + [fixed(array) for array in (keys_t, received, received_grads, *begun)],
         out_specs=jax.tree.map(fixed, out_shape),
         scratch_shapes=scratch,
-        compiler_params=pltpu.CompilerParams(vmem_limit_bytes=44 * MIB),
+        compiler_params=pltpu.CompilerParams(vmem_limit_bytes=ROOM),
         cost_estimate=cost(16 * length * length * HS, 2 * length * length),
     )(weights, sums, queries_t, keys_t, received, received_grads, *begun)
 
 
-def finish_kernel(start_ref, back_ref, x_ref, g_ref, gain_ref, *refs):
+def finish_kernel(owner_ref, back_ref, x_ref, g_ref, gain_ref, *refs):
     pieces, (out_ref, j_ref, n_ref, w_ref, sems) = refs[:-5], refs[-5:]
     copies = []
     for n, piece in enumerate(pieces):
-        to = pl.ds(pl.multiple_of(start_ref[n] * UNIT, UNIT), piece.shape[0])
+        rows = piece.shape[0]
+        to = pl.ds(pl.multiple_of(owner_ref[n] * rows, rows), rows)
         copies.append(pltpu.make_async_copy(piece, w_ref.at[to, :], sems.at[n]))
         copies[-1].start()
     records = x_ref.shape[0]
@@ -322,24 +327,27 @@
         out_ref[r] = (g_ref[r].astype(F32) + residual).astype(BF16)
 
 
-def finish(starts, pieces, back, inputs, grads, gain):
+def finish(owners, pieces, back, inputs, grads, gain):
     records, frames, width = inputs.shape
     anywhere = pl.BlockSpec(memory_space=pltpu.HBM)
     depth = pieces[0].shape[1]
     return pl.pallas_call(
         finish_kernel,
+        grid=(1,),
         out_shape=jax.ShapeDtypeStruct(inputs.shape, BF16),
-        in_specs=[pl.BlockSpec(memory_space=pltpu.SMEM)] + [WHOLE] * 4 + [anywhere] * len(pieces),
-        out_specs=WHOLE,
+        in_specs=[pl.BlockSpec(memory_space=pltpu.SMEM)]
+        + [fixed(array) for array in (back, inputs, grads, gain)]
+        + [anywhere] * len(pieces),
+        out_specs=fixed(inputs),
         scratch_shapes=[
             pltpu.VMEM((records * frames, depth), BF16),
             pltpu.VMEM((records * frames, width), F32),
             pltpu.VMEM((width, depth), BF16),
             pltpu.SemaphoreType.DMA((len(pieces),)),
         ],
-        compiler_params=pltpu.CompilerParams(vmem_limit_bytes=32 * MIB),
+        compiler_params=pltpu.CompilerParams(vmem_limit_bytes=ROOM),
         cost_estimate=cost(2 * records * frames * width * depth, 2 * depth * width),
-    )(starts, back, inputs, grads, gain, *pieces)
+    )(owners, back, inputs, grads, gain, *pieces)
 
 
 def exchange(items, groups=None):
@@ -413,11 +421,8 @@
     diagonal = [across(partner, 1, 0), across(partner, 3, 0)]
     gradients, *diagonal = lax.optimization_barrier((gradients, *diagonal))
     back = exchange(gradients)
-    far = []
-    for down, up in ((below, above), tuple(diagonal)):
-        far += [across(down[:UNIT], 1, 0), across(up[UNIT:], 3, 0)]
-    starts = jnp.concatenate([2 * places[:6], jnp.stack([2 * places[6], 2 * places[6] + 1, 2 * places[7], 2 * places[7] + 1])])
-    result = finish(starts, [qkv_group] + near + diagonal + far, back, inputs, grads, norm_gain)
+    far = [across(after(below, gradients), 1, 0), across(diagonal[1], 3, 0)]
+    result = finish(places, [qkv_group] + near + diagonal + far, back, inputs, grads, norm_gain)
     count = lax.axis_size("section")
     moved = lax.ppermute(result, "section", [(i, (i - 1) % count) for i in range(count)])
     return moved.transpose(1, 0, 2)[None]

time: 288 us -> 289 us (level)
  local copies, waits for them, and re-layouts: 33.1 us -> 11.1 us
  Pallas kernels: 92.9 us -> 107 us
  waiting for transfers between devices: 102 us -> 113 us
    unnamed x59 -> x37, local copies, waits for them, and re-layouts: 21.7 us -> 6.66 us
    ppermute x16 -> x14, waiting for transfers between devices: 65.9 us -> 76.1 us  [across(): return lax.ppermute(rows, 'seq', seq_pairs(dy, dx, 0))]
    slice x4 -> x0, local copies, waits for them, and re-layouts: 6.78 us -> none  [on_device(): far += [across(down[:UNIT], 1, 0), across(up[UNIT:], 3, 0)]]
    pallas_call x2, Pallas kernels: 47.8 us -> 54.3 us  [attention_grads(): pl.pallas_call(functools.partial(grads_kernel, part), grid=(blocks,), out...]
    pallas_call x2, Pallas kernels: 9.04 us -> 14.5 us  [the longest x1 9.88 us: finish(): pl.pallas_call(finish_kernel, grid=(1,), out_shape=jax.ShapeDtypeStruct(i...]
    ppermute x16 -> x14, starting transfers between devices: 20 us -> 17 us  [across(): return lax.ppermute(rows, 'seq', seq_pairs(dy, dx, 0))]
  transfers between devices with their start and end apart: 22 -> 20, of which waited for: 10 -> 7; matrix products, arithmetic and copies ran while one was open for 4% -> 1% of each run, Pallas kernels for 30% -> 34%
where the time goes in v4:
time: 289 us; the launch traced here: 288 us
  waiting for transfers between devices  113 us (39%)
  Pallas kernels  107 us (37%)
  starting transfers between devices  56.3 us (19%)
  local copies, waits for them, and re-layouts  11.1 us (4%)
    ppermute x14, waiting for transfers between devices, across(): return lax.ppermute(rows, 'seq', seq_pairs(dy, dx, 0))  76.1 us
    pallas_call x2, Pallas kernels, attention_grads(): pl.pallas_call(functools.partial(grads_kernel, part), grid=(blocks,), out...  54.3 us
    all_to_all x5, starting transfers between devices, exchange(): lax.all_to_all(items, 'seq', split_axis=0, concat_axis=0, tiled=True, axi...  35.6 us
    pallas_call x2, Pallas kernels, softmax_weights(): pl.pallas_call(weights_kernel, grid=(blocks,), out_shape=[jax.ShapeDtypeS...  32.7 us
    all_to_all x5, waiting for transfers between devices, exchange(): lax.all_to_all(items, 'seq', split_axis=0, concat_axis=0, tiled=True, axi...  24.8 us
    ppermute x14, starting transfers between devices, across(): return lax.ppermute(rows, 'seq', seq_pairs(dy, dx, 0))  17 us
    ppermute x1, waiting for transfers between devices, on_device(): lax.ppermute(result, 'section', [(i, (i - 1) % count) for i in range(coun...  12.2 us
    pallas_call x1, Pallas kernels, finish(): pl.pallas_call(finish_kernel, grid=(1,), out_shape=jax.ShapeDtypeStruct(i...  9.88 us
  transfers between devices with their start and end apart: 20, of which 7 were waited for; matrix products, arithmetic and copies ran while one was open for 1% of the time, Pallas kernels for 34%

profile of v4, /device:TPU:1, one launch (start us, length us, event | category | flops | bytes accessed | tf_op | source)
XLA Modules:
  0.0 288.4 jit_solution(12709085072091263641)
XLA Ops:
  1.7 9.0 %all-to-all-start = ((bf16[8,16,1536]{2,1,0:T(8,128)(2,1)}), bf16[8,16,1536]{2,1,0:T(8,128)(2,1)S(1)}, u32[]{:S(2)}, u32[]{:S(2)}) async-start(bf16[8,16,1536]{2,1,0:T(8,128)(2,1)} %broadcast_in_dim.23), calls=%async_computation | async-start | bytes 786432 | tf_op jit(solution)/shard_map/all_to_all | solution.py:354
  13.5 11.3 %all-to-all-done = bf16[8,16,1536]{2,1,0:T(8,128)(2,1)S(1)} async-done(((bf16[8,16,1536]{2,1,0:T(8,128)(2,1)}), bf16[8,16,1536]{2,1,0:T(8,128)(2,1)S(1)}, u32[]{:S(2)}, u32[]{:S(2)}) %all-to-all-start) | async-done | bytes 393248 | tf_op jit(solution)/shard_map/all_to_all | solution.py:354
  24.9 6.4 %all-to-all-start.1 = ((bf16[64,96,128]{2,1,0:T(8,128)(2,1)}), bf16[64,96,128]{2,1,0:T(8,128)(2,1)}, u32[]{:S(2)}, u32[]{:S(2)}) async-start(bf16[64,96,128]{2,1,0:T(8,128)(2,1)} %shard_map.92), calls=%async_computation.1 | async-start | bytes 3145728 | tf_op jit(solution)/shard_map/all_to_all | solution.py:354
  33.5 15.5 %collective-permute-done.1.refs_2_ = bf16[128,1536]{1,0:T(8,128)(2,1)S(1)} collective-permute-done((bf16[128,1536]{1,0:T(8,128)(2,1)S(1)}, bf16[128,1536]{1,0:T(8,128)(2,1)S(1)}, u32[]{:S(2)}, u32[]{:S(2)}) %collective-permute-start.1) | collective-permute-done | bytes 393248 | tf_op jit(solution)/shard_map/ppermute | solution.py:362
  49.0 2.7 collective-permute-start.2
  51.7 2.7 collective-permute-start.4
  54.3 12.9 %collective-permute-done.5.refs_6_ = bf16[128,1536]{1,0:T(8,128)(2,1)S(1)} collective-permute-done((bf16[128,1536]{1,0:T(8,128)(2,1)S(1)}, bf16[128,1536]{1,0:T(8,128)(2,1)S(1)}, u32[]{:S(2)}, u32[]{:S(2)}) %collective-permute-start.5) | collective-permute-done | bytes 393248 | tf_op jit(solution)/shard_map/ppermute | solution.py:362
  68.7 8.9 %collective-permute-done.3.refs_4_ = bf16[128,1536]{1,0:T(8,128)(2,1)S(1)} collective-permute-done((bf16[128,1536]{1,0:T(8,128)(2,1)S(1)}, bf16[128,1536]{1,0:T(8,128)(2,1)S(1)}, u32[]{:S(2)}, u32[]{:S(2)}) %collective-permute-start.3) | collective-permute-done | bytes 393248 | tf_op jit(solution)/shard_map/ppermute | solution.py:362
  77.6 3.7 %shard_map.91 = bf16[64,32,128]{2,1,0:T(8,128)(2,1)} custom-call(s32[8]{0:T(128)S(1)} %stack.35.owner_ref, bf16[256,1536]{1,0:T(8,128)(2,1)S(1)} %bitcast.39, bf16[128,1536]{1,0:T(8,128)(2,1)S(1)} %bitcast.47, bf16[128,1536]{1,0:T(8,128)(2,1)S(1)} %collective-permute-done.refs_1_, bf16[128,1536]{1,0:T(8,128)(2,1)S(1)} %collective-permute-done.1.refs_2_, ...), custom_call_target="tpu_custom_call" | custom-call | flops 805306368 | bytes 4456448 | tf_op jit(solution)/shard_map/pallas_call | solution.py:92
  81.3 9.4 %all-to-all-start.2 = ((bf16[64,32,128]{2,1,0:T(8,128)(2,1)}), bf16[64,32,128]{2,1,0:T(8,128)(2,1)S(1)}, u32[]{:S(2)}, u32[]{:S(2)}) async-start(bf16[64,32,128]{2,1,0:T(8,128)(2,1)} %shard_map.91), calls=%async_computation.2 | async-start | bytes 1048576 | tf_op jit(solution)/shard_map/all_to_all | solution.py:354
  91.4 4.6 %shard_map.93 = (bf16[4096,128]{1,0:T(8,128)(2,1)}, bf16[128,4096]{1,0:T(8,128)(2,1)}, bf16[64,4096]{1,0:T(8,128)(2,1)}) custom-call(s32[1]{0:T(128)} %bitcast.9.length_ref.gate_ref, bf16[64,96,128]{2,1,0:T(8,128)(2,1)} %all-to-all-done.1.r_ref), custom_call_target="tpu_custom_call" | custom-call | bytes 4194304 | tf_op jit(solution)/shard_map/pallas_call | solution.py:136
  95.9 16.4 %shard_map.94 = (f32[8,4096,256]{2,1,0:T(8,128)}, f32[1,2048]{1,0:T(1,128)}) custom-call(s32[1]{0:T(128)} %bitcast.9.length_ref.gate_ref, bf16[4096,128]{1,0:T(8,128)(2,1)} %get-tuple-element.29.kz_ref, bf16[128,4096]{1,0:T(8,128)(2,1)} %get-tuple-element.30.qt_ref), custom_call_target="tpu_custom_call" | custom-call | flops 4294967296 | bytes 33554432 | tf_op jit(solution)/shard_map/pallas_call | solution.py:173
  113.6 6.0 %all-to-all-start.3 = ((bf16[8,24,3072]{2,1,0:T(8,128)(2,1)}), bf16[8,24,3072]{2,1,0:T(8,128)(2,1)S(1)}, u32[]{:S(2)}, u32[]{:S(2)}) async-start(bf16[8,24,3072]{2,1,0:T(8,128)(2,1)} %broadcast_in_dim.25), calls=%async_computation.3 | async-start | bytes 2359296 | tf_op jit(solution)/shard_map/all_to_all | solution.py:354
  119.6 16.3 %shard_map.95 = (f32[8,4096,256]{2,1,0:T(8,128)}, f32[1,2048]{1,0:T(1,128)}) custom-call(s32[1]{0:T(128)} %bitcast.9.length_ref.gate_ref, bf16[4096,128]{1,0:T(8,128)(2,1)} %get-tuple-element.29.kz_ref, bf16[128,4096]{1,0:T(8,128)(2,1)} %get-tuple-element.30.qt_ref), custom_call_target="tpu_custom_call" | custom-call | flops 4294967296 | bytes 33554432 | tf_op jit(solution)/shard_map/pallas_call | solution.py:173
  136.0 13.5 %all-to-all-done.3 = bf16[8,24,3072]{2,1,0:T(8,128)(2,1)S(1)} async-done(((bf16[8,24,3072]{2,1,0:T(8,128)(2,1)}), bf16[8,24,3072]{2,1,0:T(8,128)(2,1)S(1)}, u32[]{:S(2)}, u32[]{:S(2)}) %all-to-all-start.3) | async-done | bytes 1179680 | tf_op jit(solution)/shard_map/all_to_all | solution.py:354
  153.3 26.1 %shard_map.96 = (f32[64,2048]{1,0:T(8,128)}, f32[4096,128]{1,0:T(8,128)}) custom-call(f32[8,4096,256]{2,1,0:T(8,128)} %get-tuple-element.38.w_ref, f32[1,2048]{1,0:T(1,128)} %get-tuple-element.39.l_ref, bf16[128,4096]{1,0:T(8,128)(2,1)} %get-tuple-element.30.qt_ref, bf16[64,4096]{1,0:T(8,128)(2,1)} %get-tuple-element.37.kt_ref, ...), custom_call_target="tpu_custom_call" | custom-call | flops 17179869184 | bytes 33554432 | tf_op jit(solution)/shard_map/pallas_call | solution.py:268
  179.6 2.7 collective-permute-start.11
  182.3 28.2 %shard_map.97 = bf16[64,96,128]{2,1,0:T(8,128)(2,1)} custom-call(f32[8,4096,256]{2,1,0:T(8,128)} %get-tuple-element.33.w_ref, f32[1,2048]{1,0:T(1,128)} %get-tuple-element.36.l_ref, bf16[128,4096]{1,0:T(8,128)(2,1)} %get-tuple-element.30.qt_ref, bf16[64,4096]{1,0:T(8,128)(2,1)} %get-tuple-element.37.kt_ref, bf16[64,96,128]{2,1,0:T(8,128)(2,1)} %all-to-all-done.1.r_ref, ...), custom_call_target="tpu_custom_call" | custom-call | flops 17179869184 | bytes 33554432 | tf_op jit(solution)/shard_map/pallas_call | solution.py:268
  211.5 4.8 %all-to-all-start.4 = ((bf16[64,96,128]{2,1,0:T(8,128)(2,1)}), bf16[64,96,128]{2,1,0:T(8,128)(2,1)S(1)}, u32[]{:S(2)}, u32[]{:S(2)}) async-start(bf16[64,96,128]{2,1,0:T(8,128)(2,1)} %shard_map.97), calls=%async_computation.4 | async-start | bytes 3145728 | tf_op jit(solution)/shard_map/all_to_all | solution.py:354
  217.4 1.7 collective-permute-start.13
  220.1 38.8 %collective-permute-done.12.refs_6_ = bf16[192,3072]{1,0:T(8,128)(2,1)S(1)} collective-permute-done((bf16[192,3072]{1,0:T(8,128)(2,1)S(1)}, bf16[192,3072]{1,0:T(8,128)(2,1)S(1)}, u32[]{:S(2)}, u32[]{:S(2)}) %collective-permute-start.12) | collective-permute-done | bytes 1179680 | tf_op jit(solution)/shard_map/ppermute | solution.py:362
  261.1 9.9 %shard_map.98 = bf16[4,64,1536]{2,1,0:T(8,128)(2,1)} custom-call(s32[8]{0:T(128)} %copy-done.1, bf16[64,96,128]{2,1,0:T(8,128)(2,1)} %copy-done.2, bf16[4,64,1536]{2,1,0:T(8,128)(2,1)} %bitcast.52, bf16[4,64,1536]{2,1,0:T(8,128)(2,1)} %bitcast.40, f32[1,1536]{1,0:T(1,128)} %gain_ref.1, bf16[192,3072]{1,0:T(8,128)(2,1)} %bitcast.51, ...), custom_call_target="tpu_custom_call" | custom-call | flops 2415919104 | bytes 9437184 | tf_op jit(solution)/shard_map/pallas_call | solution.py:334
  270.9 3.8 %collective-permute-start.14 = (bf16[4,64,1536]{2,1,0:T(8,128)(2,1)}, bf16[4,64,1536]{2,1,0:T(8,128)(2,1)S(1)}, u32[]{:S(2)}, u32[]{:S(2)}) collective-permute-start(bf16[4,64,1536]{2,1,0:T(8,128)(2,1)} %shard_map.98), channel_id=1, source_target_pairs={{0,192},{64,0},{128,64},{192,128},{1,193},{65,1},{129,65},{193,129... | collective-permute-start | bytes 2359304 | tf_op jit(solution)/shard_map/ppermute | solution.py:427
  274.7 12.2 %collective-permute-done.14 = bf16[4,64,1536]{2,1,0:T(8,128)(2,1)S(1)} collective-permute-done((bf16[4,64,1536]{2,1,0:T(8,128)(2,1)}, bf16[4,64,1536]{2,1,0:T(8,128)(2,1)S(1)}, u32[]{:S(2)}, u32[]{:S(2)}) %collective-permute-start.14) | collective-permute-done | bytes 786464 | tf_op jit(solution)/shard_map/ppermute | solution.py:427
  (66 shorter events, 20.8 us)
Async XLA Ops:
  1.7 23.2 %all-to-all-start = ((bf16[8,16,1536]{2,1,0:T(8,128)(2,1)}), bf16[8,16,1536]{2,1,0:T(8,128)(2,1)S(1)}, u32[]{:S(2)}, u32[]{:S(2)}) async-start(bf16[8,16,1536]{2,1,0:T(8,128)(2,1)} %broadcast_in_dim.23), calls=%async_computation | async-start | bytes 786432 | tf_op jit(solution)/shard_map/all_to_all | solution.py:354
  24.9 56.4 %all-to-all-start.1 = ((bf16[64,96,128]{2,1,0:T(8,128)(2,1)}), bf16[64,96,128]{2,1,0:T(8,128)(2,1)}, u32[]{:S(2)}, u32[]{:S(2)}) async-start(bf16[64,96,128]{2,1,0:T(8,128)(2,1)} %shard_map.92), calls=%async_computation.1 | async-start | bytes 3145728 | tf_op jit(solution)/shard_map/all_to_all | solution.py:354
  31.2 17.7 %collective-permute-start.1 = (bf16[128,1536]{1,0:T(8,128)(2,1)S(1)}, bf16[128,1536]{1,0:T(8,128)(2,1)S(1)}, u32[]{:S(2)}, u32[]{:S(2)}) collective-permute-start(bf16[128,1536]{1,0:T(8,128)(2,1)S(1)} %bitcast.44), channel_id=1, source_target_pairs={{0,16},{1,17},{2,18},{3,19},{4,20},{5,21},{6,22},{7,23},{8,24},{9,... | collective-permute-start | bytes 1179656 | tf_op jit(solution)/shard_map/ppermute | solution.py:362
  32.3 19.4 %collective-permute-start = (bf16[128,1536]{1,0:T(8,128)(2,1)S(1)}, bf16[128,1536]{1,0:T(8,128)(2,1)S(1)}, u32[]{:S(2)}, u32[]{:S(2)}) collective-permute-start(bf16[128,1536]{1,0:T(8,128)(2,1)S(1)} %bitcast.45), channel_id=1, source_target_pairs={{0,8},{1,9},{2,10},{3,11},{4,12},{5,13},{6,14},{7,15},{8,0},{9,1},... | collective-permute-start | bytes 1179656 | tf_op jit(solution)/shard_map/ppermute | solution.py:362
  49.0 18.3 %collective-permute-start.5 = (bf16[128,1536]{1,0:T(8,128)(2,1)S(1)}, bf16[128,1536]{1,0:T(8,128)(2,1)S(1)}, u32[]{:S(2)}, u32[]{:S(2)}) collective-permute-start(bf16[128,1536]{1,0:T(8,128)(2,1)S(1)} %collective-permute-done.1.refs_2_), channel_id=1, source_target_pairs={{0,16},{1,17},{2,18},{3,19},{4,20},{5,21},{6,22},{7,23},{8,24},{9,... | collective-permute-start | bytes 1179656 | tf_op jit(solution)/shard_map/ppermute | solution.py:362
  49.0 19.7 %collective-permute-start.2 = (bf16[128,1536]{1,0:T(8,128)(2,1)S(1)}, bf16[128,1536]{1,0:T(8,128)(2,1)S(1)}, u32[]{:S(2)}, u32[]{:S(2)}) collective-permute-start(bf16[128,1536]{1,0:T(8,128)(2,1)S(1)} %bitcast.46), channel_id=1, source_target_pairs={{0,48},{1,49},{2,50},{3,51},{4,52},{5,53},{6,54},{7,55},{8,56},{9,... | collective-permute-start | bytes 1179656 | tf_op jit(solution)/shard_map/ppermute | solution.py:362
  51.7 25.9 %collective-permute-start.3 = (bf16[128,1536]{1,0:T(8,128)(2,1)S(1)}, bf16[128,1536]{1,0:T(8,128)(2,1)S(1)}, u32[]{:S(2)}, u32[]{:S(2)}) collective-permute-start(bf16[128,1536]{1,0:T(8,128)(2,1)S(1)} %collective-permute-done.refs_1_), channel_id=1, source_target_pairs={{0,16},{1,17},{2,18},{3,19},{4,20},{5,21},{6,22},{7,23},{8,24},{9,... | collective-permute-start | bytes 1179656 | tf_op jit(solution)/shard_map/ppermute | solution.py:362
  51.7 25.9 %collective-permute-start.4 = (bf16[128,1536]{1,0:T(8,128)(2,1)S(1)}, bf16[128,1536]{1,0:T(8,128)(2,1)S(1)}, u32[]{:S(2)}, u32[]{:S(2)}) collective-permute-start(bf16[128,1536]{1,0:T(8,128)(2,1)S(1)} %collective-permute-done.refs_1_), channel_id=1, source_target_pairs={{0,48},{1,49},{2,50},{3,51},{4,52},{5,53},{6,54},{7,55},{8,56},{9,... | collective-permute-start | bytes 1179656 | tf_op jit(solution)/shard_map/ppermute | solution.py:362
  67.3 10.3 %collective-permute-start.6 = (bf16[128,1536]{1,0:T(8,128)(2,1)S(1)}, bf16[128,1536]{1,0:T(8,128)(2,1)}, u32[]{:S(2)}, u32[]{:S(2)}) collective-permute-start(bf16[128,1536]{1,0:T(8,128)(2,1)S(1)} %collective-permute-done.5.refs_6_), channel_id=1, source_target_pairs={{0,8},{1,9},{2,10},{3,11},{4,12},{5,13},{6,14},{7,15},{8,0},{9,1},... | collective-permute-start | bytes 1179656 | tf_op jit(solution)/shard_map/ppermute | solution.py:362
  81.3 31.1 %all-to-all-start.2 = ((bf16[64,32,128]{2,1,0:T(8,128)(2,1)}), bf16[64,32,128]{2,1,0:T(8,128)(2,1)S(1)}, u32[]{:S(2)}, u32[]{:S(2)}) async-start(bf16[64,32,128]{2,1,0:T(8,128)(2,1)} %shard_map.91), calls=%async_computation.2 | async-start | bytes 1048576 | tf_op jit(solution)/shard_map/all_to_all | solution.py:354
  95.9 16.4 %copy-start.14 = (bf16[1,24,3072]{2,1,0:T(8,128)(2,1)S(1)}, bf16[1,24,3072]{2,1,0:T(8,128)(2,1)}, u32[]{:S(2)}) copy-start(bf16[1,24,3072]{2,1,0:T(8,128)(2,1)} %param.16) | copy-start | bytes 442372
  113.6 35.8 %all-to-all-start.3 = ((bf16[8,24,3072]{2,1,0:T(8,128)(2,1)}), bf16[8,24,3072]{2,1,0:T(8,128)(2,1)S(1)}, u32[]{:S(2)}, u32[]{:S(2)}) async-start(bf16[8,24,3072]{2,1,0:T(8,128)(2,1)} %broadcast_in_dim.25), calls=%async_computation.3 | async-start | bytes 2359296 | tf_op jit(solution)/shard_map/all_to_all | solution.py:354
  149.4 30.0 %copy-start.3 = (bf16[8,24,3072]{2,1,0:T(8,128)(2,1)}, bf16[8,24,3072]{2,1,0:T(8,128)(2,1)S(1)}, u32[]{:S(2)}) copy-start(bf16[8,24,3072]{2,1,0:T(8,128)(2,1)S(1)} %all-to-all-done.3) | copy-start | bytes 3538948
  149.4 30.0 %collective-permute-start.7 = (bf16[192,3072]{1,0:T(8,128)(2,1)S(1)}, bf16[192,3072]{1,0:T(8,128)(2,1)S(1)}, u32[]{:S(2)}, u32[]{:S(2)}) collective-permute-start(bf16[192,3072]{1,0:T(8,128)(2,1)S(1)} %bitcast.48), channel_id=1, source_target_pairs={{0,8},{1,9},{2,10},{3,11},{4,12},{5,13},{6,14},{7,15},{8,0},{9,1},... | collective-permute-start | bytes 3538952 | tf_op jit(solution)/shard_map/ppermute | solution.py:362
  150.6 28.8 %collective-permute-start.8 = (bf16[192,3072]{1,0:T(8,128)(2,1)S(1)}, bf16[192,3072]{1,0:T(8,128)(2,1)S(1)}, u32[]{:S(2)}, u32[]{:S(2)}) collective-permute-start(bf16[192,3072]{1,0:T(8,128)(2,1)S(1)} %bitcast.49), channel_id=1, source_target_pairs={{0,16},{1,17},{2,18},{3,19},{4,20},{5,21},{6,22},{7,23},{8,24},{9,... | collective-permute-start | bytes 3538952 | tf_op jit(solution)/shard_map/ppermute | solution.py:362
  151.9 27.6 %collective-permute-start.9 = (bf16[192,3072]{1,0:T(8,128)(2,1)S(1)}, bf16[192,3072]{1,0:T(8,128)(2,1)}, u32[]{:S(2)}, u32[]{:S(2)}) collective-permute-start(bf16[192,3072]{1,0:T(8,128)(2,1)S(1)} %bitcast.50), channel_id=1, source_target_pairs={{0,48},{1,49},{2,50},{3,51},{4,52},{5,53},{6,54},{7,55},{8,56},{9,... | collective-permute-start | bytes 3538952 | tf_op jit(solution)/shard_map/ppermute | solution.py:362
  179.5 31.0 %copy-start.4 = (bf16[192,3072]{1,0:T(8,128)(2,1)}, bf16[192,3072]{1,0:T(8,128)(2,1)S(1)}, u32[]{:S(2)}) copy-start(bf16[192,3072]{1,0:T(8,128)(2,1)S(1)} %collective-permute-done.7.refs_1_) | copy-start | bytes 3538948
  179.5 31.0 %copy-start.5 = (bf16[192,3072]{1,0:T(8,128)(2,1)}, bf16[192,3072]{1,0:T(8,128)(2,1)S(1)}, u32[]{:S(2)}) copy-start(bf16[192,3072]{1,0:T(8,128)(2,1)S(1)} %collective-permute-done.8.refs_2_) | copy-start | bytes 3538948
  179.5 31.0 %collective-permute-start.10 = (bf16[192,3072]{1,0:T(8,128)(2,1)S(1)}, bf16[192,3072]{1,0:T(8,128)(2,1)S(1)}, u32[]{:S(2)}, u32[]{:S(2)}) collective-permute-start(bf16[192,3072]{1,0:T(8,128)(2,1)S(1)} %collective-permute-done.7.refs_1_), channel_id=1, source_target_pairs={{0,16},{1,17},{2,18},{3,19},{4,20},{5,21},{6,22},{7,23},{8,24},{9,... | collective-permute-start | bytes 3538952 | tf_op jit(solution)/shard_map/ppermute | solution.py:362
  179.6 30.9 %collective-permute-start.11 = (bf16[192,3072]{1,0:T(8,128)(2,1)S(1)}, bf16[192,3072]{1,0:T(8,128)(2,1)}, u32[]{:S(2)}, u32[]{:S(2)}) collective-permute-start(bf16[192,3072]{1,0:T(8,128)(2,1)S(1)} %collective-permute-done.7.refs_1_), channel_id=1, source_target_pairs={{0,48},{1,49},{2,50},{3,51},{4,52},{5,53},{6,54},{7,55},{8,56},{9,... | collective-permute-start | bytes 3538952 | tf_op jit(solution)/shard_map/ppermute | solution.py:362
  211.5 48.4 %all-to-all-start.4 = ((bf16[64,96,128]{2,1,0:T(8,128)(2,1)}), bf16[64,96,128]{2,1,0:T(8,128)(2,1)S(1)}, u32[]{:S(2)}, u32[]{:S(2)}) async-start(bf16[64,96,128]{2,1,0:T(8,128)(2,1)} %shard_map.97), calls=%async_computation.4 | async-start | bytes 3145728 | tf_op jit(solution)/shard_map/all_to_all | solution.py:354
  216.3 42.5 %collective-permute-start.12 = (bf16[192,3072]{1,0:T(8,128)(2,1)S(1)}, bf16[192,3072]{1,0:T(8,128)(2,1)S(1)}, u32[]{:S(2)}, u32[]{:S(2)}) collective-permute-start(bf16[192,3072]{1,0:T(8,128)(2,1)S(1)} %copy-done.6), channel_id=1, source_target_pairs={{0,16},{1,17},{2,18},{3,19},{4,20},{5,21},{6,22},{7,23},{8,24},{9,... | collective-permute-start | bytes 3538952 | tf_op jit(solution)/shard_map/ppermute | solution.py:362
  217.4 42.5 %collective-permute-start.13 = (bf16[192,3072]{1,0:T(8,128)(2,1)}, bf16[192,3072]{1,0:T(8,128)(2,1)}, u32[]{:S(2)}, u32[]{:S(2)}) collective-permute-start(bf16[192,3072]{1,0:T(8,128)(2,1)} %collective-permute-done.11.refs_5_), channel_id=1, source_target_pairs={{0,48},{1,49},{2,50},{3,51},{4,52},{5,53},{6,54},{7,55},{8,56},{9,... | collective-permute-start | bytes 3538952 | tf_op jit(solution)/shard_map/ppermute | solution.py:362
  270.9 16.0 %collective-permute-start.14 = (bf16[4,64,1536]{2,1,0:T(8,128)(2,1)}, bf16[4,64,1536]{2,1,0:T(8,128)(2,1)S(1)}, u32[]{:S(2)}, u32[]{:S(2)}) collective-permute-start(bf16[4,64,1536]{2,1,0:T(8,128)(2,1)} %shard_map.98), channel_id=1, source_target_pairs={{0,192},{64,0},{128,64},{192,128},{1,193},{65,1},{129,65},{193,129... | collective-permute-start | bytes 2359304 | tf_op jit(solution)/shard_map/ppermute | solution.py:427
  (12 other events, 79.9 us)

commit v5 on v4

--- a/solution.py
+++ b/solution.py
@@ -50,9 +50,10 @@
     return pairs
 
 
-def pack_kernel(q_ref, k_ref, v_ref, out_ref):
-    half = q_ref.shape[0] // 2
-    for n, ref in enumerate((q_ref, k_ref, v_ref)):
+def pack_kernel(*refs):
+    out_ref = refs[-1]
+    half = refs[0].shape[0] // 2
+    for n, ref in enumerate(refs[:-1]):
         for pair in range(ref.shape[1] // 128):
             tile = ref[:, pair * 128 : (pair + 1) * 128]
             first, second = halves(tile[:half], tile[half:])
@@ -60,17 +61,17 @@
             out_ref[2 * pair + 1, n * half : (n + 1) * half, :] = second
 
 
-def pack_items(q, k, v):
-    frames, lanes = q.shape
-    out = jax.ShapeDtypeStruct((lanes // HS, 3 * frames // 2, 128), BF16)
+def pack_items(*arrays):
+    frames, lanes = arrays[0].shape
+    count = len(arrays)
     return pl.pallas_call(
         pack_kernel,
-        out_shape=out,
-        in_specs=[WHOLE] * 3,
+        out_shape=jax.ShapeDtypeStruct((lanes // HS, count * frames // 2, 128), BF16),
+        in_specs=[WHOLE] * count,
         out_specs=WHOLE,
         compiler_params=pltpu.CompilerParams(vmem_limit_bytes=16 * MIB),
-        cost_estimate=cost(0, 3 * MIB),
-    )(q, k, v)
+        cost_estimate=cost(0, count * MIB),
+    )(*arrays)
 
 
 def project_kernel(owner_ref, grad_ref, *refs):
@@ -215,7 +216,7 @@
 
     def first(half, side, j, centre):
         at = pl.ds(pl.multiple_of(half * rows + j * KB, KB), KB)
-        values = r_ref[pl.ds(j * per, per), 64:96, :].reshape(KB, 128)
+        values = r_ref[pl.ds(j * per, per), :, :].reshape(KB, 128)
         dp = lax.dot_general(values, side, PLAIN_DOT, preferred_element_type=F32)
         dp_ref[at, :] = dp
         return centre + fold(w_ref[0, at, :] * inverse * dp, jnp.sum)
@@ -395,33 +396,34 @@
     copies = jnp.broadcast_to(out_weight, (Z,) + out_weight.shape[1:])
     out_group = exchange(copies, z_groups).reshape(-1, width)
     flat = lambda array: array[0].reshape(frames, records * features)
-    packed = pack_items(flat(queries), flat(key_states), flat(value_states))
+    packed = pack_items(flat(queries), flat(key_states))
+    packed_values = pack_items(flat(value_states))
     received = exchange(after(packed, out_group))
+    near = nearby(out_group)
+    received_values = exchange(after(packed_values, received, *near))
     grads = out_grad[0].transpose(1, 0, 2)
     inputs = layer_input[0].transpose(1, 0, 2)
-    near = nearby(out_group)
     far = further(near)
     out_pieces = [out_group] + near + far + [across(far[2], 0, 1)]
-    attn_grad = project(places, grads.reshape(records * frames, width), out_pieces)
-    received_grads = exchange(after(attn_grad, received))
 
     record = seq // HEADS
     valid = jnp.sum(jnp.where(jnp.arange(records) == record, lengths[0], 0)).reshape(1)
     keys, queries_t, keys_t = prepare(valid, received)
-    weights_0, sums_0 = softmax_weights(0, valid, keys, queries_t)
+    weights_0, sums_0 = softmax_weights(0, after(valid, *near), keys, queries_t)
+    attn_grad = project(after(places, sums_0), grads.reshape(records * frames, width), out_pieces)
+    received_grads = exchange(after(attn_grad, received_values))
+    weights_1, sums_1 = softmax_weights(1, after(valid, attn_grad), keys, queries_t)
     copies = jnp.broadcast_to(qkv_weight, (Z,) + qkv_weight.shape[1:])
-    qkv_group = exchange(after(copies, received_grads, sums_0), z_groups).reshape(-1, qkv_weight.shape[2])
-    weights_1, sums_1 = softmax_weights(1, after(valid, received_grads, sums_0), keys, queries_t)
-    rest = (queries_t, keys_t, received, received_grads)
-    begun = attention_grads(0, weights_0, after(sums_0, qkv_group, sums_1), *rest)
+    qkv_group = exchange(after(copies, received_grads, sums_1), z_groups).reshape(-1, qkv_weight.shape[2])
+    rest = (queries_t, keys_t, received_values, received_grads)
+    begun = attention_grads(0, weights_0, after(sums_0, sums_1), *rest)
     near = nearby(qkv_group)
-    sums_1, *near = lax.optimization_barrier((sums_1, *near))
-    gradients = attention_grads(1, weights_1, sums_1, *rest, begun)
+    gradients = attention_grads(1, weights_1, after(sums_1, qkv_group), *rest, begun)
+    gradients, *near = lax.optimization_barrier((gradients, *near))
+    back = exchange(gradients)
     partner, below, above = near
-    diagonal = [across(partner, 1, 0), across(partner, 3, 0)]
-    gradients, *diagonal = lax.optimization_barrier((gradients, *diagonal))
-    back = exchange(gradients)
-    far = [across(after(below, gradients), 1, 0), across(diagonal[1], 3, 0)]
+    diagonal = [across(below, 0, 1), across(partner, 3, 0)]
+    far = [across(below, 1, 0), across(diagonal[1], 3, 0)]
     result = finish(places, [qkv_group] + near + diagonal + far, back, inputs, grads, norm_gain)
     count = lax.axis_size("section")
     moved = lax.ppermute(result, "section", [(i, (i - 1) % count) for i in range(count)])

time: 289 us -> 302 us (1.045)
  starting transfers between devices: 56.3 us -> 70 us
    all_to_all x5 -> x6, starting transfers between devices: 35.6 us -> 45.7 us  [exchange(): lax.all_to_all(items, 'seq', split_axis=0, concat_axis=0, tiled=True, axi...]
    all_to_all x5 -> x6, waiting for transfers between devices: 24.8 us -> 23.3 us  [exchange(): lax.all_to_all(items, 'seq', split_axis=0, concat_axis=0, tiled=True, axi...]
    unnamed x37 -> x39, local copies, waits for them, and re-layouts: 6.66 us -> 7.4 us
  transfers between devices with their start and end apart: 20 -> 21, of which waited for: 7 -> 10; matrix products, arithmetic and copies ran while one was open for 1% -> 1% of each run, Pallas kernels for 34% -> 32%
where the time goes in v5:
time: 302 us
  waiting for transfers between devices  113 us (37%)
  Pallas kernels  106 us (35%)
  starting transfers between devices  70 us (23%)
  local copies, waits for them, and re-layouts  11.8 us (4%)
    ppermute x14, waiting for transfers between devices, across(): return lax.ppermute(rows, 'seq', seq_pairs(dy, dx, 0))  77.2 us
    pallas_call x2, Pallas kernels, attention_grads(): pl.pallas_call(functools.partial(grads_kernel, part), grid=(blocks,), out...  53.7 us
    all_to_all x6, starting transfers between devices, exchange(): lax.all_to_all(items, 'seq', split_axis=0, concat_axis=0, tiled=True, axi...  45.7 us
    pallas_call x2, Pallas kernels, softmax_weights(): pl.pallas_call(weights_kernel, grid=(blocks,), out_shape=[jax.ShapeDtypeS...  32.5 us
    all_to_all x6, waiting for transfers between devices, exchange(): lax.all_to_all(items, 'seq', split_axis=0, concat_axis=0, tiled=True, axi...  23.3 us
    ppermute x14, starting transfers between devices, across(): return lax.ppermute(rows, 'seq', seq_pairs(dy, dx, 0))  19.9 us
    ppermute x1, waiting for transfers between devices, on_device(): lax.ppermute(result, 'section', [(i, (i - 1) % count) for i in range(coun...  12.2 us
    pallas_call x1, Pallas kernels, finish(): pl.pallas_call(finish_kernel, grid=(1,), out_shape=jax.ShapeDtypeStruct(i...  9.93 us
  transfers between devices with their start and end apart: 21, of which 10 were waited for; matrix products, arithmetic and copies ran while one was open for 1% of the time, Pallas kernels for 32%

profile of v5, /device:TPU:1, one launch (start us, length us, event | category | flops | bytes accessed | tf_op | source)
XLA Modules:
  0.0 301.5 jit_solution(10916690130001714541)
XLA Ops:
  1.7 9.0 %all-to-all-start = ((bf16[8,16,1536]{2,1,0:T(8,128)(2,1)}), bf16[8,16,1536]{2,1,0:T(8,128)(2,1)S(1)}, u32[]{:S(2)}, u32[]{:S(2)}) async-start(bf16[8,16,1536]{2,1,0:T(8,128)(2,1)} %broadcast_in_dim.23), calls=%async_computation | async-start | bytes 786432 | tf_op jit(solution)/shard_map/all_to_all | solution.py:355
  12.4 12.5 %all-to-all-done = bf16[8,16,1536]{2,1,0:T(8,128)(2,1)S(1)} async-done(((bf16[8,16,1536]{2,1,0:T(8,128)(2,1)}), bf16[8,16,1536]{2,1,0:T(8,128)(2,1)S(1)}, u32[]{:S(2)}, u32[]{:S(2)}) %all-to-all-start) | async-done | bytes 393248 | tf_op jit(solution)/shard_map/all_to_all | solution.py:355
  24.9 6.1 %all-to-all-start.1 = ((bf16[64,64,128]{2,1,0:T(8,128)(2,1)}), bf16[64,64,128]{2,1,0:T(8,128)(2,1)S(1)}, u32[]{:S(2)}, u32[]{:S(2)}) async-start(bf16[64,64,128]{2,1,0:T(8,128)(2,1)} %shard_map.91), calls=%async_computation.1 | async-start | bytes 2097152 | tf_op jit(solution)/shard_map/all_to_all | solution.py:355
  36.0 9.3 %collective-permute-done.refs_1_ = bf16[128,1536]{1,0:T(8,128)(2,1)S(1)} collective-permute-done((bf16[128,1536]{1,0:T(8,128)(2,1)S(1)}, bf16[128,1536]{1,0:T(8,128)(2,1)S(1)}, u32[]{:S(2)}, u32[]{:S(2)}) %collective-permute-start) | collective-permute-done | bytes 393248 | tf_op jit(solution)/shard_map/ppermute | solution.py:363
  48.4 8.1 %all-to-all-done.1.r_ref = bf16[64,64,128]{2,1,0:T(8,128)(2,1)S(1)} async-done(((bf16[64,64,128]{2,1,0:T(8,128)(2,1)}), bf16[64,64,128]{2,1,0:T(8,128)(2,1)S(1)}, u32[]{:S(2)}, u32[]{:S(2)}) %all-to-all-start.1) | async-done | bytes 1048608 | tf_op jit(solution)/shard_map/all_to_all | solution.py:355
  57.5 8.2 %all-to-all-start.2 = ((bf16[64,32,128]{2,1,0:T(8,128)(2,1)}), bf16[64,32,128]{2,1,0:T(8,128)(2,1)}, u32[]{:S(2)}, u32[]{:S(2)}) async-start(bf16[64,32,128]{2,1,0:T(8,128)(2,1)} %shard_map.96), calls=%async_computation.2 | async-start | bytes 1048576 | tf_op jit(solution)/shard_map/all_to_all | solution.py:355
  71.5 8.9 %collective-permute-done.5.refs_6_ = bf16[128,1536]{1,0:T(8,128)(2,1)S(1)} collective-permute-done((bf16[128,1536]{1,0:T(8,128)(2,1)S(1)}, bf16[128,1536]{1,0:T(8,128)(2,1)S(1)}, u32[]{:S(2)}, u32[]{:S(2)}) %collective-permute-start.5) | collective-permute-done | bytes 393248 | tf_op jit(solution)/shard_map/ppermute | solution.py:363
  81.8 4.3 %shard_map.92 = (bf16[4096,128]{1,0:T(8,128)(2,1)}, bf16[128,4096]{1,0:T(8,128)(2,1)}, bf16[64,4096]{1,0:T(8,128)(2,1)}) custom-call(s32[1]{0:T(128)} %bitcast.9.length_ref.gate_ref, bf16[64,64,128]{2,1,0:T(8,128)(2,1)} %copy-done.4), custom_call_target="tpu_custom_call" | custom-call | bytes 4194304 | tf_op jit(solution)/shard_map/pallas_call | solution.py:137
  86.1 16.3 %shard_map.93 = (f32[8,4096,256]{2,1,0:T(8,128)}, f32[1,2048]{1,0:T(1,128)}) custom-call(s32[1]{0:T(128)} %bitcast.9.length_ref.gate_ref, bf16[4096,128]{1,0:T(8,128)(2,1)} %get-tuple-element.29.kz_ref, bf16[128,4096]{1,0:T(8,128)(2,1)} %get-tuple-element.30.qt_ref), custom_call_target="tpu_custom_call" | custom-call | flops 4294967296 | bytes 33554432 | tf_op jit(solution)/shard_map/pallas_call | solution.py:174
  102.4 3.2 %shard_map.94 = bf16[64,32,128]{2,1,0:T(8,128)(2,1)} custom-call(s32[8]{0:T(128)S(1)} %stack.35.owner_ref, bf16[256,1536]{1,0:T(8,128)(2,1)S(1)} %bitcast.39, bf16[128,1536]{1,0:T(8,128)(2,1)S(1)} %bitcast.47, bf16[128,1536]{1,0:T(8,128)(2,1)S(1)} %collective-permute-done.refs_1_, bf16[128,1536]{1,0:T(8,128)(2,1)S(1)} %collective-permute-done.1.refs_2_, ...), custom_call_target="tpu_custom_call" | custom-call | flops 805306368 | bytes 4456448 | tf_op jit(solution)/shard_map/pallas_call | solution.py:93
  105.6 9.5 %all-to-all-start.3 = ((bf16[64,32,128]{2,1,0:T(8,128)(2,1)}), bf16[64,32,128]{2,1,0:T(8,128)(2,1)S(1)}, u32[]{:S(2)}, u32[]{:S(2)}) async-start(bf16[64,32,128]{2,1,0:T(8,128)(2,1)} %shard_map.94), calls=%async_computation.3 | async-start | bytes 1048576 | tf_op jit(solution)/shard_map/all_to_all | solution.py:355
  115.1 16.2 %shard_map.95 = (f32[8,4096,256]{2,1,0:T(8,128)}, f32[1,2048]{1,0:T(1,128)}) custom-call(s32[1]{0:T(128)} %bitcast.9.length_ref.gate_ref, bf16[4096,128]{1,0:T(8,128)(2,1)} %get-tuple-element.29.kz_ref, bf16[128,4096]{1,0:T(8,128)(2,1)} %get-tuple-element.30.qt_ref), custom_call_target="tpu_custom_call" | custom-call | flops 4294967296 | bytes 33554432 | tf_op jit(solution)/shard_map/pallas_call | solution.py:174
  132.5 6.2 %all-to-all-start.4 = ((bf16[8,24,3072]{2,1,0:T(8,128)(2,1)}), bf16[8,24,3072]{2,1,0:T(8,128)(2,1)S(1)}, u32[]{:S(2)}, u32[]{:S(2)}) async-start(bf16[8,24,3072]{2,1,0:T(8,128)(2,1)} %broadcast_in_dim.25), calls=%async_computation.4 | async-start | bytes 2359296 | tf_op jit(solution)/shard_map/all_to_all | solution.py:355
  138.7 25.8 %shard_map.97 = (f32[64,2048]{1,0:T(8,128)}, f32[4096,128]{1,0:T(8,128)}) custom-call(f32[8,4096,256]{2,1,0:T(8,128)} %get-tuple-element.41.w_ref, f32[1,2048]{1,0:T(1,128)} %get-tuple-element.42.l_ref, bf16[128,4096]{1,0:T(8,128)(2,1)} %get-tuple-element.30.qt_ref, bf16[64,4096]{1,0:T(8,128)(2,1)} %get-tuple-element.40.kt_ref, ...), custom_call_target="tpu_custom_call" | custom-call | flops 17179869184 | bytes 33554432 | tf_op jit(solution)/shard_map/pallas_call | solution.py:269
  164.6 2.7 all-to-all-done.4
  171.1 27.9 %shard_map.98 = bf16[64,96,128]{2,1,0:T(8,128)(2,1)} custom-call(f32[8,4096,256]{2,1,0:T(8,128)} %get-tuple-element.34.w_ref, f32[1,2048]{1,0:T(1,128)} %get-tuple-element.39.l_ref, bf16[128,4096]{1,0:T(8,128)(2,1)} %get-tuple-element.30.qt_ref, bf16[64,4096]{1,0:T(8,128)(2,1)} %get-tuple-element.40.kt_ref, bf16[64,32,128]{2,1,0:T(8,128)(2,1)} %all-to-all-done.2.r_ref, ...), custom_call_target="tpu_custom_call" | custom-call | flops 17179869184 | bytes 33554432 | tf_op jit(solution)/shard_map/pallas_call | solution.py:269
  199.1 6.6 %all-to-all-start.5 = ((bf16[64,96,128]{2,1,0:T(8,128)(2,1)}), bf16[64,96,128]{2,1,0:T(8,128)(2,1)S(1)}, u32[]{:S(2)}, u32[]{:S(2)}) async-start(bf16[64,96,128]{2,1,0:T(8,128)(2,1)} %shard_map.98), calls=%async_computation.5 | async-start | bytes 3145728 | tf_op jit(solution)/shard_map/all_to_all | solution.py:355
  205.7 2.7 collective-permute-start.11
  209.6 37.2 %collective-permute-done.11.refs_5_ = bf16[192,3072]{1,0:T(8,128)(2,1)S(1)} collective-permute-done((bf16[192,3072]{1,0:T(8,128)(2,1)S(1)}, bf16[192,3072]{1,0:T(8,128)(2,1)S(1)}, u32[]{:S(2)}, u32[]{:S(2)}) %collective-permute-start.11) | collective-permute-done | bytes 1179680 | tf_op jit(solution)/shard_map/ppermute | solution.py:363
  246.9 3.2 %collective-permute-start.13 = (bf16[192,3072]{1,0:T(8,128)(2,1)S(1)}, bf16[192,3072]{1,0:T(8,128)(2,1)S(1)}, u32[]{:S(2)}, u32[]{:S(2)}) collective-permute-start(bf16[192,3072]{1,0:T(8,128)(2,1)S(1)} %collective-permute-done.11.refs_5_), channel_id=1, source_target_pairs={{0,48},{1,49},{2,50},{3,51},{4,52},{5,53},{6,54},{7,55},{8,56},{9,... | collective-permute-start | bytes 3538952 | tf_op jit(solution)/shard_map/ppermute | solution.py:363
  253.1 18.7 %collective-permute-done.13.refs_7_ = bf16[192,3072]{1,0:T(8,128)(2,1)S(1)} collective-permute-done((bf16[192,3072]{1,0:T(8,128)(2,1)S(1)}, bf16[192,3072]{1,0:T(8,128)(2,1)S(1)}, u32[]{:S(2)}, u32[]{:S(2)}) %collective-permute-start.13) | collective-permute-done | bytes 1179680 | tf_op jit(solution)/shard_map/ppermute | solution.py:363
  273.4 9.9 %shard_map.99 = bf16[4,64,1536]{2,1,0:T(8,128)(2,1)} custom-call(s32[8]{0:T(128)} %copy-done.1, bf16[64,96,128]{2,1,0:T(8,128)(2,1)} %copy-done.2, bf16[4,64,1536]{2,1,0:T(8,128)(2,1)} %bitcast.52, bf16[4,64,1536]{2,1,0:T(8,128)(2,1)} %bitcast.40, f32[1,1536]{1,0:T(1,128)} %gain_ref.1, bf16[192,3072]{1,0:T(8,128)(2,1)} %bitcast.51, ...), custom_call_target="tpu_custom_call" | custom-call | flops 2415919104 | bytes 9437184 | tf_op jit(solution)/shard_map/pallas_call | solution.py:335
  283.3 4.5 %collective-permute-start.14 = (bf16[4,64,1536]{2,1,0:T(8,128)(2,1)}, bf16[4,64,1536]{2,1,0:T(8,128)(2,1)S(1)}, u32[]{:S(2)}, u32[]{:S(2)}) collective-permute-start(bf16[4,64,1536]{2,1,0:T(8,128)(2,1)} %shard_map.99), channel_id=1, source_target_pairs={{0,192},{64,0},{128,64},{192,128},{1,193},{65,1},{129,65},{193,129... | collective-permute-start | bytes 2359304 | tf_op jit(solution)/shard_map/ppermute | solution.py:429
  287.8 12.2 %collective-permute-done.14 = bf16[4,64,1536]{2,1,0:T(8,128)(2,1)S(1)} collective-permute-done((bf16[4,64,1536]{2,1,0:T(8,128)(2,1)}, bf16[4,64,1536]{2,1,0:T(8,128)(2,1)S(1)}, u32[]{:S(2)}, u32[]{:S(2)}) %collective-permute-start.14) | collective-permute-done | bytes 786464 | tf_op jit(solution)/shard_map/ppermute | solution.py:429
  (71 shorter events, 32.0 us)
Async XLA Ops:
  1.7 23.2 %all-to-all-start = ((bf16[8,16,1536]{2,1,0:T(8,128)(2,1)}), bf16[8,16,1536]{2,1,0:T(8,128)(2,1)S(1)}, u32[]{:S(2)}, u32[]{:S(2)}) async-start(bf16[8,16,1536]{2,1,0:T(8,128)(2,1)} %broadcast_in_dim.23), calls=%async_computation | async-start | bytes 786432 | tf_op jit(solution)/shard_map/all_to_all | solution.py:355
  24.9 31.6 %all-to-all-start.1 = ((bf16[64,64,128]{2,1,0:T(8,128)(2,1)}), bf16[64,64,128]{2,1,0:T(8,128)(2,1)S(1)}, u32[]{:S(2)}, u32[]{:S(2)}) async-start(bf16[64,64,128]{2,1,0:T(8,128)(2,1)} %shard_map.91), calls=%async_computation.1 | async-start | bytes 2097152 | tf_op jit(solution)/shard_map/all_to_all | solution.py:355
  31.0 14.2 %collective-permute-start = (bf16[128,1536]{1,0:T(8,128)(2,1)S(1)}, bf16[128,1536]{1,0:T(8,128)(2,1)S(1)}, u32[]{:S(2)}, u32[]{:S(2)}) collective-permute-start(bf16[128,1536]{1,0:T(8,128)(2,1)S(1)} %bitcast.44), channel_id=1, source_target_pairs={{0,8},{1,9},{2,10},{3,11},{4,12},{5,13},{6,14},{7,15},{8,0},{9,1},... | collective-permute-start | bytes 1179656 | tf_op jit(solution)/shard_map/ppermute | solution.py:363
  32.1 15.5 %collective-permute-start.1 = (bf16[128,1536]{1,0:T(8,128)(2,1)S(1)}, bf16[128,1536]{1,0:T(8,128)(2,1)S(1)}, u32[]{:S(2)}, u32[]{:S(2)}) collective-permute-start(bf16[128,1536]{1,0:T(8,128)(2,1)S(1)} %bitcast.45), channel_id=1, source_target_pairs={{0,16},{1,17},{2,18},{3,19},{4,20},{5,21},{6,22},{7,23},{8,24},{9,... | collective-permute-start | bytes 1179656 | tf_op jit(solution)/shard_map/ppermute | solution.py:363
  33.3 15.0 %collective-permute-start.2 = (bf16[128,1536]{1,0:T(8,128)(2,1)S(1)}, bf16[128,1536]{1,0:T(8,128)(2,1)S(1)}, u32[]{:S(2)}, u32[]{:S(2)}) collective-permute-start(bf16[128,1536]{1,0:T(8,128)(2,1)S(1)} %bitcast.46), channel_id=1, source_target_pairs={{0,48},{1,49},{2,50},{3,51},{4,52},{5,53},{6,54},{7,55},{8,56},{9,... | collective-permute-start | bytes 1179656 | tf_op jit(solution)/shard_map/ppermute | solution.py:363
  57.5 48.1 %all-to-all-start.2 = ((bf16[64,32,128]{2,1,0:T(8,128)(2,1)}), bf16[64,32,128]{2,1,0:T(8,128)(2,1)}, u32[]{:S(2)}, u32[]{:S(2)}) async-start(bf16[64,32,128]{2,1,0:T(8,128)(2,1)} %shard_map.96), calls=%async_computation.2 | async-start | bytes 1048576 | tf_op jit(solution)/shard_map/all_to_all | solution.py:355
  65.7 14.6 %collective-permute-start.5 = (bf16[128,1536]{1,0:T(8,128)(2,1)S(1)}, bf16[128,1536]{1,0:T(8,128)(2,1)S(1)}, u32[]{:S(2)}, u32[]{:S(2)}) collective-permute-start(bf16[128,1536]{1,0:T(8,128)(2,1)S(1)} %collective-permute-done.1.refs_2_), channel_id=1, source_target_pairs={{0,16},{1,17},{2,18},{3,19},{4,20},{5,21},{6,22},{7,23},{8,24},{9,... | collective-permute-start | bytes 1179656 | tf_op jit(solution)/shard_map/ppermute | solution.py:363
  68.0 34.3 %copy-start = (bf16[1,64,4,1536]{3,1,2,0:T(8,128)(2,1)}, bf16[1,64,4,1536]{3,1,2,0:T(8,128)(2,1)S(1)}, u32[]{:S(2)}) copy-start(bf16[1,64,4,1536]{3,1,2,0:T(8,128)(2,1)S(1)} %copy.20) | copy-start | bytes 2359300
  68.1 34.3 %copy-start.1 = (s32[8]{0:T(128)}, s32[8]{0:T(128)S(1)}, u32[]{:S(2)}) copy-start(s32[8]{0:T(128)S(1)} %stack.35.owner_ref) | copy-start | bytes 100
  68.8 33.5 %collective-permute-start.3 = (bf16[128,1536]{1,0:T(8,128)(2,1)S(1)}, bf16[128,1536]{1,0:T(8,128)(2,1)S(1)}, u32[]{:S(2)}, u32[]{:S(2)}) collective-permute-start(bf16[128,1536]{1,0:T(8,128)(2,1)S(1)} %collective-permute-done.refs_1_), channel_id=1, source_target_pairs={{0,16},{1,17},{2,18},{3,19},{4,20},{5,21},{6,22},{7,23},{8,24},{9,... | collective-permute-start | bytes 1179656 | tf_op jit(solution)/shard_map/ppermute | solution.py:363
  70.1 32.2 %collective-permute-start.4 = (bf16[128,1536]{1,0:T(8,128)(2,1)S(1)}, bf16[128,1536]{1,0:T(8,128)(2,1)S(1)}, u32[]{:S(2)}, u32[]{:S(2)}) collective-permute-start(bf16[128,1536]{1,0:T(8,128)(2,1)S(1)} %collective-permute-done.refs_1_), channel_id=1, source_target_pairs={{0,48},{1,49},{2,50},{3,51},{4,52},{5,53},{6,54},{7,55},{8,56},{9,... | collective-permute-start | bytes 1179656 | tf_op jit(solution)/shard_map/ppermute | solution.py:363
  80.4 22.0 %collective-permute-start.6 = (bf16[128,1536]{1,0:T(8,128)(2,1)S(1)}, bf16[128,1536]{1,0:T(8,128)(2,1)S(1)}, u32[]{:S(2)}, u32[]{:S(2)}) collective-permute-start(bf16[128,1536]{1,0:T(8,128)(2,1)S(1)} %collective-permute-done.5.refs_6_), channel_id=1, source_target_pairs={{0,8},{1,9},{2,10},{3,11},{4,12},{5,13},{6,14},{7,15},{8,0},{9,1},... | collective-permute-start | bytes 1179656 | tf_op jit(solution)/shard_map/ppermute | solution.py:363
  105.6 25.7 %all-to-all-start.3 = ((bf16[64,32,128]{2,1,0:T(8,128)(2,1)}), bf16[64,32,128]{2,1,0:T(8,128)(2,1)S(1)}, u32[]{:S(2)}, u32[]{:S(2)}) async-start(bf16[64,32,128]{2,1,0:T(8,128)(2,1)} %shard_map.94), calls=%async_computation.3 | async-start | bytes 1048576 | tf_op jit(solution)/shard_map/all_to_all | solution.py:355
  132.5 34.7 %all-to-all-start.4 = ((bf16[8,24,3072]{2,1,0:T(8,128)(2,1)}), bf16[8,24,3072]{2,1,0:T(8,128)(2,1)S(1)}, u32[]{:S(2)}, u32[]{:S(2)}) async-start(bf16[8,24,3072]{2,1,0:T(8,128)(2,1)} %broadcast_in_dim.25), calls=%async_computation.4 | async-start | bytes 2359296 | tf_op jit(solution)/shard_map/all_to_all | solution.py:355
  167.2 31.8 %collective-permute-start.7 = (bf16[192,3072]{1,0:T(8,128)(2,1)S(1)}, bf16[192,3072]{1,0:T(8,128)(2,1)S(1)}, u32[]{:S(2)}, u32[]{:S(2)}) collective-permute-start(bf16[192,3072]{1,0:T(8,128)(2,1)S(1)} %bitcast.48), channel_id=1, source_target_pairs={{0,8},{1,9},{2,10},{3,11},{4,12},{5,13},{6,14},{7,15},{8,0},{9,1},... | collective-permute-start | bytes 3538952 | tf_op jit(solution)/shard_map/ppermute | solution.py:363
  168.4 30.6 %collective-permute-start.8 = (bf16[192,3072]{1,0:T(8,128)(2,1)S(1)}, bf16[192,3072]{1,0:T(8,128)(2,1)}, u32[]{:S(2)}, u32[]{:S(2)}) collective-permute-start(bf16[192,3072]{1,0:T(8,128)(2,1)S(1)} %bitcast.49), channel_id=1, source_target_pairs={{0,16},{1,17},{2,18},{3,19},{4,20},{5,21},{6,22},{7,23},{8,24},{9,... | collective-permute-start | bytes 3538952 | tf_op jit(solution)/shard_map/ppermute | solution.py:363
  169.7 29.4 %collective-permute-start.9 = (bf16[192,3072]{1,0:T(8,128)(2,1)S(1)}, bf16[192,3072]{1,0:T(8,128)(2,1)}, u32[]{:S(2)}, u32[]{:S(2)}) collective-permute-start(bf16[192,3072]{1,0:T(8,128)(2,1)S(1)} %bitcast.50), channel_id=1, source_target_pairs={{0,48},{1,49},{2,50},{3,51},{4,52},{5,53},{6,54},{7,55},{8,56},{9,... | collective-permute-start | bytes 3538952 | tf_op jit(solution)/shard_map/ppermute | solution.py:363
  199.0 51.0 %copy-start.10 = (bf16[1,64,4,1536]{3,2,1,0:T(4,128)(2,1)S(1)}, bf16[1,64,4,1536]{3,2,1,0:T(4,128)(2,1)}, u32[]{:S(2)}) copy-start(bf16[1,64,4,1536]{3,2,1,0:T(4,128)(2,1)} %param.9) | copy-start | bytes 2359300
  199.1 72.8 %all-to-all-start.5 = ((bf16[64,96,128]{2,1,0:T(8,128)(2,1)}), bf16[64,96,128]{2,1,0:T(8,128)(2,1)S(1)}, u32[]{:S(2)}, u32[]{:S(2)}) async-start(bf16[64,96,128]{2,1,0:T(8,128)(2,1)} %shard_map.98), calls=%async_computation.5 | async-start | bytes 3145728 | tf_op jit(solution)/shard_map/all_to_all | solution.py:355
  205.7 41.2 %collective-permute-start.11 = (bf16[192,3072]{1,0:T(8,128)(2,1)S(1)}, bf16[192,3072]{1,0:T(8,128)(2,1)S(1)}, u32[]{:S(2)}, u32[]{:S(2)}) collective-permute-start(bf16[192,3072]{1,0:T(8,128)(2,1)S(1)} %collective-permute-done.7.refs_1_), channel_id=1, source_target_pairs={{0,48},{1,49},{2,50},{3,51},{4,52},{5,53},{6,54},{7,55},{8,56},{9,... | collective-permute-start | bytes 3538952 | tf_op jit(solution)/shard_map/ppermute | solution.py:363
  208.4 42.7 %collective-permute-start.10 = (bf16[192,3072]{1,0:T(8,128)(2,1)}, bf16[192,3072]{1,0:T(8,128)(2,1)S(1)}, u32[]{:S(2)}, u32[]{:S(2)}) collective-permute-start(bf16[192,3072]{1,0:T(8,128)(2,1)} %collective-permute-done.8.refs_2_), channel_id=1, source_target_pairs={{0,8},{1,9},{2,10},{3,11},{4,12},{5,13},{6,14},{7,15},{8,0},{9,1},... | collective-permute-start | bytes 3538952 | tf_op jit(solution)/shard_map/ppermute | solution.py:363
  209.6 41.4 %collective-permute-start.12 = (bf16[192,3072]{1,0:T(8,128)(2,1)}, bf16[192,3072]{1,0:T(8,128)(2,1)S(1)}, u32[]{:S(2)}, u32[]{:S(2)}) collective-permute-start(bf16[192,3072]{1,0:T(8,128)(2,1)} %collective-permute-done.8.refs_2_), channel_id=1, source_target_pairs={{0,16},{1,17},{2,18},{3,19},{4,20},{5,21},{6,22},{7,23},{8,24},{9,... | collective-permute-start | bytes 3538952 | tf_op jit(solution)/shard_map/ppermute | solution.py:363
  246.9 24.9 %collective-permute-start.13 = (bf16[192,3072]{1,0:T(8,128)(2,1)S(1)}, bf16[192,3072]{1,0:T(8,128)(2,1)S(1)}, u32[]{:S(2)}, u32[]{:S(2)}) collective-permute-start(bf16[192,3072]{1,0:T(8,128)(2,1)S(1)} %collective-permute-done.11.refs_5_), channel_id=1, source_target_pairs={{0,48},{1,49},{2,50},{3,51},{4,52},{5,53},{6,54},{7,55},{8,56},{9,... | collective-permute-start | bytes 3538952 | tf_op jit(solution)/shard_map/ppermute | solution.py:363
  283.3 16.7 %collective-permute-start.14 = (bf16[4,64,1536]{2,1,0:T(8,128)(2,1)}, bf16[4,64,1536]{2,1,0:T(8,128)(2,1)S(1)}, u32[]{:S(2)}, u32[]{:S(2)}) collective-permute-start(bf16[4,64,1536]{2,1,0:T(8,128)(2,1)} %shard_map.99), channel_id=1, source_target_pairs={{0,192},{64,0},{128,64},{192,128},{1,193},{65,1},{129,65},{193,129... | collective-permute-start | bytes 2359304 | tf_op jit(solution)/shard_map/ppermute | solution.py:429
  (14 other events, 141.8 us)

commit v6 on v5

--- a/solution.py
+++ b/solution.py
@@ -216,7 +216,7 @@
 
     def first(half, side, j, centre):
         at = pl.ds(pl.multiple_of(half * rows + j * KB, KB), KB)
-        values = r_ref[pl.ds(j * per, per), :, :].reshape(KB, 128)
+        values = r_ref[pl.ds(j * per, per), 64:96, :].reshape(KB, 128)
         dp = lax.dot_general(values, side, PLAIN_DOT, preferred_element_type=F32)
         dp_ref[at, :] = dp
         return centre + fold(w_ref[0, at, :] * inverse * dp, jnp.sum)
@@ -396,11 +396,9 @@
     copies = jnp.broadcast_to(out_weight, (Z,) + out_weight.shape[1:])
     out_group = exchange(copies, z_groups).reshape(-1, width)
     flat = lambda array: array[0].reshape(frames, records * features)
-    packed = pack_items(flat(queries), flat(key_states))
-    packed_values = pack_items(flat(value_states))
+    packed = pack_items(flat(queries), flat(key_states), flat(value_states))
     received = exchange(after(packed, out_group))
     near = nearby(out_group)
-    received_values = exchange(after(packed_values, received, *near))
     grads = out_grad[0].transpose(1, 0, 2)
     inputs = layer_input[0].transpose(1, 0, 2)
     far = further(near)
@@ -409,21 +407,22 @@
     record = seq // HEADS
     valid = jnp.sum(jnp.where(jnp.arange(records) == record, lengths[0], 0)).reshape(1)
     keys, queries_t, keys_t = prepare(valid, received)
+    copies = jnp.broadcast_to(qkv_weight, (Z,) + qkv_weight.shape[1:])
+    qkv_group = exchange(after(copies, far[2], *near), z_groups).reshape(-1, qkv_weight.shape[2])
     weights_0, sums_0 = softmax_weights(0, after(valid, *near), keys, queries_t)
     attn_grad = project(after(places, sums_0), grads.reshape(records * frames, width), out_pieces)
-    received_grads = exchange(after(attn_grad, received_values))
+    received_grads = exchange(after(attn_grad, qkv_group))
     weights_1, sums_1 = softmax_weights(1, after(valid, attn_grad), keys, queries_t)
-    copies = jnp.broadcast_to(qkv_weight, (Z,) + qkv_weight.shape[1:])
-    qkv_group = exchange(after(copies, received_grads, sums_1), z_groups).reshape(-1, qkv_weight.shape[2])
-    rest = (queries_t, keys_t, received_values, received_grads)
+    rest = (queries_t, keys_t, received, received_grads)
     begun = attention_grads(0, weights_0, after(sums_0, sums_1), *rest)
-    near = nearby(qkv_group)
-    gradients = attention_grads(1, weights_1, after(sums_1, qkv_group), *rest, begun)
-    gradients, *near = lax.optimization_barrier((gradients, *near))
+    near = nearby(after(qkv_group, attn_grad))
+    sums_1, *near = lax.optimization_barrier((sums_1, *near))
+    gradients = attention_grads(1, weights_1, sums_1, *rest, begun)
+    partner, below, above = near
+    diagonal = [across(partner, 1, 0), across(partner, 3, 0)]
+    gradients, *diagonal = lax.optimization_barrier((gradients, *diagonal))
     back = exchange(gradients)
-    partner, below, above = near
-    diagonal = [across(below, 0, 1), across(partner, 3, 0)]
-    far = [across(below, 1, 0), across(diagonal[1], 3, 0)]
+    far = [across(after(below, gradients), 1, 0), across(diagonal[1], 3, 0)]
     result = finish(places, [qkv_group] + near + diagonal + far, back, inputs, grads, norm_gain)
     count = lax.axis_size("section")
     moved = lax.ppermute(result, "section", [(i, (i - 1) % count) for i in range(count)])

time: 302 us -> 273 us (0.904)
  waiting for transfers between devices: 113 us -> 94.9 us
  starting transfers between devices: 70 us -> 58.7 us
    all_to_all x6 -> x5, waiting for transfers between devices: 23.3 us -> 13 us  [exchange(): lax.all_to_all(items, 'seq', split_axis=0, concat_axis=0, tiled=True, axi...]
    all_to_all x6 -> x5, starting transfers between devices: 45.7 us -> 36.5 us  [exchange(): lax.all_to_all(items, 'seq', split_axis=0, concat_axis=0, tiled=True, axi...]
    ppermute x14, waiting for transfers between devices: 77.2 us -> 69.7 us  [across(): return lax.ppermute(rows, 'seq', seq_pairs(dy, dx, 0))]
    unnamed x39 -> x33, local copies, waits for them, and re-layouts: 7.4 us -> 6.8 us
  transfers between devices with their start and end apart: 21 -> 20, of which waited for: 10 -> 7; matrix products, arithmetic and copies ran while one was open for 1% -> 2% of each run, Pallas kernels for 32% -> 35%
where the time goes in v6:
time: 273 us; the launch traced here: 272 us
  Pallas kernels  106 us (39%)
  waiting for transfers between devices  94.9 us (35%)
  starting transfers between devices  58.7 us (22%)
  local copies, waits for them, and re-layouts  11.2 us (4%)
    ppermute x14, waiting for transfers between devices, across(): return lax.ppermute(rows, 'seq', seq_pairs(dy, dx, 0))  69.7 us
    pallas_call x2, Pallas kernels, attention_grads(): pl.pallas_call(functools.partial(grads_kernel, part), grid=(blocks,), out...  54.3 us
    all_to_all x5, starting transfers between devices, exchange(): lax.all_to_all(items, 'seq', split_axis=0, concat_axis=0, tiled=True, axi...  36.5 us
    pallas_call x2, Pallas kernels, softmax_weights(): pl.pallas_call(weights_kernel, grid=(blocks,), out_shape=[jax.ShapeDtypeS...  32.6 us
    ppermute x14, starting transfers between devices, across(): return lax.ppermute(rows, 'seq', seq_pairs(dy, dx, 0))  18.2 us
    all_to_all x5, waiting for transfers between devices, exchange(): lax.all_to_all(items, 'seq', split_axis=0, concat_axis=0, tiled=True, axi...  13 us
    ppermute x1, waiting for transfers between devices, on_device(): lax.ppermute(result, 'section', [(i, (i - 1) % count) for i in range(coun...  12.2 us
    pallas_call x1, Pallas kernels, finish(): pl.pallas_call(finish_kernel, grid=(1,), out_shape=jax.ShapeDtypeStruct(i...  9.86 us
  transfers between devices with their start and end apart: 20, of which 7 were waited for; matrix products, arithmetic and copies ran while one was open for 2% of the time, Pallas kernels for 35%

profile of v6, /device:TPU:1, one launch (start us, length us, event | category | flops | bytes accessed | tf_op | source)
XLA Modules:
  0.0 272.1 jit_solution(5964452156571462894)
XLA Ops:
  1.7 9.0 %all-to-all-start = ((bf16[8,16,1536]{2,1,0:T(8,128)(2,1)}), bf16[8,16,1536]{2,1,0:T(8,128)(2,1)S(1)}, u32[]{:S(2)}, u32[]{:S(2)}) async-start(bf16[8,16,1536]{2,1,0:T(8,128)(2,1)} %broadcast_in_dim.23), calls=%async_computation | async-start | bytes 786432 | tf_op jit(solution)/shard_map/all_to_all | solution.py:355
  11.9 1.7 shard_map.91
  13.6 11.3 %all-to-all-done = bf16[8,16,1536]{2,1,0:T(8,128)(2,1)S(1)} async-done(((bf16[8,16,1536]{2,1,0:T(8,128)(2,1)}), bf16[8,16,1536]{2,1,0:T(8,128)(2,1)S(1)}, u32[]{:S(2)}, u32[]{:S(2)}) %all-to-all-start) | async-done | bytes 393248 | tf_op jit(solution)/shard_map/all_to_all | solution.py:355
  24.9 6.5 %all-to-all-start.1 = ((bf16[64,96,128]{2,1,0:T(8,128)(2,1)}), bf16[64,96,128]{2,1,0:T(8,128)(2,1)}, u32[]{:S(2)}, u32[]{:S(2)}) async-start(bf16[64,96,128]{2,1,0:T(8,128)(2,1)} %shard_map.91), calls=%async_computation.1 | async-start | bytes 3145728 | tf_op jit(solution)/shard_map/all_to_all | solution.py:355
  35.2 14.0 %collective-permute-done.1.refs_2_ = bf16[128,1536]{1,0:T(8,128)(2,1)S(1)} collective-permute-done((bf16[128,1536]{1,0:T(8,128)(2,1)S(1)}, bf16[128,1536]{1,0:T(8,128)(2,1)S(1)}, u32[]{:S(2)}, u32[]{:S(2)}) %collective-permute-start.1) | collective-permute-done | bytes 393248 | tf_op jit(solution)/shard_map/ppermute | solution.py:363
  50.4 17.1 %collective-permute-done.5.refs_6_ = bf16[128,1536]{1,0:T(8,128)(2,1)S(1)} collective-permute-done((bf16[128,1536]{1,0:T(8,128)(2,1)S(1)}, bf16[128,1536]{1,0:T(8,128)(2,1)S(1)}, u32[]{:S(2)}, u32[]{:S(2)}) %collective-permute-start.5) | collective-permute-done | bytes 393248 | tf_op jit(solution)/shard_map/ppermute | solution.py:363
  68.6 7.3 %all-to-all-start.2 = ((bf16[8,24,3072]{2,1,0:T(8,128)(2,1)}), bf16[8,24,3072]{2,1,0:T(8,128)(2,1)}, u32[]{:S(2)}, u32[]{:S(2)}) async-start(bf16[8,24,3072]{2,1,0:T(8,128)(2,1)} %broadcast_in_dim.25), calls=%async_computation.2 | async-start | bytes 2359296 | tf_op jit(solution)/shard_map/all_to_all | solution.py:355
  77.3 2.7 collective-permute-start.4
  80.0 2.2 collective-permute-start.6
  82.2 4.6 %shard_map.92 = (bf16[4096,128]{1,0:T(8,128)(2,1)}, bf16[128,4096]{1,0:T(8,128)(2,1)}, bf16[64,4096]{1,0:T(8,128)(2,1)}) custom-call(s32[1]{0:T(128)} %bitcast.9.length_ref.gate_ref, bf16[64,96,128]{2,1,0:T(8,128)(2,1)} %all-to-all-done.1.r_ref), custom_call_target="tpu_custom_call" | custom-call | bytes 4194304 | tf_op jit(solution)/shard_map/pallas_call | solution.py:137
  86.8 16.3 %shard_map.93 = (f32[8,4096,256]{2,1,0:T(8,128)}, f32[1,2048]{1,0:T(1,128)}) custom-call(s32[1]{0:T(128)} %bitcast.9.length_ref.gate_ref, bf16[4096,128]{1,0:T(8,128)(2,1)} %get-tuple-element.32.kz_ref, bf16[128,4096]{1,0:T(8,128)(2,1)} %get-tuple-element.33.qt_ref), custom_call_target="tpu_custom_call" | custom-call | flops 4294967296 | bytes 33554432 | tf_op jit(solution)/shard_map/pallas_call | solution.py:174
  103.2 3.2 %shard_map.94 = bf16[64,32,128]{2,1,0:T(8,128)(2,1)} custom-call(s32[8]{0:T(128)S(1)} %stack.35.owner_ref, bf16[256,1536]{1,0:T(8,128)(2,1)S(1)} %bitcast.39, bf16[128,1536]{1,0:T(8,128)(2,1)S(1)} %bitcast.47, bf16[128,1536]{1,0:T(8,128)(2,1)S(1)} %collective-permute-done.refs_1_, bf16[128,1536]{1,0:T(8,128)(2,1)S(1)} %collective-permute-done.1.refs_2_, ...), custom_call_target="tpu_custom_call" | custom-call | flops 805306368 | bytes 4456448 | tf_op jit(solution)/shard_map/pallas_call | solution.py:93
  108.0 6.0 %all-to-all-start.3 = ((bf16[64,32,128]{2,1,0:T(8,128)(2,1)}), bf16[64,32,128]{2,1,0:T(8,128)(2,1)S(1)}, u32[]{:S(2)}, u32[]{:S(2)}) async-start(bf16[64,32,128]{2,1,0:T(8,128)(2,1)} %shard_map.94), calls=%async_computation.3 | async-start | bytes 1048576 | tf_op jit(solution)/shard_map/all_to_all | solution.py:355
  117.8 16.3 %shard_map.95 = (f32[8,4096,256]{2,1,0:T(8,128)}, f32[1,2048]{1,0:T(1,128)}) custom-call(s32[1]{0:T(128)} %bitcast.9.length_ref.gate_ref, bf16[4096,128]{1,0:T(8,128)(2,1)} %get-tuple-element.32.kz_ref, bf16[128,4096]{1,0:T(8,128)(2,1)} %get-tuple-element.33.qt_ref), custom_call_target="tpu_custom_call" | custom-call | flops 4294967296 | bytes 33554432 | tf_op jit(solution)/shard_map/pallas_call | solution.py:174
  134.9 26.1 %shard_map.96 = (f32[64,2048]{1,0:T(8,128)}, f32[4096,128]{1,0:T(8,128)}) custom-call(f32[8,4096,256]{2,1,0:T(8,128)} %get-tuple-element.44.w_ref, f32[1,2048]{1,0:T(1,128)} %get-tuple-element.45.l_ref, bf16[128,4096]{1,0:T(8,128)(2,1)} %get-tuple-element.33.qt_ref, bf16[64,4096]{1,0:T(8,128)(2,1)} %get-tuple-element.42.kt_ref, ...), custom_call_target="tpu_custom_call" | custom-call | flops 17179869184 | bytes 33554432 | tf_op jit(solution)/shard_map/pallas_call | solution.py:269
  161.2 2.7 collective-permute-start.11
  163.8 28.2 %shard_map.97 = bf16[64,96,128]{2,1,0:T(8,128)(2,1)} custom-call(f32[8,4096,256]{2,1,0:T(8,128)} %get-tuple-element.37.w_ref, f32[1,2048]{1,0:T(1,128)} %get-tuple-element.41.l_ref, bf16[128,4096]{1,0:T(8,128)(2,1)} %get-tuple-element.33.qt_ref, bf16[64,4096]{1,0:T(8,128)(2,1)} %get-tuple-element.42.kt_ref, bf16[64,96,128]{2,1,0:T(8,128)(2,1)} %all-to-all-done.1.r_ref, ...), custom_call_target="tpu_custom_call" | custom-call | flops 17179869184 | bytes 33554432 | tf_op jit(solution)/shard_map/pallas_call | solution.py:269
  192.1 7.7 %all-to-all-start.4 = ((bf16[64,96,128]{2,1,0:T(8,128)(2,1)}), bf16[64,96,128]{2,1,0:T(8,128)(2,1)S(1)}, u32[]{:S(2)}, u32[]{:S(2)}) async-start(bf16[64,96,128]{2,1,0:T(8,128)(2,1)} %shard_map.97), calls=%async_computation.4 | async-start | bytes 3145728 | tf_op jit(solution)/shard_map/all_to_all | solution.py:355
  201.1 1.7 collective-permute-start.13
  202.8 2.1 copy.19
  204.9 37.4 %collective-permute-done.12.refs_6_ = bf16[192,3072]{1,0:T(8,128)(2,1)S(1)} collective-permute-done((bf16[192,3072]{1,0:T(8,128)(2,1)S(1)}, bf16[192,3072]{1,0:T(8,128)(2,1)S(1)}, u32[]{:S(2)}, u32[]{:S(2)}) %collective-permute-start.12) | collective-permute-done | bytes 1179680 | tf_op jit(solution)/shard_map/ppermute | solution.py:363
  244.6 9.9 %shard_map.98 = bf16[4,64,1536]{2,1,0:T(8,128)(2,1)} custom-call(s32[8]{0:T(128)} %copy-done.1, bf16[64,96,128]{2,1,0:T(8,128)(2,1)} %copy-done.2, bf16[4,64,1536]{2,1,0:T(8,128)(2,1)} %bitcast.48, bf16[4,64,1536]{2,1,0:T(8,128)(2,1)} %bitcast.40, f32[1,1536]{1,0:T(1,128)} %gain_ref.1, bf16[192,3072]{1,0:T(8,128)(2,1)} %bitcast.16.refs_0_, ...), custom_call_target="tpu_custom_call" | custom-call | flops 2415919104 | bytes 9437184 | tf_op jit(solution)/shard_map/pallas_call | solution.py:335
  254.4 4.0 %collective-permute-start.14 = (bf16[4,64,1536]{2,1,0:T(8,128)(2,1)}, bf16[4,64,1536]{2,1,0:T(8,128)(2,1)S(1)}, u32[]{:S(2)}, u32[]{:S(2)}) collective-permute-start(bf16[4,64,1536]{2,1,0:T(8,128)(2,1)} %shard_map.98), channel_id=1, source_target_pairs={{0,192},{64,0},{128,64},{192,128},{1,193},{65,1},{129,65},{193,129... | collective-permute-start | bytes 2359304 | tf_op jit(solution)/shard_map/ppermute | solution.py:428
  258.4 12.2 %collective-permute-done.14 = bf16[4,64,1536]{2,1,0:T(8,128)(2,1)S(1)} collective-permute-done((bf16[4,64,1536]{2,1,0:T(8,128)(2,1)}, bf16[4,64,1536]{2,1,0:T(8,128)(2,1)S(1)}, u32[]{:S(2)}, u32[]{:S(2)}) %collective-permute-start.14) | collective-permute-done | bytes 786464 | tf_op jit(solution)/shard_map/ppermute | solution.py:428
  (62 shorter events, 21.7 us)
Async XLA Ops:
  1.7 23.2 %all-to-all-start = ((bf16[8,16,1536]{2,1,0:T(8,128)(2,1)}), bf16[8,16,1536]{2,1,0:T(8,128)(2,1)S(1)}, u32[]{:S(2)}, u32[]{:S(2)}) async-start(bf16[8,16,1536]{2,1,0:T(8,128)(2,1)} %broadcast_in_dim.23), calls=%async_computation | async-start | bytes 786432 | tf_op jit(solution)/shard_map/all_to_all | solution.py:355
  24.9 42.6 %copy-start.12 = (bf16[1,24,3072]{2,1,0:T(8,128)(2,1)S(1)}, bf16[1,24,3072]{2,1,0:T(8,128)(2,1)}, u32[]{:S(2)}) copy-start(bf16[1,24,3072]{2,1,0:T(8,128)(2,1)} %param.16) | copy-start | bytes 442372
  24.9 43.8 %all-to-all-start.1 = ((bf16[64,96,128]{2,1,0:T(8,128)(2,1)}), bf16[64,96,128]{2,1,0:T(8,128)(2,1)}, u32[]{:S(2)}, u32[]{:S(2)}) async-start(bf16[64,96,128]{2,1,0:T(8,128)(2,1)} %shard_map.91), calls=%async_computation.1 | async-start | bytes 3145728 | tf_op jit(solution)/shard_map/all_to_all | solution.py:355
  31.4 17.7 %collective-permute-start.1 = (bf16[128,1536]{1,0:T(8,128)(2,1)S(1)}, bf16[128,1536]{1,0:T(8,128)(2,1)S(1)}, u32[]{:S(2)}, u32[]{:S(2)}) collective-permute-start(bf16[128,1536]{1,0:T(8,128)(2,1)S(1)} %bitcast.44), channel_id=1, source_target_pairs={{0,16},{1,17},{2,18},{3,19},{4,20},{5,21},{6,22},{7,23},{8,24},{9,... | collective-permute-start | bytes 1179656 | tf_op jit(solution)/shard_map/ppermute | solution.py:363
  32.4 16.7 %collective-permute-start = (bf16[128,1536]{1,0:T(8,128)(2,1)S(1)}, bf16[128,1536]{1,0:T(8,128)(2,1)S(1)}, u32[]{:S(2)}, u32[]{:S(2)}) collective-permute-start(bf16[128,1536]{1,0:T(8,128)(2,1)S(1)} %bitcast.45), channel_id=1, source_target_pairs={{0,8},{1,9},{2,10},{3,11},{4,12},{5,13},{6,14},{7,15},{8,0},{9,1},... | collective-permute-start | bytes 1179656 | tf_op jit(solution)/shard_map/ppermute | solution.py:363
  33.6 16.7 %collective-permute-start.2 = (bf16[128,1536]{1,0:T(8,128)(2,1)S(1)}, bf16[128,1536]{1,0:T(8,128)(2,1)S(1)}, u32[]{:S(2)}, u32[]{:S(2)}) collective-permute-start(bf16[128,1536]{1,0:T(8,128)(2,1)S(1)} %bitcast.46), channel_id=1, source_target_pairs={{0,48},{1,49},{2,50},{3,51},{4,52},{5,53},{6,54},{7,55},{8,56},{9,... | collective-permute-start | bytes 1179656 | tf_op jit(solution)/shard_map/ppermute | solution.py:363
  49.1 18.3 %collective-permute-start.5 = (bf16[128,1536]{1,0:T(8,128)(2,1)S(1)}, bf16[128,1536]{1,0:T(8,128)(2,1)S(1)}, u32[]{:S(2)}, u32[]{:S(2)}) collective-permute-start(bf16[128,1536]{1,0:T(8,128)(2,1)S(1)} %collective-permute-done.1.refs_2_), channel_id=1, source_target_pairs={{0,16},{1,17},{2,18},{3,19},{4,20},{5,21},{6,22},{7,23},{8,24},{9,... | collective-permute-start | bytes 1179656 | tf_op jit(solution)/shard_map/ppermute | solution.py:363
  68.6 39.4 %all-to-all-start.2 = ((bf16[8,24,3072]{2,1,0:T(8,128)(2,1)}), bf16[8,24,3072]{2,1,0:T(8,128)(2,1)}, u32[]{:S(2)}, u32[]{:S(2)}) async-start(bf16[8,24,3072]{2,1,0:T(8,128)(2,1)} %broadcast_in_dim.25), calls=%async_computation.2 | async-start | bytes 2359296 | tf_op jit(solution)/shard_map/all_to_all | solution.py:355
  76.2 27.0 %copy-start = (bf16[1,64,4,1536]{3,1,2,0:T(8,128)(2,1)}, bf16[1,64,4,1536]{3,1,2,0:T(8,128)(2,1)S(1)}, u32[]{:S(2)}) copy-start(bf16[1,64,4,1536]{3,1,2,0:T(8,128)(2,1)S(1)} %copy.20) | copy-start | bytes 2359300
  77.3 25.8 %collective-permute-start.3 = (bf16[128,1536]{1,0:T(8,128)(2,1)S(1)}, bf16[128,1536]{1,0:T(8,128)(2,1)S(1)}, u32[]{:S(2)}, u32[]{:S(2)}) collective-permute-start(bf16[128,1536]{1,0:T(8,128)(2,1)S(1)} %collective-permute-done.refs_1_), channel_id=1, source_target_pairs={{0,16},{1,17},{2,18},{3,19},{4,20},{5,21},{6,22},{7,23},{8,24},{9,... | collective-permute-start | bytes 1179656 | tf_op jit(solution)/shard_map/ppermute | solution.py:363
  77.3 25.8 %collective-permute-start.4 = (bf16[128,1536]{1,0:T(8,128)(2,1)S(1)}, bf16[128,1536]{1,0:T(8,128)(2,1)S(1)}, u32[]{:S(2)}, u32[]{:S(2)}) collective-permute-start(bf16[128,1536]{1,0:T(8,128)(2,1)S(1)} %collective-permute-done.refs_1_), channel_id=1, source_target_pairs={{0,48},{1,49},{2,50},{3,51},{4,52},{5,53},{6,54},{7,55},{8,56},{9,... | collective-permute-start | bytes 1179656 | tf_op jit(solution)/shard_map/ppermute | solution.py:363
  80.0 23.2 %collective-permute-start.6 = (bf16[128,1536]{1,0:T(8,128)(2,1)S(1)}, bf16[128,1536]{1,0:T(8,128)(2,1)S(1)}, u32[]{:S(2)}, u32[]{:S(2)}) collective-permute-start(bf16[128,1536]{1,0:T(8,128)(2,1)S(1)} %collective-permute-done.5.refs_6_), channel_id=1, source_target_pairs={{0,8},{1,9},{2,10},{3,11},{4,12},{5,13},{6,14},{7,15},{8,0},{9,1},... | collective-permute-start | bytes 1179656 | tf_op jit(solution)/shard_map/ppermute | solution.py:363
  108.0 26.1 %all-to-all-start.3 = ((bf16[64,32,128]{2,1,0:T(8,128)(2,1)}), bf16[64,32,128]{2,1,0:T(8,128)(2,1)S(1)}, u32[]{:S(2)}, u32[]{:S(2)}) async-start(bf16[64,32,128]{2,1,0:T(8,128)(2,1)} %shard_map.94), calls=%async_computation.3 | async-start | bytes 1048576 | tf_op jit(solution)/shard_map/all_to_all | solution.py:355
  114.1 47.0 %collective-permute-start.7 = (bf16[192,3072]{1,0:T(8,128)(2,1)}, bf16[192,3072]{1,0:T(8,128)(2,1)S(1)}, u32[]{:S(2)}, u32[]{:S(2)}) collective-permute-start(bf16[192,3072]{1,0:T(8,128)(2,1)} %bitcast.16.refs_0_), channel_id=1, source_target_pairs={{0,8},{1,9},{2,10},{3,11},{4,12},{5,13},{6,14},{7,15},{8,0},{9,1},... | collective-permute-start | bytes 3538952 | tf_op jit(solution)/shard_map/ppermute | solution.py:363
  115.2 45.9 %collective-permute-start.8 = (bf16[192,3072]{1,0:T(8,128)(2,1)}, bf16[192,3072]{1,0:T(8,128)(2,1)S(1)}, u32[]{:S(2)}, u32[]{:S(2)}) collective-permute-start(bf16[192,3072]{1,0:T(8,128)(2,1)} %bitcast.16.refs_0_), channel_id=1, source_target_pairs={{0,16},{1,17},{2,18},{3,19},{4,20},{5,21},{6,22},{7,23},{8,24},{9,... | collective-permute-start | bytes 3538952 | tf_op jit(solution)/shard_map/ppermute | solution.py:363
  116.4 44.7 %collective-permute-start.9 = (bf16[192,3072]{1,0:T(8,128)(2,1)}, bf16[192,3072]{1,0:T(8,128)(2,1)}, u32[]{:S(2)}, u32[]{:S(2)}) collective-permute-start(bf16[192,3072]{1,0:T(8,128)(2,1)} %bitcast.16.refs_0_), channel_id=1, source_target_pairs={{0,48},{1,49},{2,50},{3,51},{4,52},{5,53},{6,54},{7,55},{8,56},{9,... | collective-permute-start | bytes 3538952 | tf_op jit(solution)/shard_map/ppermute | solution.py:363
  161.0 31.0 %copy-start.3 = (bf16[192,3072]{1,0:T(8,128)(2,1)}, bf16[192,3072]{1,0:T(8,128)(2,1)S(1)}, u32[]{:S(2)}) copy-start(bf16[192,3072]{1,0:T(8,128)(2,1)S(1)} %collective-permute-done.7.refs_1_) | copy-start | bytes 3538948
  161.1 31.0 %copy-start.4 = (bf16[192,3072]{1,0:T(8,128)(2,1)}, bf16[192,3072]{1,0:T(8,128)(2,1)S(1)}, u32[]{:S(2)}) copy-start(bf16[192,3072]{1,0:T(8,128)(2,1)S(1)} %collective-permute-done.8.refs_2_) | copy-start | bytes 3538948
  161.1 31.0 %collective-permute-start.10 = (bf16[192,3072]{1,0:T(8,128)(2,1)S(1)}, bf16[192,3072]{1,0:T(8,128)(2,1)}, u32[]{:S(2)}, u32[]{:S(2)}) collective-permute-start(bf16[192,3072]{1,0:T(8,128)(2,1)S(1)} %collective-permute-done.7.refs_1_), channel_id=1, source_target_pairs={{0,16},{1,17},{2,18},{3,19},{4,20},{5,21},{6,22},{7,23},{8,24},{9,... | collective-permute-start | bytes 3538952 | tf_op jit(solution)/shard_map/ppermute | solution.py:363
  161.2 30.9 %collective-permute-start.11 = (bf16[192,3072]{1,0:T(8,128)(2,1)S(1)}, bf16[192,3072]{1,0:T(8,128)(2,1)}, u32[]{:S(2)}, u32[]{:S(2)}) collective-permute-start(bf16[192,3072]{1,0:T(8,128)(2,1)S(1)} %collective-permute-done.7.refs_1_), channel_id=1, source_target_pairs={{0,48},{1,49},{2,50},{3,51},{4,52},{5,53},{6,54},{7,55},{8,56},{9,... | collective-permute-start | bytes 3538952 | tf_op jit(solution)/shard_map/ppermute | solution.py:363
  192.1 51.3 %all-to-all-start.4 = ((bf16[64,96,128]{2,1,0:T(8,128)(2,1)}), bf16[64,96,128]{2,1,0:T(8,128)(2,1)S(1)}, u32[]{:S(2)}, u32[]{:S(2)}) async-start(bf16[64,96,128]{2,1,0:T(8,128)(2,1)} %shard_map.97), calls=%async_computation.4 | async-start | bytes 3145728 | tf_op jit(solution)/shard_map/all_to_all | solution.py:355
  199.8 42.5 %collective-permute-start.12 = (bf16[192,3072]{1,0:T(8,128)(2,1)S(1)}, bf16[192,3072]{1,0:T(8,128)(2,1)S(1)}, u32[]{:S(2)}, u32[]{:S(2)}) collective-permute-start(bf16[192,3072]{1,0:T(8,128)(2,1)S(1)} %copy-done.5), channel_id=1, source_target_pairs={{0,16},{1,17},{2,18},{3,19},{4,20},{5,21},{6,22},{7,23},{8,24},{9,... | collective-permute-start | bytes 3538952 | tf_op jit(solution)/shard_map/ppermute | solution.py:363
  201.1 42.3 %collective-permute-start.13 = (bf16[192,3072]{1,0:T(8,128)(2,1)}, bf16[192,3072]{1,0:T(8,128)(2,1)}, u32[]{:S(2)}, u32[]{:S(2)}) collective-permute-start(bf16[192,3072]{1,0:T(8,128)(2,1)} %collective-permute-done.11.refs_5_), channel_id=1, source_target_pairs={{0,48},{1,49},{2,50},{3,51},{4,52},{5,53},{6,54},{7,55},{8,56},{9,... | collective-permute-start | bytes 3538952 | tf_op jit(solution)/shard_map/ppermute | solution.py:363
  254.4 16.2 %collective-permute-start.14 = (bf16[4,64,1536]{2,1,0:T(8,128)(2,1)}, bf16[4,64,1536]{2,1,0:T(8,128)(2,1)S(1)}, u32[]{:S(2)}, u32[]{:S(2)}) collective-permute-start(bf16[4,64,1536]{2,1,0:T(8,128)(2,1)} %shard_map.98), channel_id=1, source_target_pairs={{0,192},{64,0},{128,64},{192,128},{1,193},{65,1},{129,65},{193,129... | collective-permute-start | bytes 2359304 | tf_op jit(solution)/shard_map/ppermute | solution.py:428
  (10 other events, 67.9 us)
